TPU v7x, 32 devices: a whole 2x2x4 slice. The times are simulated.
32 devices in a mesh: groups: 2 (over y), blocks: 4 (over z), pairs: 2 (over x), dims: 2 (over core).
Axes of the slice: x: 2, y: 2, z: 4, core: 2. Of those that a mesh axis runs over, the one named last changes fastest.
Arguments:
- codes: bfloat16 [64, 256, 1024], P(('groups', 'blocks'), None, 'dims'), parts along dimension 0, may hold values from -6 to 6
- scales: bfloat16 [64, 256], P(('groups', 'blocks')), parts along dimension 0, may hold values from 0.5 to 2
- cluster_ids: int32 [64], P(('groups', 'blocks')), parts along dimension 0, may hold values from 0 to 2
- row_counts: int32 [64], P(('groups', 'blocks')), parts along dimension 0, may hold values from 64 to 256, as said below
- route_offsets: int32 [8, 2, 12, 1], P(('groups', 'blocks'), 'pairs'), parts along dimension 0, may hold values from 0 to 2; in each aligned block of 12 rows (0 to 11, 12 to 23, ..., all dimensions but the last counted through in order) at most 4 rows name the same one
- partner_local: int32 [8, 2, 12], P(('groups', 'blocks'), 'pairs'), parts along dimension 0, may hold values from 0 to 7
Outputs:
- log_density: float32 [64, 256], P(('groups', 'blocks')), parts along dimension 0
There are 2 independent parts, one for each index of `groups`. A program takes and returns all parts, laid end to end along the dimension named above; each array names one. Nothing has to cross between parts.
Inputs may be any that keep to these rules, and one draw needn't show every extreme that they name: `route_offsets`: in the list of one index of blocks and pairs (12 entries) no offset appears more than 4 times, and some offset appears exactly 4 times. `row_counts`: in every draw some block uses all 256 rows.
All inputs are finite; a program needn't handle non-finite values.
Results may differ from a plain program's by a relative error of at most 0.0005.
Values may be sent and summed in bfloat16 or wider, within the bound.
No kernel may reach another device: no remote copies, remote signals or barrier semaphores. Data moves between devices by JAX's collectives and lax.ppermute only.
A program may use at most 64 MiB of HBM per device.

v0:
```python
import math

import jax
import jax.numpy as jnp
from jax import lax
from jax.sharding import PartitionSpec as P


def slot_table(slot_ids, values, slot_total):
    hits = slot_ids[None, :] == jnp.arange(slot_total, dtype=jnp.int32)[:, None]
    filled = jnp.sum(jnp.where(hits, values[None, :] + 1, 0), axis=1)
    return filled - 1


def kernel_sums(
    local_mat,
    local_scale,
    local_valid,
    local_cluster,
    partner_codes,
    partner_scale,
    partner_valid,
    partner_cluster,
    inverse_root,
):

    def one_partner(row_total, partner_item):
        codes_one, scale_one, valid_one, cluster_one = partner_item
        gram_tile = jnp.einsum(
            "ae,re->ar", local_mat, codes_one, preferred_element_type=jnp.float32
        )
        weight = local_scale[:, None] * scale_one[None, :]
        keep_rows = (local_cluster == cluster_one).astype(jnp.float32) * local_valid
        kernel_tile = (
            jnp.exp(gram_tile * weight * inverse_root) * keep_rows[:, None] * valid_one[None, :]
        )
        return (row_total + jnp.sum(kernel_tile, axis=1), jnp.sum(kernel_tile, axis=0))

    row_start = jnp.zeros((local_mat.shape[0],), jnp.float32)
    return lax.scan(
        one_partner, row_start, (partner_codes, partner_scale, partner_valid, partner_cluster)
    )


def per_device(codes, scales, cluster_ids, row_counts, route_offsets, partner_local):
    highest = lax.Precision.HIGHEST
    owner_count = lax.axis_size("blocks")
    dims_count = lax.axis_size("dims")
    owner_index = lax.axis_index("blocks")
    dim_index = lax.axis_index("dims")
    own_blocks, rows, width_part = codes.shape
    pair_count = partner_local.shape[-1]
    capacity = max(2, (pair_count + owner_count - 2) // (owner_count - 1))
    slot_total = owner_count * capacity
    inverse_root = 1.0 / math.sqrt(width_part * dims_count)
    offsets = route_offsets.reshape(pair_count)
    wanted = partner_local.reshape(pair_count)
    targets = (owner_index + 1 + offsets) % owner_count
    position = jnp.arange(pair_count, dtype=jnp.int32)
    same_owner = (targets[:, None] == targets[None, :]) & (position[None, :] < position[:, None])
    slot_rank = jnp.sum(same_owner.astype(jnp.int32), axis=1)
    slot_ids = targets * capacity + slot_rank
    request_table = slot_table(slot_ids, wanted, slot_total).reshape(owner_count, capacity)
    asked_blocks = lax.all_to_all(
        request_table, "blocks", split_axis=0, concat_axis=0, tiled=True
    ).reshape(slot_total)
    chosen = jnp.maximum(asked_blocks, 0)
    valid_rows = (jnp.arange(rows, dtype=jnp.int32)[None, :] < row_counts[:, None]).astype(
        jnp.float32
    )
    scale_wide = scales.astype(jnp.float32)
    metadata = jnp.stack([cluster_ids[chosen], row_counts[chosen]], axis=1)
    source_width = codes.shape[2]
    outgoing = (
        codes[chosen].reshape(owner_count, capacity, rows, source_width),
        scales[chosen].reshape(owner_count, capacity, rows),
        metadata.reshape(owner_count, capacity, 2),
    )
    arrived = (
        lax.all_to_all(outgoing[0], "blocks", split_axis=0, concat_axis=0, tiled=True),
        lax.all_to_all(outgoing[1], "blocks", split_axis=0, concat_axis=0, tiled=True),
        lax.all_to_all(outgoing[2], "blocks", split_axis=0, concat_axis=0, tiled=True),
    )
    partner_codes = arrived[0].reshape(slot_total, rows, source_width)[slot_ids]
    partner_scale = arrived[1].reshape(slot_total, rows)[slot_ids].astype(jnp.float32)
    partner_info = arrived[2].reshape(slot_total, 2)[slot_ids]
    partner_cluster = partner_info[:, 0]
    partner_rows_idx = jnp.arange(rows, dtype=jnp.int32)
    partner_valid = (partner_rows_idx[None, :] < partner_info[:, 1:2]).astype(jnp.float32)
    half_blocks = own_blocks // dims_count
    block_start = dim_index * half_blocks
    local_whole = lax.all_to_all(codes, "dims", split_axis=0, concat_axis=2, tiled=True)
    partner_whole = lax.all_gather(partner_codes, "dims", axis=2, tiled=True)
    local_mat = local_whole.reshape(half_blocks * rows, local_whole.shape[2])
    local_scale = lax.dynamic_slice_in_dim(scale_wide, block_start, half_blocks, 0).reshape(
        half_blocks * rows
    )
    local_valid = lax.dynamic_slice_in_dim(valid_rows, block_start, half_blocks, 0).reshape(
        half_blocks * rows
    )
    local_cluster_ids = lax.dynamic_slice_in_dim(cluster_ids, block_start, half_blocks, 0)
    local_cluster = jnp.broadcast_to(local_cluster_ids[:, None], (half_blocks, rows)).reshape(
        half_blocks * rows
    )
    row_total, column_sums = kernel_sums(
        local_mat,
        local_scale,
        local_valid,
        local_cluster,
        partner_whole,
        partner_scale,
        partner_valid,
        partner_cluster,
        inverse_root,
    )
    row_part = lax.dynamic_update_slice_in_dim(
        jnp.zeros((own_blocks, rows), jnp.float32),
        row_total.reshape(half_blocks, rows),
        block_start,
        0,
    )
    column_width = column_sums.shape[1]
    place_matrix = (jnp.arange(slot_total, dtype=jnp.int32)[:, None] == slot_ids[None, :]).astype(
        jnp.float32
    )
    slot_sums = jnp.dot(
        place_matrix, column_sums, precision=highest, preferred_element_type=jnp.float32
    )
    returned = lax.all_to_all(
        slot_sums.reshape(owner_count, capacity, column_width).astype(jnp.bfloat16),
        "blocks",
        split_axis=0,
        concat_axis=0,
        tiled=True,
    ).astype(jnp.float32)
    gather_back = (
        jnp.arange(own_blocks, dtype=jnp.int32)[:, None] == asked_blocks[None, :]
    ).astype(jnp.float32)
    own_columns = jnp.dot(
        gather_back,
        returned.reshape(slot_total, column_width),
        precision=highest,
        preferred_element_type=jnp.float32,
    )
    density = own_columns + row_part
    density = lax.psum(density, ("pairs", "dims"))
    return jnp.log1p(density)


def solution(mesh):
    return jax.shard_map(
        per_device,
        mesh=mesh,
        in_specs=(
            P(("groups", "blocks"), None, "dims"),
            P(("groups", "blocks"), None),
            P(("groups", "blocks")),
            P(("groups", "blocks")),
            P(("groups", "blocks"), "pairs", None, None),
            P(("groups", "blocks"), "pairs", None),
        ),
        out_specs=P(("groups", "blocks"), None),
        check_vma=False,
    )
```

profile of v0, /device:TPU:0, one launch (start us, length us, event | category | flops | bytes accessed | tf_op | source)
XLA Modules:
  0.0 223.2 jit_solution(11196809685982642744)
XLA Ops:
  6.5 0.7 add_bitcast_fusion
  7.2 0.7 and_select_fusion.1
  8.0 0.7 multiply_add_fusion
  8.9 11.7 %all_to_all.41 = s32[4,1,4]{2,1,0:T(1,128)S(1)} all-to-all(s32[4,1,4]{2,1,0:T(1,128)S(1)} %bitcast.89), channel_id=1, replica_groups=mesh['groups'=2,'blocks'=4,'pairs'=2,'dims'=2] {'blocks'}, dimensions={0} | all-to-all | bytes 128 | tf_op jit(solution)/shard_map/all_to_all | solution.py:64
  21.1 0.7 fusion.21
  21.9 4.4 %gather_fusion = bf16[16,256,512]{2,1,0:T(8,128)(2,1)} fusion(bf16[8,256,512]{2,1,0:T(8,128)(2,1)} %param.8, s32[1024]{0:T(1024)S(1)} %pad_clamp_fusion.1), kind=kCustom, calls=%fused_computation | custom fusion | bytes 8388672 | tf_op jit(solution)/shard_map/gather | solution.py:75
  26.2 5.0 %all-to-all-start.1 = ((bf16[4,4,256,512]{3,2,1,0:T(8,128)(2,1)}), bf16[4,4,256,512]{3,2,1,0:T(8,128)(2,1)}, u32[]{:S(2)}, u32[]{:S(2)}) async-start(bf16[4,4,256,512]{3,2,1,0:T(8,128)(2,1)} %bitcast.77), calls=%async_computation.1 | async-start | bytes 8388608 | tf_op jit(solution)/shard_map/all_to_all | solution.py:80
  31.3 92.0 %all-to-all-done.1 = bf16[4,4,256,512]{3,2,1,0:T(8,128)(2,1)} async-done(((bf16[4,4,256,512]{3,2,1,0:T(8,128)(2,1)}), bf16[4,4,256,512]{3,2,1,0:T(8,128)(2,1)}, u32[]{:S(2)}, u32[]{:S(2)}) %all-to-all-start.1) | async-done | bytes 4194336 | tf_op jit(solution)/shard_map/all_to_all | solution.py:80
  123.3 4.7 %gather_fusion.1 = bf16[12,256,512]{2,1,0:T(8,128)(2,1)} fusion(bf16[16,256,512]{2,1,0:T(8,128)(2,1)} %bitcast.4, s32[1024]{0:T(1024)S(1)} %pad_clamp_fusion), kind=kCustom, calls=%fused_computation.1 | custom fusion | bytes 6291504 | tf_op jit(solution)/shard_map/gather | solution.py:84
  128.0 3.8 %all-to-all-start.2 = ((bf16[8,256,512]{2,1,0:T(8,128)(2,1)}), bf16[8,256,512]{2,1,0:T(8,128)(2,1)S(1)}, u32[]{:S(2)}, u32[]{:S(2)}) async-start(bf16[8,256,512]{2,1,0:T(8,128)(2,1)} %param.8), calls=%async_computation.2 | async-start | bytes 4194304 | tf_op jit(solution)/shard_map/all_to_all | solution.py:92
  131.8 2.8 %all-to-all-done.2 = bf16[8,256,512]{2,1,0:T(8,128)(2,1)S(1)} async-done(((bf16[8,256,512]{2,1,0:T(8,128)(2,1)}), bf16[8,256,512]{2,1,0:T(8,128)(2,1)S(1)}, u32[]{:S(2)}, u32[]{:S(2)}) %all-to-all-start.2) | async-done | bytes 2097184 | tf_op jit(solution)/shard_map/all_to_all | solution.py:92
  134.7 2.2 copy.17
  137.7 0.7 gather_fusion.5
  138.4 0.7 gather_fusion.4
  139.2 0.6 copy.18
  139.8 3.2 %all-to-all-start.4 = ((s32[4,4,2]{1,2,0:T(2,128)}), s32[4,4,2]{1,2,0:T(2,128)S(1)}, u32[]{:S(2)}, u32[]{:S(2)}) async-start(s32[4,4,2]{1,2,0:T(2,128)} %copy.18), calls=%async_computation.4 | async-start | bytes 8192 | tf_op jit(solution)/shard_map/all_to_all | solution.py:82
  143.1 0.6 gather_fusion.2
  143.7 0.6 reshape.184
  144.3 4.2 %all-to-all-done.4 = s32[4,4,2]{1,2,0:T(2,128)S(1)} async-done(((s32[4,4,2]{1,2,0:T(2,128)}), s32[4,4,2]{1,2,0:T(2,128)S(1)}, u32[]{:S(2)}, u32[]{:S(2)}) %all-to-all-start.4) | async-done | bytes 160 | tf_op jit(solution)/shard_map/all_to_all | solution.py:82
  148.5 3.2 %all-to-all-start.3 = ((bf16[4,4,256]{2,1,0:T(4,128)(2,1)}), bf16[4,4,256]{2,1,0:T(4,128)(2,1)S(1)}, u32[]{:S(2)}, u32[]{:S(2)}) async-start(bf16[4,4,256]{2,1,0:T(4,128)(2,1)} %reshape.184), calls=%async_computation.3 | async-start | bytes 16384 | tf_op jit(solution)/shard_map/all_to_all | solution.py:81
  152.7 4.6 %all-to-all-done.3 = bf16[4,4,256]{2,1,0:T(4,128)(2,1)S(1)} async-done(((bf16[4,4,256]{2,1,0:T(4,128)(2,1)}), bf16[4,4,256]{2,1,0:T(4,128)(2,1)S(1)}, u32[]{:S(2)}, u32[]{:S(2)}) %all-to-all-start.3) | async-done | bytes 8224 | tf_op jit(solution)/shard_map/all_to_all | solution.py:81
  157.3 0.6 gather_fusion.3
  157.9 42.3 %while.13 = (s32[]{:T(128)}, f32[1024]{0:T(1024)S(1)}, f32[12,256]{1,0:T(8,128)S(1)}, bf16[12,256,1024]{2,1,0:T(8,128)(2,1)}, bf16[1024,1024]{1,0:T(8,128)(2,1)S...) while((s32[]{:T(128)}, f32[1024]{0:T(1024)S(1)}, ...), condition=%wide.region_5.6_spmd.clone, body=%wide.region_2.5_spmd.clone.sunk | while | flops 538708736 | bytes 2688187 | solution.py:40
  158.0 0.6 dynamic_slice.46
  158.6 0.6 compare_select_fusion.7
  159.3 2.1 fusion.28
  161.6 0.6 dynamic_slice.46
  162.2 0.6 compare_select_fusion.7
  162.8 2.1 fusion.28
  165.1 0.6 dynamic_slice.46
  165.7 0.6 compare_select_fusion.7
  166.3 2.1 fusion.28
  168.6 0.6 dynamic_slice.46
  169.2 0.6 compare_select_fusion.7
  169.9 2.1 fusion.28
  172.2 0.6 dynamic_slice.46
  172.7 0.6 compare_select_fusion.7
  173.4 2.1 fusion.28
  175.7 0.6 dynamic_slice.46
  176.3 0.6 compare_select_fusion.7
  176.9 2.1 fusion.28
  179.2 0.6 dynamic_slice.46
  179.8 0.6 compare_select_fusion.7
  180.5 2.1 fusion.28
  182.7 0.6 dynamic_slice.46
  183.3 0.6 compare_select_fusion.7
  184.0 2.1 fusion.28
  186.3 0.6 dynamic_slice.46
  186.8 0.6 compare_select_fusion.7
  187.5 2.1 fusion.28
  189.8 0.6 dynamic_slice.46
  190.4 0.6 compare_select_fusion.7
  191.0 2.1 fusion.28
  193.3 0.6 dynamic_slice.46
  193.9 0.6 compare_select_fusion.7
  194.6 2.1 fusion.28
  196.9 0.6 dynamic_slice.46
  197.4 0.6 compare_select_fusion.7
  198.1 2.1 fusion.28
  200.4 0.6 convert_element_type.31
  201.0 3.2 %all-to-all-start.5 = ((bf16[4,4,256]{2,1,0:T(4,128)(2,1)}), bf16[4,4,256]{2,1,0:T(4,128)(2,1)S(1)}, u32[]{:S(2)}, u32[]{:S(2)}) async-start(bf16[4,4,256]{2,1,0:T(4,128)(2,1)} %convert_element_type.31), calls=%async_computation.5 | async-start | bytes 16384 | tf_op jit(solution)/shard_map/all_to_all | solution.py:129
  204.4 5.5 %all-to-all-done.5 = bf16[4,4,256]{2,1,0:T(4,128)(2,1)S(1)} async-done(((bf16[4,4,256]{2,1,0:T(4,128)(2,1)}), bf16[4,4,256]{2,1,0:T(4,128)(2,1)S(1)}, u32[]{:S(2)}, u32[]{:S(2)}) %all-to-all-start.5) | async-done | bytes 8224 | tf_op jit(solution)/shard_map/all_to_all | solution.py:129
  210.0 5.7 %psum.7 = f32[8,256]{1,0:T(8,128)S(1)} all-reduce(f32[8,256]{1,0:T(8,128)S(1)} %add_dynamic-update-slice_fusion), channel_id=1, replica_groups=mesh['groups'=2,'blocks'=4,'pairs'=2,'dims'=2] {'pairs','dims'}, use_global_device_ids=true, to_apply=%region_6.7 | all-reduce | flops 2048 | bytes 16384 | tf_op jit(solution)/shard_map/psum | solution.py:146
  215.7 0.6 log1p.3
  (115 shorter events, 5.1 us)
Async XLA Ops:
  26.2 5.0 %copy-start.3 = (s32[1,1,12,1]{2,3,1,0:T(1,128)S(1)}, s32[1,1,12,1]{2,3,1,0:T(1,128)}, u32[]{:S(2)}) copy-start(s32[1,1,12,1]{2,3,1,0:T(1,128)} %param.12) | copy-start | bytes 148
  26.2 97.0 %all-to-all-start.1 = ((bf16[4,4,256,512]{3,2,1,0:T(8,128)(2,1)}), bf16[4,4,256,512]{3,2,1,0:T(8,128)(2,1)}, u32[]{:S(2)}, u32[]{:S(2)}) async-start(bf16[4,4,256,512]{3,2,1,0:T(8,128)(2,1)} %bitcast.77), calls=%async_computation.1 | async-start | bytes 8388608 | tf_op jit(solution)/shard_map/all_to_all | solution.py:80
  31.2 126.7 %all-gather.3.cloned.1.call-start = ((), (), s32[]{:S(2)}) async-start(), calls=%async_computation.6 | async-start | bytes 9437184 | tf_op jit(solution)/shard_map/all_gather | solution.py:93
  128.0 6.6 %all-to-all-start.2 = ((bf16[8,256,512]{2,1,0:T(8,128)(2,1)}), bf16[8,256,512]{2,1,0:T(8,128)(2,1)S(1)}, u32[]{:S(2)}, u32[]{:S(2)}) async-start(bf16[8,256,512]{2,1,0:T(8,128)(2,1)} %param.8), calls=%async_computation.2 | async-start | bytes 4194304 | tf_op jit(solution)/shard_map/all_to_all | solution.py:92
  136.8 0.7 copy-start
  136.8 0.7 copy-start.1
  136.9 0.8 copy-start.2
  139.8 8.6 %all-to-all-start.4 = ((s32[4,4,2]{1,2,0:T(2,128)}), s32[4,4,2]{1,2,0:T(2,128)S(1)}, u32[]{:S(2)}, u32[]{:S(2)}) async-start(s32[4,4,2]{1,2,0:T(2,128)} %copy.18), calls=%async_computation.4 | async-start | bytes 8192 | tf_op jit(solution)/shard_map/all_to_all | solution.py:82
  148.5 8.8 %all-to-all-start.3 = ((bf16[4,4,256]{2,1,0:T(4,128)(2,1)}), bf16[4,4,256]{2,1,0:T(4,128)(2,1)S(1)}, u32[]{:S(2)}, u32[]{:S(2)}) async-start(bf16[4,4,256]{2,1,0:T(4,128)(2,1)} %reshape.184), calls=%async_computation.3 | async-start | bytes 16384 | tf_op jit(solution)/shard_map/all_to_all | solution.py:81
  201.0 8.8 %all-to-all-start.5 = ((bf16[4,4,256]{2,1,0:T(4,128)(2,1)}), bf16[4,4,256]{2,1,0:T(4,128)(2,1)S(1)}, u32[]{:S(2)}, u32[]{:S(2)}) async-start(bf16[4,4,256]{2,1,0:T(4,128)(2,1)} %convert_element_type.31), calls=%async_computation.5 | async-start | bytes 16384 | tf_op jit(solution)/shard_map/all_to_all | solution.py:129
Sparse Core Ops, SparseCore 0:
  128.2 15.8 all-gather.2
where the time goes:
time: 225 us; the launch traced here: 223 us
  waiting for transfers between devices  109 us (48%)
  local copies, waits for them, and re-layouts  27.4 us (12%)
  matrix products  25.5 us (11%)
  starting transfers between devices  18.6 us (8%)
  blocking collectives  17.4 us (8%)
  between operations  13.6 us (6%)
  other arithmetic  11 us (5%)
    all_to_all x1, waiting for transfers between devices, per_device(): lax.all_to_all(outgoing[0], 'blocks', split_axis=0, concat_axis=0, tiled=...  92 us
    dot_general x12, matrix products, one_partner(): jnp.einsum('ae,re->ar', local_mat, codes_one, preferred_element_type=jnp....  25.3 us
    all_to_all x1, blocking collectives, per_device(): lax.all_to_all(request_table, 'blocks', split_axis=0, concat_axis=0, tile...  11.7 us
    mul x12, other arithmetic, one_partner(): keep_rows = (local_cluster == cluster_one).astype(jnp.float32) * local_valid  7.76 us
    dynamic_slice x24, local copies, waits for them, and re-layouts, kernel_sums(): lax.scan(one_partner, row_start, (partner_codes, partner_scale, partner_v...  7.12 us
    psum x1, blocking collectives, per_device(): density = lax.psum(density, ('pairs', 'dims'))  5.75 us
    all_to_all x1, waiting for transfers between devices, per_device(): lax.all_to_all(slot_sums.reshape(owner_count, capacity, column_width).ast...  5.47 us
    all_to_all x1, starting transfers between devices, per_device(): lax.all_to_all(outgoing[0], 'blocks', split_axis=0, concat_axis=0, tiled=...  4.99 us
  transfers between devices with their start and end apart: 6, of which 5 were waited for; matrix products, arithmetic and copies ran while one was open for 4% of the time, Pallas kernels for 0%

commit v1 on v0

v1 whole, which is shorter than its diff:
```python
import functools
import math

import jax
import jax.numpy as jnp
from jax import lax
from jax.experimental import pallas as pl
from jax.experimental.pallas import tpu as pltpu
from jax.sharding import PartitionSpec as P

NT = (((1,), (1,)), ((), ()))


def tile_kernel(
    weight_ref, count_ref, own_ref, peer_ref, part_own_ref, part_peer_ref, scale_ref, part_scale_ref,
    rows_ref, columns_ref, total_ref,
):
    blocks, rows, _ = own_ref.shape
    part = part_own_ref.shape[0]
    lanes = 128
    rows_ref[...] = jnp.zeros_like(rows_ref)
    total_ref[...] = jnp.zeros_like(total_ref)
    part_rows = count_ref[blocks]
    part_valid = (lax.broadcasted_iota(jnp.int32, (part, 1), 0) < part_rows).astype(jnp.float32)
    part_scale = jnp.transpose(jnp.broadcast_to(part_scale_ref[...], (8, part)))[:, 0:1]
    for block in range(blocks):

        @pl.when(weight_ref[block] != 0.0)
        def _(block=block):
            gram = lax.dot_general(
                part_own_ref[...], own_ref[block], NT, preferred_element_type=jnp.float32
            ) + lax.dot_general(
                part_peer_ref[...], peer_ref[block], NT, preferred_element_type=jnp.float32
            )
            weight = weight_ref[block]
            row_valid = lax.broadcasted_iota(jnp.int32, (1, rows), 1) < count_ref[block]
            kern = jnp.exp(gram * (part_scale * scale_ref[block : block + 1, :]))
            kern = jnp.where(row_valid, kern, 0.0) * part_valid
            rows_ref[block : block + 1, :] = weight * jnp.sum(kern, axis=0, keepdims=True)
            folded = kern[:, 0:lanes]
            for start in range(lanes, rows, lanes):
                folded = folded + kern[:, start : start + lanes]
            total_ref[...] += weight * folded

    columns_ref[...] = jnp.sum(jnp.transpose(total_ref[...]), axis=0, keepdims=True)


def tile_sums(weights, counts, own, peer, part_own, part_peer, scale, part_scale):
    blocks, rows, width = own.shape
    part = part_own.shape[0]
    smem = pl.BlockSpec(memory_space=pltpu.SMEM)
    vmem = pl.BlockSpec(memory_space=pltpu.VMEM)
    return pl.pallas_call(
        tile_kernel,
        out_shape=(
            jax.ShapeDtypeStruct((blocks, rows), jnp.float32),
            jax.ShapeDtypeStruct((1, part), jnp.float32),
        ),
        in_specs=[smem, smem, vmem, vmem, vmem, vmem, vmem, vmem],
        out_specs=(vmem, vmem),
        scratch_shapes=[pltpu.VMEM((part, 128), jnp.float32)],
        compiler_params=pltpu.CompilerParams(vmem_limit_bytes=24 * 1024 * 1024),
        cost_estimate=pl.CostEstimate(
            flops=4 * blocks * rows * part * width,
            bytes_accessed=4 * blocks * rows * width + 4 * part * width,
            transcendentals=blocks * rows * part,
        ),
    )(weights, counts, own, peer, part_own, part_peer, scale, part_scale)


def per_device(codes, scales, cluster_ids, row_counts, route_offsets, partner_local):
    owners = lax.axis_size("blocks")
    pairs = lax.axis_size("pairs")
    owner = lax.axis_index("blocks")
    pair = lax.axis_index("pairs")
    core = lax.axis_index("dims")
    own_blocks, rows, width = codes.shape
    inverse_root = 1.0 / math.sqrt(width * lax.axis_size("dims"))
    total_rows = own_blocks * rows
    share = total_rows // pairs
    quarter = share // 4
    rounds = owners // 2
    swap = [(0, 1), (1, 0)]
    share_start = pair * share

    flat = codes.reshape(total_rows, width)
    first = lax.dynamic_slice_in_dim(flat, share_start, 2 * quarter, 0)
    peer_codes = lax.ppermute(codes, "dims", swap)
    second_start = share_start + (2 + core) * quarter
    second = jnp.stack([
        lax.dynamic_slice_in_dim(flat, second_start, quarter, 0),
        lax.dynamic_slice_in_dim(peer_codes.reshape(total_rows, width), second_start, quarter, 0),
    ])

    targets = (owner + 1 + route_offsets.reshape(-1)) % owners
    named = targets * own_blocks + partner_local.reshape(-1)
    block_ids = jnp.arange(owners * own_blocks, dtype=jnp.int32)
    counted = jnp.sum((named[None, :] == block_ids[:, None]).astype(jnp.float32), axis=1)
    listed = counted
    for step in range(1, pairs):
        listed = listed + lax.ppermute(
            counted, "pairs", [(i, (i + step) % pairs) for i in range(pairs)]
        )
    listed = listed.reshape(owners, own_blocks)

    scale_wide = scales.astype(jnp.float32)
    scale_root = scale_wide * inverse_root
    own_valid = row_counts

    def sends(step):
        if 2 * step == owners:
            return [((o + step - 1) % owners, (o + step) % owners) for o in range(owners // 2)]
        return [(i, (i + 1) % owners) for i in range(owners)]

    def origins(step):
        return owners // 2 if 2 * step == owners else owners

    row_total = jnp.zeros((own_blocks, rows), jnp.float32)
    column_total = jnp.zeros((total_rows,), jnp.float32)
    first_place = share_start + core * quarter
    for step in range(1, rounds + 1):
        perm = sends(step)
        direct = [(o, (o + step) % owners) for o in range(origins(step))]
        back = [(b, a) for a, b in direct]
        first = lax.ppermute(first, "blocks", perm)
        second = lax.ppermute(second, "blocks", perm)
        to_owner = (owner + step) % owners
        note = jnp.concatenate([
            cluster_ids.astype(jnp.float32),
            row_counts.astype(jnp.float32),
            lax.dynamic_index_in_dim(listed, to_owner, 0, keepdims=False),
        ])
        packed = jnp.concatenate([scale_wide.reshape(-1), note])
        packed = lax.ppermute(packed, "blocks", direct)
        from_owner = (owner - step) % owners
        active = (from_owner < origins(step)).astype(jnp.float32)
        part_scales = packed[:total_rows]
        part_cluster, part_counts, part_listed = [
            packed[total_rows + i * own_blocks : total_rows + (i + 1) * own_blocks] for i in range(3)
        ]
        own_listed = lax.dynamic_index_in_dim(listed, from_owner, 0, keepdims=False)
        all_weights = jnp.where(
            part_cluster[:, None] == cluster_ids.astype(jnp.float32)[None, :],
            own_listed[:, None] + part_listed[None, :],
            0.0,
        ) * active

        def chunk_sums(place, part_own, part_peer):
            block = place // rows
            offset = place % rows
            weights = lax.dynamic_index_in_dim(all_weights, block, 0, keepdims=False)
            left = lax.dynamic_index_in_dim(part_counts, block, 0).astype(jnp.int32) - offset
            counts = jnp.concatenate([row_counts, left])
            part_scale = lax.dynamic_slice_in_dim(part_scales, place, quarter, 0)[None, :]
            return tile_sums(
                weights, counts, codes, peer_codes, part_own, part_peer, scale_root, part_scale
            )

        mine = lax.dynamic_slice_in_dim(first, core * quarter, quarter, 0)
        other = lax.dynamic_slice_in_dim(first, (1 - core) * quarter, quarter, 0)
        first_rows, first_columns = chunk_sums(first_place, mine, lax.ppermute(other, "dims", swap))
        second_rows, second_columns = chunk_sums(second_start, second[0], second[1])
        row_total = row_total + first_rows + second_rows
        columns = lax.ppermute(
            jnp.concatenate([first_columns, second_columns], axis=0), "blocks", back
        )
        column_total = lax.dynamic_update_slice_in_dim(
            column_total,
            lax.dynamic_slice_in_dim(column_total, first_place, quarter, 0) + columns[0],
            first_place, 0,
        )
        column_total = lax.dynamic_update_slice_in_dim(
            column_total,
            lax.dynamic_slice_in_dim(column_total, second_start, quarter, 0) + columns[1],
            second_start, 0,
        )
    density = row_total + column_total.reshape(own_blocks, rows)
    density = lax.psum(density, ("pairs", "dims"))
    return jnp.log1p(density)


def solution(mesh):
    return jax.shard_map(
        per_device,
        mesh=mesh,
        in_specs=(
            P(("groups", "blocks"), None, "dims"),
            P(("groups", "blocks"), None),
            P(("groups", "blocks")),
            P(("groups", "blocks")),
            P(("groups", "blocks"), "pairs", None, None),
            P(("groups", "blocks"), "pairs", None),
        ),
        out_specs=P(("groups", "blocks"), None),
        check_vma=False,
    )
```

time: 225 us -> 79.1 us (0.35)
  waiting for transfers between devices: 109 us -> 22.4 us
  matrix products: 25.5 us -> 0 us
  local copies, waits for them, and re-layouts: 27.4 us -> 5.26 us
  blocking collectives: 17.4 us -> 6.02 us
  between operations: 13.6 us -> 2.82 us
  starting transfers between devices: 18.6 us -> 28.3 us
  Pallas kernels: 0 us -> 9.33 us
  other arithmetic: 11 us -> 4.87 us
    all_to_all x5 -> x0, waiting for transfers between devices: 109 us -> none  [the longest x1 92 us: per_device(): lax.all_to_all(outgoing[0], 'blocks', split_axis=0, concat_axis=0, tiled=...]
    ppermute x0 -> x12, starting transfers between devices: none -> 28.3 us  [the longest x2 13.8 us: per_device(): lax.ppermute(jnp.concatenate([first_columns, second_columns], axis=0), 'b...]
    dot_general x14 -> x0, matrix products: 25.5 us -> none  [the longest x12 25.3 us: one_partner(): jnp.einsum('ae,re->ar', local_mat, codes_one, preferred_element_type=jnp....]
    ppermute x0 -> x12, waiting for transfers between devices: none -> 22.4 us  [the longest x2 8.58 us: per_device(): lax.ppermute(jnp.concatenate([first_columns, second_columns], axis=0), 'b...]
    all_to_all x5 -> x0, starting transfers between devices: 18.5 us -> none  [the longest x1 4.99 us: per_device(): lax.all_to_all(outgoing[0], 'blocks', split_axis=0, concat_axis=0, tiled=...]
    gather x7 -> x0, local copies, waits for them, and re-layouts: 12.2 us -> none  [the longest x1 4.74 us: per_device(): partner_codes = arrived[0].reshape(slot_total, rows, source_width)[slot_ids]]
    all_to_all x1 -> x0, blocking collectives: 11.7 us -> none  [per_device(): lax.all_to_all(request_table, 'blocks', split_axis=0, concat_axis=0, tile...]
    pallas_call x0 -> x4, Pallas kernels: none -> 9.33 us  [tile_sums(): pl.pallas_call(tile_kernel, out_shape=(jax.ShapeDtypeStruct((blocks, rows...]
  transfers between devices with their start and end apart: 6 -> 12, of which waited for: 5 -> 4; matrix products, arithmetic and copies ran while one was open for 4% -> 12% of each run, Pallas kernels for 0% -> 9%
where the time goes in v1:
time: 79.1 us; the launch traced here: 79 us
  starting transfers between devices  28.3 us (36%)
  waiting for transfers between devices  22.4 us (28%)
  Pallas kernels  9.33 us (12%)
  blocking collectives  6.02 us (8%)
  local copies, waits for them, and re-layouts  5.26 us (7%)
  other arithmetic  4.87 us (6%)
  between operations  2.82 us (4%)
    ppermute x2, starting transfers between devices, per_device(): lax.ppermute(jnp.concatenate([first_columns, second_columns], axis=0), 'b...  13.8 us
    pallas_call x4, Pallas kernels, tile_sums(): pl.pallas_call(tile_kernel, out_shape=(jax.ShapeDtypeStruct((blocks, rows...  9.33 us
    ppermute x2, waiting for transfers between devices, per_device(): lax.ppermute(jnp.concatenate([first_columns, second_columns], axis=0), 'b...  8.58 us
    ppermute x2, waiting for transfers between devices, per_device(): second = lax.ppermute(second, 'blocks', perm)  7.21 us
    psum x1, blocking collectives, per_device(): density = lax.psum(density, ('pairs', 'dims'))  6.02 us
    ppermute x2, waiting for transfers between devices, per_device(): packed = lax.ppermute(packed, 'blocks', direct)  5.75 us
    ppermute x2, starting transfers between devices, per_device(): packed = lax.ppermute(packed, 'blocks', direct)  4.84 us
    ppermute x2, starting transfers between devices, per_device(): second = lax.ppermute(second, 'blocks', perm)  3.68 us
  transfers between devices with their start and end apart: 12, of which 4 were waited for; matrix products, arithmetic and copies ran while one was open for 12% of the time, Pallas kernels for 9%

profile of v1, /device:TPU:0, one launch (start us, length us, event | category | flops | bytes accessed | tf_op | source)
XLA Modules:
  0.0 79.0 jit_solution(10061505694143990941)
XLA Ops:
  0.0 0.5 collective-permute-start.2
  0.5 0.7 fusion.1
  1.1 0.1 convert_reduce_fusion
  1.2 2.5 %collective-permute-start = (f32[32]{0:T(128)S(1)}, f32[32]{0:T(128)S(1)}, u32[]{:S(2)}, u32[]{:S(2)}) collective-permute-start(f32[32]{0:T(128)S(1)} %convert_reduce_fusion), channel_id=1, source_target_pairs={{0,2},{2,0},{1,3},{3,1},{4,6},{6,4},{5,7},{7,5},{8,10},{10,8},{9,1... | collective-permute-start | bytes 392 | tf_op jit(solution)/shard_map/ppermute | solution.py:101
  3.8 1.1 %constant_dynamic-slice_fusion.9 = bf16[512,512]{1,0:T(8,128)(2,1)S(1)} fusion(bf16[2048,512]{1,0:T(8,128)(2,1)} %bitcast.47, s32[]{:T(128)S(6)} %select_n.121), kind=kLoop, calls=%fused_computation.23 | loop fusion | bytes 1048580 | tf_op jit(solution)/shard_map/dynamic_slice | solution.py:87
  4.9 1.6 %collective-permute-start.3 = (bf16[512,512]{1,0:T(8,128)(2,1)S(1)}, bf16[512,512]{1,0:T(8,128)(2,1)S(1)}, u32[]{:S(2)}, u32[]{:S(2)}) collective-permute-start(bf16[512,512]{1,0:T(8,128)(2,1)S(1)} %constant_dynamic-slice_fusion.9), channel_id=1, source_target_pairs={{0,4},{4,8},{8,12},{12,0},{1,5},{5,9},{9,13},{13,1},{2,6},{6,10},{... | collective-permute-start | bytes 1572872 | tf_op jit(solution)/shard_map/ppermute | solution.py:125
  6.5 0.7 convert_element_type.35
  7.1 0.7 convert_element_type.36
  7.8 0.7 convert_bitcast_fusion
  8.5 0.7 convert_multiply_fusion.scale_ref
  9.2 0.0 collective-permute-done
  9.2 0.1 reshape.55
  9.3 0.1 concatenate.24
  9.4 1.6 %collective-permute-start.1 = (f32[2072]{0:T(1024)S(1)}, f32[2072]{0:T(1024)S(1)}, u32[]{:S(2)}, u32[]{:S(2)}) collective-permute-start(f32[2072]{0:T(1024)S(1)} %concatenate.24), channel_id=1, source_target_pairs={{0,4},{4,8},{8,12},{12,0},{1,5},{5,9},{9,13},{13,1},{2,6},{6,10},{... | collective-permute-start | bytes 24872 | tf_op jit(solution)/shard_map/ppermute | solution.py:134
  11.0 1.0 %dynamic-slice_bitcast_fusion.1 = bf16[1,256,512]{2,1,0:T(8,128)(2,1)S(1)} fusion(bf16[2048,512]{1,0:T(8,128)(2,1)} %bitcast.48, s32[]{:T(128)S(6)} %select_n.128), kind=kLoop, calls=%fused_computation.6 | loop fusion | bytes 524292 | tf_op jit(solution)/shard_map/stack | solution.py:90
  11.9 0.0 copy-start
  12.0 0.1 concatenate.27
  12.1 3.3 %collective-permute-start.6 = (f32[2072]{0:T(1024)S(1)}, f32[2072]{0:T(1024)S(1)}, u32[]{:S(2)}, u32[]{:S(2)}) collective-permute-start(f32[2072]{0:T(1024)S(1)} %concatenate.27), channel_id=1, source_target_pairs={{0,8},{4,12},{1,9},{5,13},{2,10},{6,14},{3,11},{7,15},{16,24},{20,... | collective-permute-start | bytes 24872 | tf_op jit(solution)/shard_map/ppermute | solution.py:134
  15.3 5.7 %collective-permute-done.1 = f32[2072]{0:T(1024)S(1)} collective-permute-done((f32[2072]{0:T(1024)S(1)}, f32[2072]{0:T(1024)S(1)}, u32[]{:S(2)}, u32[]{:S(2)}) %collective-permute-start.1) | collective-permute-done | bytes 8320 | tf_op jit(solution)/shard_map/ppermute | solution.py:134
  21.1 0.1 fusion.12
  21.2 0.0 collective-permute-done.6
  21.2 0.1 fusion.11
  21.2 0.7 fusion.17
  24.5 0.1 select_multiply_fusion
  24.5 0.7 pad_add_fusion.2
  25.3 0.0 collective-permute-done.3
  25.3 0.7 collective-permute-start.7
  26.0 0.0 collective-permute-done.2.peer_ref
  26.0 1.0 %dynamic-slice_bitcast_fusion = bf16[1,256,512]{2,1,0:T(8,128)(2,1)S(1)} fusion(bf16[2048,512]{1,0:T(8,128)(2,1)} %bitcast.11, s32[]{:T(128)S(6)} %select_n.128), kind=kLoop, calls=%fused_computation.5 | loop fusion | bytes 524292 | tf_op jit(solution)/shard_map/stack | solution.py:90
  27.0 0.1 pad_maximum_fusion
  27.0 3.0 %collective-permute-start.5 = (bf16[2,256,512]{2,1,0:T(8,128)(2,1)S(1)}, bf16[2,256,512]{2,1,0:T(8,128)(2,1)S(1)}, u32[]{:S(2)}, u32[]{:S(2)}) collective-permute-start(bf16[2,256,512]{2,1,0:T(8,128)(2,1)S(1)} %pad_maximum_fusion), channel_id=1, source_target_pairs={{0,4},{4,8},{8,12},{12,0},{1,5},{5,9},{9,13},{13,1},{2,6},{6,10},{... | collective-permute-start | bytes 1572872 | tf_op jit(solution)/shard_map/ppermute | solution.py:126
  30.0 0.1 collective-permute-start.4
  30.2 0.1 fusion.13
  30.2 0.0 collective-permute-done.7
  30.3 0.5 collective-permute-start.8
  30.8 0.8 %collective-permute-done.4.part_peer_ref = bf16[256,512]{1,0:T(8,128)(2,1)S(1)} collective-permute-done((bf16[256,512]{1,0:T(8,128)(2,1)S(1)}, bf16[256,512]{1,0:T(8,128)(2,1)S(1)}, u32[]{:S(2)}, u32[]{:S(2)}) %collective-permute-start.4) | collective-permute-done | bytes 262176 | tf_op jit(solution)/shard_map/ppermute | solution.py:161
  31.6 0.0 copy-done
  31.6 3.3 %shard_map.64 = (f32[8,256]{1,0:T(8,128)S(1)}, f32[1,256]{1,0:T(1,128)S(1)}) custom-call(f32[8]{0:T(128)S(1)} %get-tuple-element.41.weight_ref, s32[9]{0:T(128)S(1)} %get-tuple-element.54.count_ref, bf16[8,256,512]{2,1,0:T(8,128)(2,1)S(1)} %copy-done, bf16[8,256,512]{2,1,0:T(8,128)(2,1)} %collective-permute-done.2.peer_ref, ...), custom_call_target="tpu_custom_call" | custom-call | flops 1073741824 | bytes 4718592 | tf_op jit(solution)/shard_map/pallas_call | solution.py:53
  35.0 7.2 %collective-permute-done.5 = bf16[2,256,512]{2,1,0:T(8,128)(2,1)S(1)} collective-permute-done((bf16[2,256,512]{2,1,0:T(8,128)(2,1)S(1)}, bf16[2,256,512]{2,1,0:T(8,128)(2,1)S(1)}, u32[]{:S(2)}, u32[]{:S(2)}) %collective-permute-start.5) | collective-permute-done | bytes 524320 | tf_op jit(solution)/shard_map/ppermute | solution.py:126
  42.2 0.7 collective-permute-start.9
  42.9 2.2 %shard_map.65 = (f32[8,256]{1,0:T(8,128)S(1)}, f32[1,256]{1,0:T(1,128)S(1)}) custom-call(f32[8]{0:T(128)S(1)} %get-tuple-element.42.weight_ref, s32[9]{0:T(128)S(1)} %get-tuple-element.52.count_ref, bf16[8,256,512]{2,1,0:T(8,128)(2,1)S(1)} %copy-done, bf16[8,256,512]{2,1,0:T(8,128)(2,1)} %collective-permute-done.2.peer_ref, ...), custom_call_target="tpu_custom_call" | custom-call | flops 1073741824 | bytes 4718592 | tf_op jit(solution)/shard_map/pallas_call | solution.py:53
  45.2 12.6 %collective-permute-start.10 = (f32[2,256]{1,0:T(2,128)S(1)}, f32[2,256]{1,0:T(2,128)S(1)}, u32[]{:S(2)}, u32[]{:S(2)}) collective-permute-start(f32[2,256]{1,0:T(2,128)S(1)} %pad_maximum_fusion.1), channel_id=1, source_target_pairs={{4,0},{8,4},{12,8},{0,12},{5,1},{9,5},{13,9},{1,13},{6,2},{10,6},{... | collective-permute-start | bytes 6152 | tf_op jit(solution)/shard_map/ppermute | solution.py:164
  57.7 0.0 collective-permute-done.8.part_peer_ref
  57.7 1.9 %shard_map.66 = (f32[8,256]{1,0:T(8,128)S(1)}, f32[1,256]{1,0:T(1,128)S(1)}) custom-call(f32[8]{0:T(128)S(1)} %get-tuple-element.39.weight_ref, s32[9]{0:T(128)S(1)} %get-tuple-element.51.count_ref, bf16[8,256,512]{2,1,0:T(8,128)(2,1)S(1)} %copy-done, bf16[8,256,512]{2,1,0:T(8,128)(2,1)} %collective-permute-done.2.peer_ref, ...), custom_call_target="tpu_custom_call" | custom-call | flops 1073741824 | bytes 4718592 | tf_op jit(solution)/shard_map/pallas_call | solution.py:53
  59.6 0.0 collective-permute-done.10
  59.7 0.3 dynamic_update_slice.12
  60.0 0.0 collective-permute-done.9
  60.0 1.9 %shard_map.67 = (f32[8,256]{1,0:T(8,128)S(1)}, f32[1,256]{1,0:T(1,128)S(1)}) custom-call(f32[8]{0:T(128)S(1)} %get-tuple-element.40.weight_ref, s32[9]{0:T(128)S(1)} %get-tuple-element.53.count_ref, bf16[8,256,512]{2,1,0:T(8,128)(2,1)S(1)} %copy-done, bf16[8,256,512]{2,1,0:T(8,128)(2,1)} %collective-permute-done.2.peer_ref, ...), custom_call_target="tpu_custom_call" | custom-call | flops 1073741824 | bytes 4718592 | tf_op jit(solution)/shard_map/pallas_call | solution.py:53
  61.9 1.3 %collective-permute-start.11 = (f32[2,256]{1,0:T(2,128)S(1)}, f32[2,256]{1,0:T(2,128)S(1)}, u32[]{:S(2)}, u32[]{:S(2)}) collective-permute-start(f32[2,256]{1,0:T(2,128)S(1)} %pad_maximum_fusion.2), channel_id=1, source_target_pairs={{8,0},{12,4},{9,1},{13,5},{10,2},{14,6},{11,3},{15,7},{24,16},{28,... | collective-permute-start | bytes 6152 | tf_op jit(solution)/shard_map/ppermute | solution.py:164
  63.2 0.2 add_dynamic-update-slice_fusion.2
  63.4 8.6 %collective-permute-done.11 = f32[2,256]{1,0:T(2,128)S(1)} collective-permute-done((f32[2,256]{1,0:T(2,128)S(1)}, f32[2,256]{1,0:T(2,128)S(1)}, u32[]{:S(2)}, u32[]{:S(2)}) %collective-permute-start.11) | collective-permute-done | bytes 2080 | tf_op jit(solution)/shard_map/ppermute | solution.py:164
  72.0 0.2 add_dynamic-update-slice_fusion.1
  72.1 0.2 add_dynamic-update-slice_fusion
  72.3 6.0 %psum.7 = f32[8,256]{1,0:T(8,128)S(1)} all-reduce(f32[8,256]{1,0:T(8,128)S(1)} %add_add_fusion), channel_id=1, replica_groups=mesh['groups'=2,'blocks'=4,'pairs'=2,'dims'=2] {'pairs','dims'}, use_global_device_ids=true, to_apply=%region_1.2 | all-reduce | flops 2048 | bytes 16384 | tf_op jit(solution)/shard_map/psum | solution.py:178
  78.3 0.6 log1p.3
  (18 shorter events, 0.2 us)
Async XLA Ops:
  0.0 26.0 %collective-permute-start.2 = (bf16[8,256,512]{2,1,0:T(8,128)(2,1)}, bf16[8,256,512]{2,1,0:T(8,128)(2,1)}, u32[]{:S(2)}, u32[]{:S(2)}) collective-permute-start(bf16[8,256,512]{2,1,0:T(8,128)(2,1)} %own_ref.7), channel_id=1, source_target_pairs={{0,1},{1,0},{2,3},{3,2},{4,5},{5,4},{6,7},{7,6},{8,9},{9,8},{10,11... | collective-permute-start | bytes 6291464 | tf_op jit(solution)/shard_map/ppermute | solution.py:88
  1.2 8.0 %collective-permute-start = (f32[32]{0:T(128)S(1)}, f32[32]{0:T(128)S(1)}, u32[]{:S(2)}, u32[]{:S(2)}) collective-permute-start(f32[32]{0:T(128)S(1)} %convert_reduce_fusion), channel_id=1, source_target_pairs={{0,2},{2,0},{1,3},{3,1},{4,6},{6,4},{5,7},{7,5},{8,10},{10,8},{9,1... | collective-permute-start | bytes 392 | tf_op jit(solution)/shard_map/ppermute | solution.py:101
  4.9 20.4 %collective-permute-start.3 = (bf16[512,512]{1,0:T(8,128)(2,1)S(1)}, bf16[512,512]{1,0:T(8,128)(2,1)S(1)}, u32[]{:S(2)}, u32[]{:S(2)}) collective-permute-start(bf16[512,512]{1,0:T(8,128)(2,1)S(1)} %constant_dynamic-slice_fusion.9), channel_id=1, source_target_pairs={{0,4},{4,8},{8,12},{12,0},{1,5},{5,9},{9,13},{13,1},{2,6},{6,10},{... | collective-permute-start | bytes 1572872 | tf_op jit(solution)/shard_map/ppermute | solution.py:125
  9.4 11.7 %collective-permute-start.1 = (f32[2072]{0:T(1024)S(1)}, f32[2072]{0:T(1024)S(1)}, u32[]{:S(2)}, u32[]{:S(2)}) collective-permute-start(f32[2072]{0:T(1024)S(1)} %concatenate.24), channel_id=1, source_target_pairs={{0,4},{4,8},{8,12},{12,0},{1,5},{5,9},{9,13},{13,1},{2,6},{6,10},{... | collective-permute-start | bytes 24872 | tf_op jit(solution)/shard_map/ppermute | solution.py:134
  11.9 19.7 %copy-start = (bf16[8,256,512]{2,1,0:T(8,128)(2,1)S(1)}, bf16[8,256,512]{2,1,0:T(8,128)(2,1)}, u32[]{:S(2)}) copy-start(bf16[8,256,512]{2,1,0:T(8,128)(2,1)} %own_ref.7) | copy-start | bytes 6291460
  12.1 9.1 %collective-permute-start.6 = (f32[2072]{0:T(1024)S(1)}, f32[2072]{0:T(1024)S(1)}, u32[]{:S(2)}, u32[]{:S(2)}) collective-permute-start(f32[2072]{0:T(1024)S(1)} %concatenate.27), channel_id=1, source_target_pairs={{0,8},{4,12},{1,9},{5,13},{2,10},{6,14},{3,11},{7,15},{16,24},{20,... | collective-permute-start | bytes 24872 | tf_op jit(solution)/shard_map/ppermute | solution.py:134
  25.3 5.0 %collective-permute-start.7 = (bf16[512,512]{1,0:T(8,128)(2,1)S(1)}, bf16[512,512]{1,0:T(8,128)(2,1)S(1)}, u32[]{:S(2)}, u32[]{:S(2)}) collective-permute-start(bf16[512,512]{1,0:T(8,128)(2,1)S(1)} %collective-permute-done.3), channel_id=1, source_target_pairs={{4,8},{8,12},{5,9},{9,13},{6,10},{10,14},{7,11},{11,15},{20,24},{2... | collective-permute-start | bytes 1572872 | tf_op jit(solution)/shard_map/ppermute | solution.py:125
  27.0 15.2 %collective-permute-start.5 = (bf16[2,256,512]{2,1,0:T(8,128)(2,1)S(1)}, bf16[2,256,512]{2,1,0:T(8,128)(2,1)S(1)}, u32[]{:S(2)}, u32[]{:S(2)}) collective-permute-start(bf16[2,256,512]{2,1,0:T(8,128)(2,1)S(1)} %pad_maximum_fusion), channel_id=1, source_target_pairs={{0,4},{4,8},{8,12},{12,0},{1,5},{5,9},{9,13},{13,1},{2,6},{6,10},{... | collective-permute-start | bytes 1572872 | tf_op jit(solution)/shard_map/ppermute | solution.py:126
  30.0 1.6 %collective-permute-start.4 = (bf16[256,512]{1,0:T(8,128)(2,1)S(1)}, bf16[256,512]{1,0:T(8,128)(2,1)S(1)}, u32[]{:S(2)}, u32[]{:S(2)}) collective-permute-start(bf16[256,512]{1,0:T(8,128)(2,1)S(1)} %get-tuple-element.25), channel_id=1, source_target_pairs={{0,1},{1,0},{2,3},{3,2},{4,5},{5,4},{6,7},{7,6},{8,9},{9,8},{10,11... | collective-permute-start | bytes 786440 | tf_op jit(solution)/shard_map/ppermute | solution.py:161
  30.3 27.5 %collective-permute-start.8 = (bf16[256,512]{1,0:T(8,128)(2,1)S(1)}, bf16[256,512]{1,0:T(8,128)(2,1)S(1)}, u32[]{:S(2)}, u32[]{:S(2)}) collective-permute-start(bf16[256,512]{1,0:T(8,128)(2,1)S(1)} %get-tuple-element.21), channel_id=1, source_target_pairs={{0,1},{1,0},{2,3},{3,2},{4,5},{5,4},{6,7},{7,6},{8,9},{9,8},{10,11... | collective-permute-start | bytes 786440 | tf_op jit(solution)/shard_map/ppermute | solution.py:161
  42.2 17.7 %collective-permute-start.9 = (bf16[2,256,512]{2,1,0:T(8,128)(2,1)S(1)}, bf16[2,256,512]{2,1,0:T(8,128)(2,1)S(1)}, u32[]{:S(2)}, u32[]{:S(2)}) collective-permute-start(bf16[2,256,512]{2,1,0:T(8,128)(2,1)S(1)} %collective-permute-done.5), channel_id=1, source_target_pairs={{4,8},{8,12},{5,9},{9,13},{6,10},{10,14},{7,11},{11,15},{20,24},{2... | collective-permute-start | bytes 1572872 | tf_op jit(solution)/shard_map/ppermute | solution.py:126
  45.2 14.4 %collective-permute-start.10 = (f32[2,256]{1,0:T(2,128)S(1)}, f32[2,256]{1,0:T(2,128)S(1)}, u32[]{:S(2)}, u32[]{:S(2)}) collective-permute-start(f32[2,256]{1,0:T(2,128)S(1)} %pad_maximum_fusion.1), channel_id=1, source_target_pairs={{4,0},{8,4},{12,8},{0,12},{5,1},{9,5},{13,9},{1,13},{6,2},{10,6},{... | collective-permute-start | bytes 6152 | tf_op jit(solution)/shard_map/ppermute | solution.py:164
  61.9 10.1 %collective-permute-start.11 = (f32[2,256]{1,0:T(2,128)S(1)}, f32[2,256]{1,0:T(2,128)S(1)}, u32[]{:S(2)}, u32[]{:S(2)}) collective-permute-start(f32[2,256]{1,0:T(2,128)S(1)} %pad_maximum_fusion.2), channel_id=1, source_target_pairs={{8,0},{12,4},{9,1},{13,5},{10,2},{14,6},{11,3},{15,7},{24,16},{28,... | collective-permute-start | bytes 6152 | tf_op jit(solution)/shard_map/ppermute | solution.py:164

commit v2 on v1

v2 whole, which is shorter than its diff:
```python
import math

import jax
import jax.numpy as jnp
from jax import lax
from jax.experimental import pallas as pl
from jax.experimental.pallas import tpu as pltpu
from jax.sharding import PartitionSpec as P

NT = (((1,), (1,)), ((), ()))
LANES = 128


def tile_kernel(info_ref, units_ref, own_ref, peer_ref, *refs):
    count = len(refs) - 7
    parts = refs[:count]
    scale_ref, part_scale_ref, rows_ref, columns_ref, held_ref, total_ref, copied = refs[count:]
    blocks, rows, _ = own_ref.shape
    segments, unit = columns_ref.shape

    def part(half, segment):
        return parts[2 * segment + half][:unit, :]

    def copies(block):
        return [
            pltpu.make_async_copy(whole.at[block], held_ref.at[block, half], copied.at[block, half])
            for half, whole in enumerate((own_ref, peer_ref))
        ]

    valid, weights = [], []
    for segment in range(segments):
        first_row = units_ref[segment] * unit
        part_block = first_row // rows
        left = info_ref[4 * blocks + part_block] - (first_row - part_block * rows)
        valid.append(left)
        weights.append([
            jnp.where(
                (info_ref[3 * blocks + part_block] == info_ref[block]) & (left > 0),
                info_ref[2 * blocks + part_block] + info_ref[5 * blocks + block],
                0,
            ) * info_ref[6 * blocks]
            for block in range(blocks)
        ])
    needed = [sum(weights[segment][block] for segment in range(segments)) for block in range(blocks)]
    for block in range(blocks):

        @pl.when(needed[block] != 0)
        def _(block=block):
            for copy in copies(block):
                copy.start()

    rows_ref[...] = jnp.zeros_like(rows_ref)
    total_ref[...] = jnp.zeros_like(total_ref)
    for block in range(blocks):

        @pl.when(needed[block] != 0)
        def _(block=block):
            for copy in copies(block):
                copy.wait()
            for segment in range(segments):

                @pl.when(weights[segment][block] != 0)
                def _(segment=segment):
                    gram = lax.dot_general(
                        part(0, segment), held_ref[block, 0], NT, preferred_element_type=jnp.float32
                    ) + lax.dot_general(
                        part(1, segment), held_ref[block, 1], NT, preferred_element_type=jnp.float32
                    )
                    part_scale = jnp.transpose(jnp.broadcast_to(
                        part_scale_ref[pl.ds(units_ref[segment], 1), :], (8, unit)
                    ))[:, 0:1]
                    kern = jnp.exp(gram * (part_scale * scale_ref[block : block + 1, :]))
                    row_valid = lax.broadcasted_iota(jnp.int32, (1, rows), 1) < info_ref[blocks + block]
                    part_valid = lax.broadcasted_iota(jnp.int32, (unit, 1), 0) < valid[segment]
                    kern = jnp.where(row_valid & part_valid, kern, 0.0)
                    factor = weights[segment][block].astype(jnp.float32)
                    rows_ref[block : block + 1, :] += factor * jnp.sum(kern, axis=0, keepdims=True)
                    folded = kern[:, 0:LANES]
                    for start in range(LANES, rows, LANES):
                        folded = folded + kern[:, start : start + LANES]
                    total_ref[segment] += factor * folded

    for segment in range(segments):
        columns_ref[segment : segment + 1, :] = jnp.sum(
            jnp.transpose(total_ref[segment]), axis=0, keepdims=True
        )


def tile_sums(info, units, own, peer, parts, scale, part_scale):
    blocks, rows, width = own.shape
    segments, unit = len(parts) // 2, part_scale.shape[1]
    smem = pl.BlockSpec(memory_space=pltpu.SMEM)
    vmem = pl.BlockSpec(memory_space=pltpu.VMEM)
    held = pl.BlockSpec(memory_space=pl.ANY)
    return pl.pallas_call(
        tile_kernel,
        out_shape=(
            jax.ShapeDtypeStruct((blocks, rows), jnp.float32),
            jax.ShapeDtypeStruct((segments, unit), jnp.float32),
        ),
        in_specs=[smem, smem, held, held] + [vmem] * (2 + len(parts)),
        out_specs=(vmem, vmem),
        scratch_shapes=[
            pltpu.VMEM((blocks, 2, rows, width), own.dtype),
            pltpu.VMEM((segments, unit, LANES), jnp.float32),
            pltpu.SemaphoreType.DMA((blocks, 2)),
        ],
        compiler_params=pltpu.CompilerParams(vmem_limit_bytes=32 * 1024 * 1024),
        cost_estimate=pl.CostEstimate(flops=0, bytes_accessed=0, transcendentals=0),
    )(info, units, own, peer, *parts, scale, part_scale)


def per_device(codes, scales, cluster_ids, row_counts, route_offsets, partner_local):
    groups = lax.axis_size("groups")
    owners = lax.axis_size("blocks")
    pairs = lax.axis_size("pairs")
    group = lax.axis_index("groups")
    owner = lax.axis_index("blocks")
    pair = lax.axis_index("pairs")
    core = lax.axis_index("dims")
    blocks, rows, width = codes.shape
    inverse_root = 1.0 / math.sqrt(width * lax.axis_size("dims"))
    share = blocks * rows // pairs
    unit = share // 4
    rounds = owners // 2
    swap = [(0, 1), (1, 0)]
    line = ("groups", "blocks")

    def place(g, o):
        o = o % owners
        return g * owners + (o if g % 2 == 0 else owners - 1 - o)

    sign = jnp.where(group % 2 == 0, 1, -1)
    ring_place = jnp.where(group % 2 == 0, owner, owners - 1 - owner)

    def origins(step):
        return owners // 2 if 2 * step == owners else owners

    def moves(step, start, stop):
        return [
            (place(g, o + start), place(g, o + stop))
            for g in range(groups) for o in range(origins(step))
        ]

    def beside(at):
        return at + owners if at // owners % 2 == 0 else at - owners

    after = lax.optimization_barrier
    detour = groups % 2 == 0

    flat = codes.reshape(-1, width)

    def quarter(number):
        return lax.dynamic_slice_in_dim(flat, pair * share + number * unit, unit, 0)

    first = [quarter(1 - core)]
    first[0], flat, route_offsets, codes_held = after((first[0], flat, route_offsets, codes))
    first.append(quarter(core))
    second = [quarter(3 - core), quarter(2 + core)]

    def send(arrays, to):
        return [lax.ppermute(array, line, to) for array in arrays]

    first = send(first, moves(1, 0, 1))
    peer_codes = lax.ppermute(codes_held, "dims", swap)

    targets = (owner + 1 + route_offsets.reshape(-1)) % owners
    named = targets * blocks + partner_local.reshape(-1)
    block_ids = jnp.arange(owners * blocks, dtype=jnp.int32)
    counted = jnp.sum((named[None, :] == block_ids[:, None]).astype(jnp.float32), axis=1)
    listed = counted
    for step in range(1, pairs):
        listed = listed + lax.ppermute(
            counted, "pairs", [(i, (i + step) % pairs) for i in range(pairs)]
        )
    note = jnp.concatenate([
        value.reshape(-1).astype(codes.dtype) for value in (scales, cluster_ids, row_counts, listed)
    ])
    note_rows = -(-note.shape[0] // (16 * width)) * 16
    note = jnp.pad(note, (0, note_rows * width - note.shape[0])).reshape(note_rows, width)
    own_listed = listed.reshape(owners, blocks).astype(jnp.int32)
    second[0] = jnp.concatenate([second[0], note], axis=0)
    second[0], second[1] = after((second[0], second[1]))
    second = send(second, moves(1, 0, 1))

    scale_root = scales.astype(jnp.float32) * inverse_root
    units = jnp.stack([pair * 4 + core, pair * 4 + core + 2]).astype(jnp.int32)

    row_parts, column_parts = [], []
    for step in range(1, rounds + 1):
        held, held_second = list(first), list(second)
        if step < rounds:
            perm = moves(step + 1, step, step + 1)
            if detour:
                aside = [(s, beside(s)) for s, _ in perm]
                home = [(beside(s), t) for s, t in perm]
                one = lax.ppermute(held[0], line, aside)
                one, held[1] = after((one, held[1]))
                two = lax.ppermute(held[1], line, aside)
                two, held_second[0] = after((two, held_second[0]))
                held_second[0], held_second[1] = after((held_second[0], held_second[1]))
                first = send([one, two], home)
            else:
                first = send(held, perm)
            second = send(held_second, perm)
        note = held_second[0][unit:].reshape(-1)
        scale_end = blocks * rows
        cluster_end, count_end = scale_end + blocks, scale_end + 2 * blocks
        part_scale = note[:scale_end].astype(jnp.float32).reshape(-1, unit)
        from_owner = (owner - sign * step) % owners
        active = ((ring_place - step) % owners) < origins(step)
        info = jnp.concatenate([
            cluster_ids,
            row_counts,
            lax.dynamic_index_in_dim(own_listed, from_owner, 0, keepdims=False),
            note[scale_end:count_end].astype(jnp.int32),
            lax.dynamic_slice_in_dim(note, count_end + owner * blocks, blocks, 0).astype(jnp.int32),
            active.astype(jnp.int32)[None],
        ])
        others = [lax.ppermute(part, "dims", swap) for part in (held[0], held_second[0])]
        row_sums, columns = tile_sums(
            info, units, codes, peer_codes, [held[1], others[0], held_second[1], others[1]],
            scale_root, part_scale,
        )
        row_parts.append(row_sums)
        columns = lax.ppermute(
            columns, line,
            [(place(g, o + step), place(g, o)) for g in range(groups) for o in range(owners)],
        )
        column_parts.append(columns)
        if step < rounds:
            first[0], first[1], second[0], second[1], columns = after(
                (first[0], first[1], second[0], second[1], columns)
            )
    here = (jnp.arange(pairs)[:, None] == pair) & (jnp.arange(2)[None, :] == core)
    column_total = jnp.where(here[:, None, :, None], sum(column_parts)[None, :, None, :], 0.0)
    density = sum(row_parts) + column_total.reshape(blocks, rows)
    density = lax.psum(density, ("pairs", "dims"))
    return jnp.log1p(density)


def solution(mesh):
    return jax.shard_map(
        per_device,
        mesh=mesh,
        in_specs=(
            P(("groups", "blocks"), None, "dims"),
            P(("groups", "blocks"), None),
            P(("groups", "blocks")),
            P(("groups", "blocks")),
            P(("groups", "blocks"), "pairs", None, None),
            P(("groups", "blocks"), "pairs", None),
        ),
        out_specs=P(("groups", "blocks"), None),
        check_vma=False,
    )
```

time: 79.1 us -> 68.4 us (0.86)
  starting transfers between devices: 28.3 us -> 22.7 us
  between operations: 2.82 us -> 0.22 us
  Pallas kernels: 9.33 us -> 6.9 us
  other arithmetic: 4.87 us -> 2.62 us
  local copies, waits for them, and re-layouts: 5.26 us -> 7.23 us
    ppermute x11 -> x17, starting transfers between devices: 25.7 us -> 21.2 us  [the longest x8 11.9 us: send(): return [lax.ppermute(array, line, to) for array in arrays]]
    unnamed x3 -> x19, local copies, waits for them, and re-layouts: 0.01 us -> 3.14 us
    pallas_call x4 -> x2, Pallas kernels: 9.33 us -> 6.9 us  [tile_sums(): pl.pallas_call(tile_kernel, out_shape=(jax.ShapeDtypeStruct((blocks, rows...]
    another operation x2 -> x0, local copies, waits for them, and re-layouts: 1.94 us -> none  [per_device(): jnp.stack([lax.dynamic_slice_in_dim(flat, second_start, quarter, 0), lax....]
    dynamic_slice x5 -> x2, local copies, waits for them, and re-layouts: 1.9 us -> 2.97 us  [quarter(): return lax.dynamic_slice_in_dim(flat, pair * share + number * unit, unit, 0)]
    ppermute x1, starting transfers between devices: 2.55 us -> 1.55 us  [per_device(): lax.ppermute(counted, 'pairs', [(i, (i + step) % pairs) for i in range(pa...]
    ppermute x11 -> x17, waiting for transfers between devices: 22.4 us -> 21.6 us  [the longest x8 12.6 us: send(): return [lax.ppermute(array, line, to) for array in arrays]]
    convert_element_type x2 -> x9, other arithmetic: 1.31 us -> 1.59 us  [the longest x2 1.4 us: per_device(): part_scale = note[:scale_end].astype(jnp.float32).reshape(-1, unit)]
  transfers between devices with their start and end apart: 12 -> 18, of which waited for: 4 -> 7; matrix products, arithmetic and copies ran while one was open for 12% -> 8% of each run, Pallas kernels for 9% -> 9%
where the time goes in v2:
time: 68.4 us; the launch traced here: 67.9 us
  starting transfers between devices  22.7 us (33%)
  waiting for transfers between devices  21.7 us (32%)
  local copies, waits for them, and re-layouts  7.23 us (11%)
  Pallas kernels  6.9 us (10%)
  blocking collectives  6.51 us (10%)
  other arithmetic  2.62 us (4%)
    ppermute x8, waiting for transfers between devices, send(): return [lax.ppermute(array, line, to) for array in arrays]  12.6 us
    ppermute x8, starting transfers between devices, send(): return [lax.ppermute(array, line, to) for array in arrays]  11.9 us
    ppermute x2, waiting for transfers between devices, per_device(): lax.ppermute(columns, line, [(place(g, o + step), place(g, o)) for g in r...  7.82 us
    pallas_call x2, Pallas kernels, tile_sums(): pl.pallas_call(tile_kernel, out_shape=(jax.ShapeDtypeStruct((blocks, rows...  6.9 us
    psum x1, blocking collectives, per_device(): density = lax.psum(density, ('pairs', 'dims'))  6.51 us
    ppermute x2, starting transfers between devices, per_device(): lax.ppermute(columns, line, [(place(g, o + step), place(g, o)) for g in r...  5.33 us
    unnamed x19, local copies, waits for them, and re-layouts  3.14 us
    dynamic_slice x2, local copies, waits for them, and re-layouts, quarter(): return lax.dynamic_slice_in_dim(flat, pair * share + number * unit, unit, 0)  2.97 us
  transfers between devices with their start and end apart: 18, of which 7 were waited for; matrix products, arithmetic and copies ran while one was open for 8% of the time, Pallas kernels for 9%

profile of v2, /device:TPU:0, one launch (start us, length us, event | category | flops | bytes accessed | tf_op | source)
XLA Modules:
  0.0 67.9 jit_solution(14327548256961094771)
XLA Ops:
  0.0 1.1 %constant_dynamic-slice_fusion.5 = bf16[256,512]{1,0:T(8,128)(2,1)S(1)} fusion(bf16[2048,512]{1,0:T(8,128)(2,1)} %bitcast.21, s32[]{:T(128)S(6)} %select_n.70), kind=kLoop, calls=%fused_computation.17 | loop fusion | bytes 524292 | tf_op jit(solution)/shard_map/dynamic_slice | solution.py:154
  1.1 0.5 collective-permute-start.7
  1.7 2.6 %collective-permute-start.1 = (bf16[256,512]{1,0:T(8,128)(2,1)S(1)}, bf16[256,512]{1,0:T(8,128)(2,1)}, u32[]{:S(2)}, u32[]{:S(2)}) collective-permute-start(bf16[256,512]{1,0:T(8,128)(2,1)S(1)} %constant_dynamic-slice_fusion.5), channel_id=1, source_target_pairs={{0,4},{4,8},{8,12},{12,0},{28,24},{24,20},{20,16},{16,28},{1,5},{5... | collective-permute-start | bytes 786440 | tf_op jit(solution)/shard_map/ppermute | solution.py:162
  4.3 0.7 %fusion.3 = s32[12]{0:T(128)S(1)} fusion(s32[1,1,12]{2,1,0:T(1,128)} %param.11, s32[1,1,12,1]{2,3,1,0:T(1,128)} %param.10, s32[]{:T(128)S(6)} %add.119), kind=kLoop, calls=%fused_computation.22 | loop fusion | flops 168 | bytes 148 | tf_op jit(solution)/shard_map/add | solution.py:168
  5.0 0.1 convert_reduce_fusion
  5.1 1.6 %collective-permute-start = (f32[32]{0:T(128)S(1)}, f32[32]{0:T(128)S(1)}, u32[]{:S(2)}, u32[]{:S(2)}) collective-permute-start(f32[32]{0:T(128)S(1)} %convert_reduce_fusion), channel_id=1, source_target_pairs={{0,2},{2,0},{1,3},{3,1},{4,6},{6,4},{5,7},{7,5},{8,10},{10,8},{9,1... | collective-permute-start | bytes 392 | tf_op jit(solution)/shard_map/ppermute | solution.py:173
  6.6 1.9 %constant_dynamic-slice_fusion.1 = (bf16[256,512]{1,0:T(8,128)(2,1)}, bf16[256,512]{1,0:T(8,128)(2,1)S(1)}, bf16[256,512]{1,0:T(8,128)(2,1)S(1)}) fusion(bf16[2048,512]{1,0:T(8,128)(2,1)} %bitcast.22, s32[]{:T(128)S(6)} %select_n.78, s32[]{:T(128)S(6)} %select_n.77, s32[]{:T(128)S(6)} %select_n.76), kind=kLoop, calls=%fused_computation.13 | loop fusion | bytes 1572876 | tf_op jit(solution)/shard_map/dynamic_slice | solution.py:154
  8.5 1.6 %collective-permute-start.3 = (bf16[256,512]{1,0:T(8,128)(2,1)S(1)}, bf16[256,512]{1,0:T(8,128)(2,1)S(1)}, u32[]{:S(2)}, u32[]{:S(2)}) collective-permute-start(bf16[256,512]{1,0:T(8,128)(2,1)S(1)} %get-tuple-element.47), channel_id=1, source_target_pairs={{0,4},{4,8},{8,12},{12,0},{28,24},{24,20},{20,16},{16,28},{1,5},{5... | collective-permute-start | bytes 786440 | tf_op jit(solution)/shard_map/ppermute | solution.py:162
  10.1 0.0 copy-done.3
  10.1 0.0 copy-done.4
  10.1 0.0 copy-done.5
  10.1 3.5 %collective-permute-done.1 = bf16[256,512]{1,0:T(8,128)(2,1)} collective-permute-done((bf16[256,512]{1,0:T(8,128)(2,1)S(1)}, bf16[256,512]{1,0:T(8,128)(2,1)}, u32[]{:S(2)}, u32[]{:S(2)}) %collective-permute-start.1) | collective-permute-done | bytes 262176 | tf_op jit(solution)/shard_map/ppermute | solution.py:162
  13.6 1.4 %collective-permute-start.2 = (bf16[256,512]{1,0:T(8,128)(2,1)}, bf16[256,512]{1,0:T(8,128)(2,1)}, u32[]{:S(2)}, u32[]{:S(2)}) collective-permute-start(bf16[256,512]{1,0:T(8,128)(2,1)} %collective-permute-done.1), channel_id=1, source_target_pairs={{4,20},{8,24},{24,8},{20,4},{5,21},{9,25},{25,9},{21,5},{6,22},{10... | collective-permute-start | bytes 786440 | tf_op jit(solution)/shard_map/ppermute | solution.py:197
  15.0 0.0 collective-permute-done
  15.0 0.1 concatenate.12
  15.1 2.0 %collective-permute-start.5 = (bf16[272,512]{1,0:T(8,128)(2,1)S(1)}, bf16[272,512]{1,0:T(8,128)(2,1)S(1)}, u32[]{:S(2)}, u32[]{:S(2)}) collective-permute-start(bf16[272,512]{1,0:T(8,128)(2,1)S(1)} %pad_maximum_fusion), channel_id=1, source_target_pairs={{0,4},{4,8},{8,12},{12,0},{28,24},{24,20},{20,16},{16,28},{1,5},{5... | collective-permute-start | bytes 835592 | tf_op jit(solution)/shard_map/ppermute | solution.py:162
  17.2 1.6 %collective-permute-start.6 = (bf16[256,512]{1,0:T(8,128)(2,1)}, bf16[256,512]{1,0:T(8,128)(2,1)S(1)}, u32[]{:S(2)}, u32[]{:S(2)}) collective-permute-start(bf16[256,512]{1,0:T(8,128)(2,1)} %get-tuple-element.31), channel_id=1, source_target_pairs={{0,4},{4,8},{8,12},{12,0},{28,24},{24,20},{20,16},{16,28},{1,5},{5... | collective-permute-start | bytes 786440 | tf_op jit(solution)/shard_map/ppermute | solution.py:162
  18.8 0.1 collective-permute-done.3.refs_0_
  18.9 0.0 collective-permute-done.2
  18.9 1.4 %collective-permute-start.4 = (bf16[256,512]{1,0:T(8,128)(2,1)S(1)}, bf16[256,512]{1,0:T(8,128)(2,1)}, u32[]{:S(2)}, u32[]{:S(2)}) collective-permute-start(bf16[256,512]{1,0:T(8,128)(2,1)S(1)} %collective-permute-done.3.refs_0_), channel_id=1, source_target_pairs={{4,20},{8,24},{24,8},{20,4},{5,21},{9,25},{25,9},{21,5},{6,22},{10... | collective-permute-start | bytes 786440 | tf_op jit(solution)/shard_map/ppermute | solution.py:199
  20.2 0.1 pad_add_fusion.units_ref
  20.3 0.1 convert_element_type.53
  20.4 0.1 collective-permute-start.8
  20.5 6.1 %collective-permute-done.5 = bf16[272,512]{1,0:T(8,128)(2,1)S(1)} collective-permute-done((bf16[272,512]{1,0:T(8,128)(2,1)S(1)}, bf16[272,512]{1,0:T(8,128)(2,1)S(1)}, u32[]{:S(2)}, u32[]{:S(2)}) %collective-permute-start.5) | collective-permute-done | bytes 278560 | tf_op jit(solution)/shard_map/ppermute | solution.py:162
  26.6 1.4 %collective-permute-start.10 = (bf16[256,512]{1,0:T(8,128)(2,1)}, bf16[256,512]{1,0:T(8,128)(2,1)}, u32[]{:S(2)}, u32[]{:S(2)}) collective-permute-start(bf16[256,512]{1,0:T(8,128)(2,1)} %collective-permute-done.2), channel_id=1, source_target_pairs={{20,8},{24,12},{8,20},{4,16},{21,9},{25,13},{9,21},{5,17},{22,10},... | collective-permute-start | bytes 786440 | tf_op jit(solution)/shard_map/ppermute | solution.py:162
  27.9 0.0 collective-permute-done.4
  27.9 0.0 copy-done.6
  27.9 2.9 %collective-permute-done.6.refs_2_ = bf16[256,512]{1,0:T(8,128)(2,1)S(1)} collective-permute-done((bf16[256,512]{1,0:T(8,128)(2,1)}, bf16[256,512]{1,0:T(8,128)(2,1)S(1)}, u32[]{:S(2)}, u32[]{:S(2)}) %collective-permute-start.6) | collective-permute-done | bytes 262176 | tf_op jit(solution)/shard_map/ppermute | solution.py:162
  30.9 0.0 collective-permute-start.9
  30.9 0.7 %slice_bitcast_fusion.1 = bf16[2,4,8,128]{3,2,1,0:T(8,128)(2,1)S(1)} fusion(bf16[272,512]{1,0:T(8,128)(2,1)} %copy-done.6), kind=kLoop, calls=%fused_computation.2 | loop fusion | bytes 32768
  31.6 1.4 %collective-permute-start.12 = (bf16[272,512]{1,0:T(8,128)(2,1)}, bf16[272,512]{1,0:T(8,128)(2,1)}, u32[]{:S(2)}, u32[]{:S(2)}) collective-permute-start(bf16[272,512]{1,0:T(8,128)(2,1)} %copy-done.6), channel_id=1, source_target_pairs={{4,8},{8,12},{24,20},{20,16},{5,9},{9,13},{25,21},{21,17},{6,10},{... | collective-permute-start | bytes 835592 | tf_op jit(solution)/shard_map/ppermute | solution.py:162
  33.0 0.7 %slice_convert_fusion.1 = f32[4,512]{1,0:T(4,128)S(1)} fusion(bf16[272,512]{1,0:T(8,128)(2,1)} %copy-done.6), kind=kLoop, calls=%fused_computation.8 | loop fusion | flops 2048 | bytes 12288 | tf_op jit(solution)/shard_map/convert_element_type | solution.py:209
  33.7 0.0 collective-permute-done.8.refs_1_
  33.7 0.7 %copy-done.1 = bf16[256,512]{1,0:T(8,128)(2,1)} copy-done((bf16[256,512]{1,0:T(8,128)(2,1)}, bf16[256,512]{1,0:T(8,128)(2,1)S(1)}, u32[]{:S(2)}) %copy-start.1) | copy-done | bytes 262168
  34.4 0.7 collective-permute-start.11
  35.1 0.0 collective-permute-done.9.refs_3_
  35.1 0.7 collective-permute-start.13
  35.8 0.1 dynamic-slice_convert_fusion.1
  35.9 0.1 concatenate.14.info_ref
  36.0 0.0 collective-permute-done.7.peer_ref
  36.0 0.9 %copy-done.2 = bf16[256,512]{1,0:T(8,128)(2,1)S(1)} copy-done((bf16[256,512]{1,0:T(8,128)(2,1)S(1)}, bf16[256,512]{1,0:T(8,128)(2,1)}, u32[]{:S(2)}) %copy-start.2) | copy-done | bytes 262168
  36.9 5.9 %shard_map.64 = (f32[8,256]{1,0:T(8,128)S(1)}, f32[2,256]{1,0:T(2,128)S(1)}) custom-call(s32[49]{0:T(128)S(1)} %concatenate.14.info_ref, s32[2]{0:T(128)S(1)} %pad_add_fusion.units_ref, bf16[8,256,512]{2,1,0:T(8,128)(2,1)S(1)} %copy-done, bf16[8,256,512]{2,1,0:T(8,128)(2,1)} %collective-permute-done.7.peer_ref, ...), custom_call_target="tpu_custom_call" | custom-call | tf_op jit(solution)/shard_map/pallas_call | solution.py:95
  42.9 0.1 collective-permute-start.14
  43.0 0.0 collective-permute-done.10
  43.0 0.0 collective-permute-done.11.refs_0_
  43.0 0.0 collective-permute-done.13.refs_2_
  43.0 0.0 collective-permute-done.12
  43.0 6.4 %collective-permute-done.14 = f32[2,256]{1,0:T(2,128)S(1)} collective-permute-done((f32[2,256]{1,0:T(2,128)S(1)}, f32[2,256]{1,0:T(2,128)S(1)}, u32[]{:S(2)}, u32[]{:S(2)}) %collective-permute-start.14) | collective-permute-done | bytes 2080 | tf_op jit(solution)/shard_map/ppermute | solution.py:226
  49.4 0.7 %slice_bitcast_fusion = bf16[2,4,8,128]{3,2,1,0:T(8,128)(2,1)S(1)} fusion(bf16[272,512]{1,0:T(8,128)(2,1)} %collective-permute-done.12), kind=kLoop, calls=%fused_computation.1 | loop fusion | bytes 32768
  50.2 0.0 collective-permute-start.16
  50.2 0.7 %slice_convert_fusion = f32[4,512]{1,0:T(4,128)S(1)} fusion(bf16[272,512]{1,0:T(8,128)(2,1)} %collective-permute-done.12), kind=kLoop, calls=%fused_computation.7 | loop fusion | flops 2048 | bytes 12288 | tf_op jit(solution)/shard_map/convert_element_type | solution.py:209
  50.9 0.6 collective-permute-start.15
  51.4 0.1 dynamic-slice_convert_fusion
  51.5 0.1 concatenate.15.info_ref
  51.6 1.2 %collective-permute-done.15.refs_1_ = bf16[256,512]{1,0:T(8,128)(2,1)S(1)} collective-permute-done((bf16[256,512]{1,0:T(8,128)(2,1)}, bf16[256,512]{1,0:T(8,128)(2,1)S(1)}, u32[]{:S(2)}, u32[]{:S(2)}) %collective-permute-start.15) | collective-permute-done | bytes 262176 | tf_op jit(solution)/shard_map/ppermute | solution.py:220
  52.8 0.0 collective-permute-done.16.refs_3_
  52.8 1.0 %shard_map.65 = (f32[8,256]{1,0:T(8,128)S(1)}, f32[2,256]{1,0:T(2,128)S(1)}) custom-call(s32[49]{0:T(128)S(1)} %concatenate.15.info_ref, s32[2]{0:T(128)S(1)} %pad_add_fusion.units_ref, bf16[8,256,512]{2,1,0:T(8,128)(2,1)S(1)} %copy-done, bf16[8,256,512]{2,1,0:T(8,128)(2,1)} %collective-permute-done.7.peer_ref, ...), custom_call_target="tpu_custom_call" | custom-call | tf_op jit(solution)/shard_map/pallas_call | solution.py:95
  53.8 5.3 %collective-permute-start.17 = (f32[2,256]{1,0:T(2,128)S(1)}, f32[2,256]{1,0:T(2,128)S(1)}, u32[]{:S(2)}, u32[]{:S(2)}) collective-permute-start(f32[2,256]{1,0:T(2,128)S(1)} %get-tuple-element.44), channel_id=1, source_target_pairs={{8,0},{12,4},{0,8},{4,12},{20,28},{16,24},{28,20},{24,16},{9,1},{1... | collective-permute-start | bytes 6152 | tf_op jit(solution)/shard_map/ppermute | solution.py:226
  59.1 0.1 broadcast_and_fusion
  59.2 0.1 broadcast_in_dim.49
  59.2 1.4 %collective-permute-done.17 = f32[2,256]{1,0:T(2,128)S(1)} collective-permute-done((f32[2,256]{1,0:T(2,128)S(1)}, f32[2,256]{1,0:T(2,128)S(1)}, u32[]{:S(2)}, u32[]{:S(2)}) %collective-permute-start.17) | collective-permute-done | bytes 2080 | tf_op jit(solution)/shard_map/ppermute | solution.py:226
  60.7 0.1 select_add_fusion
  60.7 6.5 %psum.7 = f32[8,256]{1,0:T(8,128)S(1)} all-reduce(f32[8,256]{1,0:T(8,128)S(1)} %select_add_fusion), channel_id=1, replica_groups=mesh['groups'=2,'blocks'=4,'pairs'=2,'dims'=2] {'pairs','dims'}, use_global_device_ids=true, to_apply=%region_1.2 | all-reduce | flops 2048 | bytes 16384 | tf_op jit(solution)/shard_map/psum | solution.py:238
  67.3 0.6 log1p.3
  (28 shorter events, 0.2 us)
Async XLA Ops:
  0.0 36.0 %copy-start = (bf16[8,256,512]{2,1,0:T(8,128)(2,1)S(1)}, bf16[8,256,512]{2,1,0:T(8,128)(2,1)}, u32[]{:S(2)}) copy-start(bf16[8,256,512]{2,1,0:T(8,128)(2,1)} %own_ref.3) | copy-start | bytes 6291460
  0.0 10.1 %copy-start.3 = (bf16[8,256]{1,0:T(8,128)(2,1)S(1)}, bf16[8,256]{1,0:T(8,128)(2,1)}, u32[]{:S(2)}) copy-start(bf16[8,256]{1,0:T(8,128)(2,1)} %param.7) | copy-start | bytes 12292
  0.0 10.1 %copy-start.4 = (s32[8]{0:T(128)S(1)}, s32[8]{0:T(128)}, u32[]{:S(2)}) copy-start(s32[8]{0:T(128)} %param.8) | copy-start | bytes 100
  0.0 10.1 %copy-start.5 = (s32[8]{0:T(128)S(1)}, s32[8]{0:T(128)}, u32[]{:S(2)}) copy-start(s32[8]{0:T(128)} %param.9) | copy-start | bytes 100
  1.1 34.8 %collective-permute-start.7 = (bf16[8,256,512]{2,1,0:T(8,128)(2,1)}, bf16[8,256,512]{2,1,0:T(8,128)(2,1)}, u32[]{:S(2)}, u32[]{:S(2)}) collective-permute-start(bf16[8,256,512]{2,1,0:T(8,128)(2,1)} %own_ref.3), channel_id=1, source_target_pairs={{0,1},{1,0},{2,3},{3,2},{4,5},{5,4},{6,7},{7,6},{8,9},{9,8},{10,11... | collective-permute-start | bytes 6291464 | tf_op jit(solution)/shard_map/ppermute | solution.py:165
  1.7 11.9 %collective-permute-start.1 = (bf16[256,512]{1,0:T(8,128)(2,1)S(1)}, bf16[256,512]{1,0:T(8,128)(2,1)}, u32[]{:S(2)}, u32[]{:S(2)}) collective-permute-start(bf16[256,512]{1,0:T(8,128)(2,1)S(1)} %constant_dynamic-slice_fusion.5), channel_id=1, source_target_pairs={{0,4},{4,8},{8,12},{12,0},{28,24},{24,20},{20,16},{16,28},{1,5},{5... | collective-permute-start | bytes 786440 | tf_op jit(solution)/shard_map/ppermute | solution.py:162
  5.1 9.9 %collective-permute-start = (f32[32]{0:T(128)S(1)}, f32[32]{0:T(128)S(1)}, u32[]{:S(2)}, u32[]{:S(2)}) collective-permute-start(f32[32]{0:T(128)S(1)} %convert_reduce_fusion), channel_id=1, source_target_pairs={{0,2},{2,0},{1,3},{3,1},{4,6},{6,4},{5,7},{7,5},{8,10},{10,8},{9,1... | collective-permute-start | bytes 392 | tf_op jit(solution)/shard_map/ppermute | solution.py:173
  8.5 10.4 %collective-permute-start.3 = (bf16[256,512]{1,0:T(8,128)(2,1)S(1)}, bf16[256,512]{1,0:T(8,128)(2,1)S(1)}, u32[]{:S(2)}, u32[]{:S(2)}) collective-permute-start(bf16[256,512]{1,0:T(8,128)(2,1)S(1)} %get-tuple-element.47), channel_id=1, source_target_pairs={{0,4},{4,8},{8,12},{12,0},{28,24},{24,20},{20,16},{16,28},{1,5},{5... | collective-permute-start | bytes 786440 | tf_op jit(solution)/shard_map/ppermute | solution.py:162
  13.6 5.3 %collective-permute-start.2 = (bf16[256,512]{1,0:T(8,128)(2,1)}, bf16[256,512]{1,0:T(8,128)(2,1)}, u32[]{:S(2)}, u32[]{:S(2)}) collective-permute-start(bf16[256,512]{1,0:T(8,128)(2,1)} %collective-permute-done.1), channel_id=1, source_target_pairs={{4,20},{8,24},{24,8},{20,4},{5,21},{9,25},{25,9},{21,5},{6,22},{10... | collective-permute-start | bytes 786440 | tf_op jit(solution)/shard_map/ppermute | solution.py:197
  15.1 11.4 %collective-permute-start.5 = (bf16[272,512]{1,0:T(8,128)(2,1)S(1)}, bf16[272,512]{1,0:T(8,128)(2,1)S(1)}, u32[]{:S(2)}, u32[]{:S(2)}) collective-permute-start(bf16[272,512]{1,0:T(8,128)(2,1)S(1)} %pad_maximum_fusion), channel_id=1, source_target_pairs={{0,4},{4,8},{8,12},{12,0},{28,24},{24,20},{20,16},{16,28},{1,5},{5... | collective-permute-start | bytes 835592 | tf_op jit(solution)/shard_map/ppermute | solution.py:162
  17.2 13.7 %collective-permute-start.6 = (bf16[256,512]{1,0:T(8,128)(2,1)}, bf16[256,512]{1,0:T(8,128)(2,1)S(1)}, u32[]{:S(2)}, u32[]{:S(2)}) collective-permute-start(bf16[256,512]{1,0:T(8,128)(2,1)} %get-tuple-element.31), channel_id=1, source_target_pairs={{0,4},{4,8},{8,12},{12,0},{28,24},{24,20},{20,16},{16,28},{1,5},{5... | collective-permute-start | bytes 786440 | tf_op jit(solution)/shard_map/ppermute | solution.py:162
  18.9 9.1 %collective-permute-start.4 = (bf16[256,512]{1,0:T(8,128)(2,1)S(1)}, bf16[256,512]{1,0:T(8,128)(2,1)}, u32[]{:S(2)}, u32[]{:S(2)}) collective-permute-start(bf16[256,512]{1,0:T(8,128)(2,1)S(1)} %collective-permute-done.3.refs_0_), channel_id=1, source_target_pairs={{4,20},{8,24},{24,8},{20,4},{5,21},{9,25},{25,9},{21,5},{6,22},{10... | collective-permute-start | bytes 786440 | tf_op jit(solution)/shard_map/ppermute | solution.py:199
  20.4 13.3 %collective-permute-start.8 = (bf16[256,512]{1,0:T(8,128)(2,1)}, bf16[256,512]{1,0:T(8,128)(2,1)S(1)}, u32[]{:S(2)}, u32[]{:S(2)}) collective-permute-start(bf16[256,512]{1,0:T(8,128)(2,1)} %collective-permute-done.1), channel_id=1, source_target_pairs={{0,1},{1,0},{2,3},{3,2},{4,5},{5,4},{6,7},{7,6},{8,9},{9,8},{10,11... | collective-permute-start | bytes 786440 | tf_op jit(solution)/shard_map/ppermute | solution.py:220
  26.6 1.4 %copy-start.6 = (bf16[272,512]{1,0:T(8,128)(2,1)}, bf16[272,512]{1,0:T(8,128)(2,1)S(1)}, u32[]{:S(2)}) copy-start(bf16[272,512]{1,0:T(8,128)(2,1)S(1)} %collective-permute-done.5) | copy-start | bytes 835588
  26.6 16.4 %collective-permute-start.10 = (bf16[256,512]{1,0:T(8,128)(2,1)}, bf16[256,512]{1,0:T(8,128)(2,1)}, u32[]{:S(2)}, u32[]{:S(2)}) collective-permute-start(bf16[256,512]{1,0:T(8,128)(2,1)} %collective-permute-done.2), channel_id=1, source_target_pairs={{20,8},{24,12},{8,20},{4,16},{21,9},{25,13},{9,21},{5,17},{22,10},... | collective-permute-start | bytes 786440 | tf_op jit(solution)/shard_map/ppermute | solution.py:162
  30.9 4.2 %collective-permute-start.9 = (bf16[272,512]{1,0:T(8,128)(2,1)}, bf16[272,512]{1,0:T(8,128)(2,1)S(1)}, u32[]{:S(2)}, u32[]{:S(2)}) collective-permute-start(bf16[272,512]{1,0:T(8,128)(2,1)} %copy-done.6), channel_id=1, source_target_pairs={{0,1},{1,0},{2,3},{3,2},{4,5},{5,4},{6,7},{7,6},{8,9},{9,8},{10,11... | collective-permute-start | bytes 835592 | tf_op jit(solution)/shard_map/ppermute | solution.py:220
  31.6 11.4 %collective-permute-start.12 = (bf16[272,512]{1,0:T(8,128)(2,1)}, bf16[272,512]{1,0:T(8,128)(2,1)}, u32[]{:S(2)}, u32[]{:S(2)}) collective-permute-start(bf16[272,512]{1,0:T(8,128)(2,1)} %copy-done.6), channel_id=1, source_target_pairs={{4,8},{8,12},{24,20},{20,16},{5,9},{9,13},{25,21},{21,17},{6,10},{... | collective-permute-start | bytes 835592 | tf_op jit(solution)/shard_map/ppermute | solution.py:162
  33.7 0.7 %copy-start.1 = (bf16[256,512]{1,0:T(8,128)(2,1)}, bf16[256,512]{1,0:T(8,128)(2,1)S(1)}, u32[]{:S(2)}) copy-start(bf16[256,512]{1,0:T(8,128)(2,1)S(1)} %collective-permute-done.8.refs_1_) | copy-start | bytes 786436
  34.4 8.6 %collective-permute-start.11 = (bf16[256,512]{1,0:T(8,128)(2,1)}, bf16[256,512]{1,0:T(8,128)(2,1)S(1)}, u32[]{:S(2)}, u32[]{:S(2)}) collective-permute-start(bf16[256,512]{1,0:T(8,128)(2,1)} %collective-permute-done.4), channel_id=1, source_target_pairs={{20,8},{24,12},{8,20},{4,16},{21,9},{25,13},{9,21},{5,17},{22,10},... | collective-permute-start | bytes 786440 | tf_op jit(solution)/shard_map/ppermute | solution.py:162
  35.1 7.9 %collective-permute-start.13 = (bf16[256,512]{1,0:T(8,128)(2,1)S(1)}, bf16[256,512]{1,0:T(8,128)(2,1)S(1)}, u32[]{:S(2)}, u32[]{:S(2)}) collective-permute-start(bf16[256,512]{1,0:T(8,128)(2,1)S(1)} %collective-permute-done.6.refs_2_), channel_id=1, source_target_pairs={{4,8},{8,12},{24,20},{20,16},{5,9},{9,13},{25,21},{21,17},{6,10},{... | collective-permute-start | bytes 786440 | tf_op jit(solution)/shard_map/ppermute | solution.py:162
  36.0 1.0 %copy-start.2 = (bf16[256,512]{1,0:T(8,128)(2,1)S(1)}, bf16[256,512]{1,0:T(8,128)(2,1)}, u32[]{:S(2)}) copy-start(bf16[256,512]{1,0:T(8,128)(2,1)} %copy-done.1) | copy-start | bytes 786436
  42.9 6.6 %collective-permute-start.14 = (f32[2,256]{1,0:T(2,128)S(1)}, f32[2,256]{1,0:T(2,128)S(1)}, u32[]{:S(2)}, u32[]{:S(2)}) collective-permute-start(f32[2,256]{1,0:T(2,128)S(1)} %get-tuple-element.38), channel_id=1, source_target_pairs={{4,0},{8,4},{12,8},{0,12},{24,28},{20,24},{16,20},{28,16},{5,1},{9... | collective-permute-start | bytes 6152 | tf_op jit(solution)/shard_map/ppermute | solution.py:226
  50.2 2.7 %collective-permute-start.16 = (bf16[272,512]{1,0:T(8,128)(2,1)}, bf16[272,512]{1,0:T(8,128)(2,1)S(1)}, u32[]{:S(2)}, u32[]{:S(2)}) collective-permute-start(bf16[272,512]{1,0:T(8,128)(2,1)} %collective-permute-done.12), channel_id=1, source_target_pairs={{0,1},{1,0},{2,3},{3,2},{4,5},{5,4},{6,7},{7,6},{8,9},{9,8},{10,11... | collective-permute-start | bytes 835592 | tf_op jit(solution)/shard_map/ppermute | solution.py:220
  50.9 1.9 %collective-permute-start.15 = (bf16[256,512]{1,0:T(8,128)(2,1)}, bf16[256,512]{1,0:T(8,128)(2,1)S(1)}, u32[]{:S(2)}, u32[]{:S(2)}) collective-permute-start(bf16[256,512]{1,0:T(8,128)(2,1)} %collective-permute-done.10), channel_id=1, source_target_pairs={{0,1},{1,0},{2,3},{3,2},{4,5},{5,4},{6,7},{7,6},{8,9},{9,8},{10,11... | collective-permute-start | bytes 786440 | tf_op jit(solution)/shard_map/ppermute | solution.py:220
  53.8 6.8 %collective-permute-start.17 = (f32[2,256]{1,0:T(2,128)S(1)}, f32[2,256]{1,0:T(2,128)S(1)}, u32[]{:S(2)}, u32[]{:S(2)}) collective-permute-start(f32[2,256]{1,0:T(2,128)S(1)} %get-tuple-element.44), channel_id=1, source_target_pairs={{8,0},{12,4},{0,8},{4,12},{20,28},{16,24},{28,20},{24,16},{9,1},{1... | collective-permute-start | bytes 6152 | tf_op jit(solution)/shard_map/ppermute | solution.py:226

commit v3 on v2

--- a/solution.py
+++ b/solution.py
@@ -153,16 +153,19 @@
     def quarter(number):
         return lax.dynamic_slice_in_dim(flat, pair * share + number * unit, unit, 0)
 
+    def follow(value, *others):
+        return lax.optimization_barrier((value, *others))[0]
+
+    def send(arrays, to):
+        return [lax.ppermute(array, line, to) for array in arrays]
+
     first = [quarter(1 - core)]
-    first[0], flat, route_offsets, codes_held = after((first[0], flat, route_offsets, codes))
+    flat = follow(flat, first[0])
     first.append(quarter(core))
     second = [quarter(3 - core), quarter(2 + core)]
-
-    def send(arrays, to):
-        return [lax.ppermute(array, line, to) for array in arrays]
-
+    peer_codes = lax.ppermute(follow(codes, first[0]), "dims", swap)
+    route_offsets = follow(route_offsets, peer_codes)
     first = send(first, moves(1, 0, 1))
-    peer_codes = lax.ppermute(codes_held, "dims", swap)
 
     targets = (owner + 1 + route_offsets.reshape(-1)) % owners
     named = targets * blocks + partner_local.reshape(-1)
@@ -180,13 +183,15 @@
     note = jnp.pad(note, (0, note_rows * width - note.shape[0])).reshape(note_rows, width)
     own_listed = listed.reshape(owners, blocks).astype(jnp.int32)
     second[0] = jnp.concatenate([second[0], note], axis=0)
-    second[0], second[1] = after((second[0], second[1]))
+    ready = second[0]
+    second[1] = follow(second[1], first[0])
     second = send(second, moves(1, 0, 1))
 
     scale_root = scales.astype(jnp.float32) * inverse_root
     units = jnp.stack([pair * 4 + core, pair * 4 + core + 2]).astype(jnp.int32)
 
     row_parts, column_parts = [], []
+    given = None
     for step in range(1, rounds + 1):
         held, held_second = list(first), list(second)
         if step < rounds:
@@ -194,15 +199,12 @@
             if detour:
                 aside = [(s, beside(s)) for s, _ in perm]
                 home = [(beside(s), t) for s, t in perm]
-                one = lax.ppermute(held[0], line, aside)
-                one, held[1] = after((one, held[1]))
+                one = lax.ppermute(follow(held[0], ready), line, aside)
                 two = lax.ppermute(held[1], line, aside)
-                two, held_second[0] = after((two, held_second[0]))
-                held_second[0], held_second[1] = after((held_second[0], held_second[1]))
                 first = send([one, two], home)
+                second = send([follow(held_second[0], one), held_second[1]], perm)
             else:
-                first = send(held, perm)
-            second = send(held_second, perm)
+                first, second = send(held, perm), send(held_second, perm)
         note = held_second[0][unit:].reshape(-1)
         scale_end = blocks * rows
         cluster_end, count_end = scale_end + blocks, scale_end + 2 * blocks
@@ -217,9 +219,13 @@
             lax.dynamic_slice_in_dim(note, count_end + owner * blocks, blocks, 0).astype(jnp.int32),
             active.astype(jnp.int32)[None],
         ])
-        others = [lax.ppermute(part, "dims", swap) for part in (held[0], held_second[0])]
+        others = given or [lax.ppermute(part, "dims", swap) for part in (held[0], held_second[0])]
+        if step < rounds:
+            given = [lax.ppermute(part, "dims", swap) for part in (first[0], second[0])]
+            info = follow(info, first[0], second[0])
         row_sums, columns = tile_sums(
-            info, units, codes, peer_codes, [held[1], others[0], held_second[1], others[1]],
+            info, units, codes, peer_codes,
+            [held[1], others[0], follow(held_second[1], others[0], others[1], info), others[1]],
             scale_root, part_scale,
         )
         row_parts.append(row_sums)
@@ -229,9 +235,7 @@
         )
         column_parts.append(columns)
         if step < rounds:
-            first[0], first[1], second[0], second[1], columns = after(
-                (first[0], first[1], second[0], second[1], columns)
-            )
+            first[1], second[1] = follow(first[1], columns), follow(second[1], columns)
     here = (jnp.arange(pairs)[:, None] == pair) & (jnp.arange(2)[None, :] == core)
     column_total = jnp.where(here[:, None, :, None], sum(column_parts)[None, :, None, :], 0.0)
     density = sum(row_parts) + column_total.reshape(blocks, rows)

time: 68.4 us -> 66 us (0.965)
  waiting for transfers between devices: 21.7 us -> 10.2 us
  starting transfers between devices: 22.7 us -> 33.8 us
  blocking collectives: 6.51 us -> 8.72 us
  Pallas kernels: 6.9 us -> 4.97 us
  local copies, waits for them, and re-layouts: 7.23 us -> 5.57 us
    ppermute x2, starting transfers between devices: 5.33 us -> 14.1 us  [per_device(): lax.ppermute(columns, line, [(place(g, o + step), place(g, o)) for g in r...]
    ppermute x8, waiting for transfers between devices: 12.6 us -> 6.04 us  [send(): return [lax.ppermute(array, line, to) for array in arrays]]
    ppermute x2, waiting for transfers between devices: 7.82 us -> 1.96 us  [per_device(): lax.ppermute(columns, line, [(place(g, o + step), place(g, o)) for g in r...]
    psum x1, blocking collectives: 6.51 us -> 8.72 us  [per_device(): density = lax.psum(density, ('pairs', 'dims'))]
    ppermute x8, starting transfers between devices: 11.9 us -> 14.1 us  [send(): return [lax.ppermute(array, line, to) for array in arrays]]
    ppermute x1, waiting for transfers between devices: 0.01 us -> 2.05 us  [per_device(): lax.ppermute(counted, 'pairs', [(i, (i + step) % pairs) for i in range(pa...]
    pallas_call x2, Pallas kernels: 6.9 us -> 4.97 us  [tile_sums(): pl.pallas_call(tile_kernel, out_shape=(jax.ShapeDtypeStruct((blocks, rows...]
    unnamed x19 -> x17, local copies, waits for them, and re-layouts: 3.14 us -> 1.48 us
  transfers between devices with their start and end apart: 18 -> 18, of which waited for: 7 -> 7; matrix products, arithmetic and copies ran while one was open for 8% -> 10% of each run, Pallas kernels for 9% -> 5%
where the time goes in v3:
time: 66 us
  starting transfers between devices  33.8 us (51%)
  waiting for transfers between devices  10.2 us (15%)
  blocking collectives  8.72 us (13%)
  local copies, waits for them, and re-layouts  5.57 us (8%)
  Pallas kernels  4.97 us (8%)
  other arithmetic  2.64 us (4%)
    ppermute x2, starting transfers between devices, per_device(): lax.ppermute(columns, line, [(place(g, o + step), place(g, o)) for g in r...  14.1 us
    ppermute x8, starting transfers between devices, send(): return [lax.ppermute(array, line, to) for array in arrays]  14.1 us
    psum x1, blocking collectives, per_device(): density = lax.psum(density, ('pairs', 'dims'))  8.72 us
    ppermute x8, waiting for transfers between devices, send(): return [lax.ppermute(array, line, to) for array in arrays]  6.04 us
    pallas_call x2, Pallas kernels, tile_sums(): pl.pallas_call(tile_kernel, out_shape=(jax.ShapeDtypeStruct((blocks, rows...  4.97 us
    dynamic_slice x2, local copies, waits for them, and re-layouts, quarter(): return lax.dynamic_slice_in_dim(flat, pair * share + number * unit, unit, 0)  2.97 us
    ppermute x1, waiting for transfers between devices, per_device(): lax.ppermute(counted, 'pairs', [(i, (i + step) % pairs) for i in range(pa...  2.05 us
    ppermute x2, waiting for transfers between devices, per_device(): lax.ppermute(columns, line, [(place(g, o + step), place(g, o)) for g in r...  1.96 us
  transfers between devices with their start and end apart: 18, of which 7 were waited for; matrix products, arithmetic and copies ran while one was open for 10% of the time, Pallas kernels for 5%

profile of v3, /device:TPU:0, one launch (start us, length us, event | category | flops | bytes accessed | tf_op | source)
XLA Modules:
  0.0 66.0 jit_solution(18296950589435563905)
XLA Ops:
  0.0 0.0 copy-start.4
  0.0 1.1 %constant_dynamic-slice_fusion.5 = bf16[256,512]{1,0:T(8,128)(2,1)S(1)} fusion(bf16[2048,512]{1,0:T(8,128)(2,1)} %bitcast.21, s32[]{:T(128)S(6)} %select_n.70), kind=kLoop, calls=%fused_computation.17 | loop fusion | bytes 524292 | tf_op jit(solution)/shard_map/dynamic_slice | solution.py:154
  1.2 0.5 collective-permute-start
  1.7 2.6 %collective-permute-start.3 = (bf16[256,512]{1,0:T(8,128)(2,1)S(1)}, bf16[256,512]{1,0:T(8,128)(2,1)}, u32[]{:S(2)}, u32[]{:S(2)}) collective-permute-start(bf16[256,512]{1,0:T(8,128)(2,1)S(1)} %constant_dynamic-slice_fusion.5), channel_id=1, source_target_pairs={{0,4},{4,8},{8,12},{12,0},{28,24},{24,20},{20,16},{16,28},{1,5},{5... | collective-permute-start | bytes 786440 | tf_op jit(solution)/shard_map/ppermute | solution.py:160
  4.3 1.9 %constant_dynamic-slice_fusion.1 = (bf16[256,512]{1,0:T(8,128)(2,1)S(1)}, bf16[256,512]{1,0:T(8,128)(2,1)}, bf16[256,512]{1,0:T(8,128)(2,1)S(1)}) fusion(bf16[2048,512]{1,0:T(8,128)(2,1)} %bitcast.22, s32[]{:T(128)S(6)} %select_n.81, s32[]{:T(128)S(6)} %select_n.80, s32[]{:T(128)S(6)} %select_n.76), kind=kLoop, calls=%fused_computation.13 | loop fusion | bytes 1572876 | tf_op jit(solution)/shard_map/dynamic_slice | solution.py:154
  6.2 1.6 %collective-permute-start.7 = (bf16[256,512]{1,0:T(8,128)(2,1)}, bf16[256,512]{1,0:T(8,128)(2,1)S(1)}, u32[]{:S(2)}, u32[]{:S(2)}) collective-permute-start(bf16[256,512]{1,0:T(8,128)(2,1)} %get-tuple-element.36), channel_id=1, source_target_pairs={{0,4},{4,8},{8,12},{12,0},{28,24},{24,20},{20,16},{16,28},{1,5},{5... | collective-permute-start | bytes 786440 | tf_op jit(solution)/shard_map/ppermute | solution.py:160
  7.8 0.0 copy-done.1
  7.8 0.0 copy-done.2
  7.8 0.0 copy-done.3
  7.8 0.0 collective-permute-done.peer_ref
  7.8 0.0 copy-done.5
  7.9 0.1 convert_reduce_fusion
  8.0 1.6 %collective-permute-start.1 = (f32[32]{0:T(128)S(1)}, f32[32]{0:T(128)S(1)}, u32[]{:S(2)}, u32[]{:S(2)}) collective-permute-start(f32[32]{0:T(128)S(1)} %convert_reduce_fusion), channel_id=1, source_target_pairs={{0,2},{2,0},{1,3},{3,1},{4,6},{6,4},{5,7},{7,5},{8,10},{10,8},{9,1... | collective-permute-start | bytes 392 | tf_op jit(solution)/shard_map/ppermute | solution.py:176
  9.5 2.0 %collective-permute-done.1 = f32[32]{0:T(128)S(1)} collective-permute-done((f32[32]{0:T(128)S(1)}, f32[32]{0:T(128)S(1)}, u32[]{:S(2)}, u32[]{:S(2)}) %collective-permute-start.1) | collective-permute-done | bytes 160 | tf_op jit(solution)/shard_map/ppermute | solution.py:176
  11.6 0.1 concatenate.12
  11.7 0.7 %pad_maximum_fusion = bf16[272,512]{1,0:T(8,128)(2,1)} fusion(bf16[16,512]{1,0:T(8,128)(2,1)S(1)} %reshape.98, bf16[256,512]{1,0:T(8,128)(2,1)S(1)} %get-tuple-element.37), kind=kLoop, calls=%fused_computation | loop fusion | flops 557056 | bytes 557056 | tf_op jit(solution)/shard_map/concatenate | solution.py:185
  12.4 1.6 %collective-permute-start.2 = (bf16[272,512]{1,0:T(8,128)(2,1)}, bf16[272,512]{1,0:T(8,128)(2,1)}, u32[]{:S(2)}, u32[]{:S(2)}) collective-permute-start(bf16[272,512]{1,0:T(8,128)(2,1)} %pad_maximum_fusion), channel_id=1, source_target_pairs={{0,4},{4,8},{8,12},{12,0},{28,24},{24,20},{20,16},{16,28},{1,5},{5... | collective-permute-start | bytes 835592 | tf_op jit(solution)/shard_map/ppermute | solution.py:160
  14.0 0.0 collective-permute-done.3
  14.0 1.4 %collective-permute-start.4 = (bf16[256,512]{1,0:T(8,128)(2,1)}, bf16[256,512]{1,0:T(8,128)(2,1)}, u32[]{:S(2)}, u32[]{:S(2)}) collective-permute-start(bf16[256,512]{1,0:T(8,128)(2,1)} %collective-permute-done.3), channel_id=1, source_target_pairs={{4,20},{8,24},{24,8},{20,4},{5,21},{9,25},{25,9},{21,5},{6,22},{10... | collective-permute-start | bytes 786440 | tf_op jit(solution)/shard_map/ppermute | solution.py:202
  15.4 0.1 pad_add_fusion.units_ref
  15.4 3.5 %collective-permute-start.9 = (bf16[256,512]{1,0:T(8,128)(2,1)S(1)}, bf16[256,512]{1,0:T(8,128)(2,1)S(1)}, u32[]{:S(2)}, u32[]{:S(2)}) collective-permute-start(bf16[256,512]{1,0:T(8,128)(2,1)S(1)} %get-tuple-element.26), channel_id=1, source_target_pairs={{0,4},{4,8},{8,12},{12,0},{28,24},{24,20},{20,16},{16,28},{1,5},{5... | collective-permute-start | bytes 786440 | tf_op jit(solution)/shard_map/ppermute | solution.py:160
  18.9 0.0 collective-permute-start.8
  19.0 0.2 collective-permute-done.7.refs_0_
  19.1 1.4 %collective-permute-start.11 = (bf16[256,512]{1,0:T(8,128)(2,1)S(1)}, bf16[256,512]{1,0:T(8,128)(2,1)}, u32[]{:S(2)}, u32[]{:S(2)}) collective-permute-start(bf16[256,512]{1,0:T(8,128)(2,1)S(1)} %collective-permute-done.7.refs_0_), channel_id=1, source_target_pairs={{4,20},{8,24},{24,8},{20,4},{5,21},{9,25},{25,9},{21,5},{6,22},{10... | collective-permute-start | bytes 786440 | tf_op jit(solution)/shard_map/ppermute | solution.py:203
  20.5 0.1 convert_element_type.53
  20.6 0.0 collective-permute-done.4
  20.6 1.4 %collective-permute-start.5 = (bf16[256,512]{1,0:T(8,128)(2,1)}, bf16[256,512]{1,0:T(8,128)(2,1)}, u32[]{:S(2)}, u32[]{:S(2)}) collective-permute-start(bf16[256,512]{1,0:T(8,128)(2,1)} %collective-permute-done.4), channel_id=1, source_target_pairs={{20,8},{24,12},{8,20},{4,16},{21,9},{25,13},{9,21},{5,17},{22,10},... | collective-permute-start | bytes 786440 | tf_op jit(solution)/shard_map/ppermute | solution.py:160
  22.0 3.2 %collective-permute-done.2 = bf16[272,512]{1,0:T(8,128)(2,1)} collective-permute-done((bf16[272,512]{1,0:T(8,128)(2,1)}, bf16[272,512]{1,0:T(8,128)(2,1)}, u32[]{:S(2)}, u32[]{:S(2)}) %collective-permute-start.2) | collective-permute-done | bytes 278560 | tf_op jit(solution)/shard_map/ppermute | solution.py:160
  25.2 0.7 %slice_bitcast_fusion.1 = bf16[2,4,8,128]{3,2,1,0:T(8,128)(2,1)S(1)} fusion(bf16[272,512]{1,0:T(8,128)(2,1)} %collective-permute-done.2), kind=kLoop, calls=%fused_computation.2 | loop fusion | bytes 32768
  25.9 1.4 %collective-permute-start.6 = (bf16[272,512]{1,0:T(8,128)(2,1)}, bf16[272,512]{1,0:T(8,128)(2,1)}, u32[]{:S(2)}, u32[]{:S(2)}) collective-permute-start(bf16[272,512]{1,0:T(8,128)(2,1)} %collective-permute-done.2), channel_id=1, source_target_pairs={{4,8},{8,12},{24,20},{20,16},{5,9},{9,13},{25,21},{21,17},{6,10},{... | collective-permute-start | bytes 835592 | tf_op jit(solution)/shard_map/ppermute | solution.py:160
  27.3 0.7 %slice_convert_fusion.1 = f32[4,512]{1,0:T(4,128)S(1)} fusion(bf16[272,512]{1,0:T(8,128)(2,1)} %collective-permute-done.2), kind=kLoop, calls=%fused_computation.8 | loop fusion | flops 2048 | bytes 12288 | tf_op jit(solution)/shard_map/convert_element_type | solution.py:211
  28.0 2.6 %collective-permute-done.9.refs_2_ = bf16[256,512]{1,0:T(8,128)(2,1)S(1)} collective-permute-done((bf16[256,512]{1,0:T(8,128)(2,1)S(1)}, bf16[256,512]{1,0:T(8,128)(2,1)S(1)}, u32[]{:S(2)}, u32[]{:S(2)}) %collective-permute-start.9) | collective-permute-done | bytes 262176 | tf_op jit(solution)/shard_map/ppermute | solution.py:160
  30.6 0.0 collective-permute-start.10
  30.6 0.1 dynamic-slice_convert_fusion.1
  30.7 0.1 concatenate.14.info_ref
  30.8 0.0 collective-permute-done.11
  30.8 0.7 %collective-permute-start.12 = (bf16[256,512]{1,0:T(8,128)(2,1)}, bf16[256,512]{1,0:T(8,128)(2,1)S(1)}, u32[]{:S(2)}, u32[]{:S(2)}) collective-permute-start(bf16[256,512]{1,0:T(8,128)(2,1)} %collective-permute-done.11), channel_id=1, source_target_pairs={{20,8},{24,12},{8,20},{4,16},{21,9},{25,13},{9,21},{5,17},{22,10},... | collective-permute-start | bytes 786440 | tf_op jit(solution)/shard_map/ppermute | solution.py:160
  31.5 0.0 collective-permute-done.5
  31.5 1.4 %collective-permute-start.15 = (bf16[256,512]{1,0:T(8,128)(2,1)S(1)}, bf16[256,512]{1,0:T(8,128)(2,1)}, u32[]{:S(2)}, u32[]{:S(2)}) collective-permute-start(bf16[256,512]{1,0:T(8,128)(2,1)S(1)} %collective-permute-done.9.refs_2_), channel_id=1, source_target_pairs={{4,8},{8,12},{24,20},{20,16},{5,9},{9,13},{25,21},{21,17},{6,10},{... | collective-permute-start | bytes 786440 | tf_op jit(solution)/shard_map/ppermute | solution.py:160
  32.8 0.0 collective-permute-done.6
  32.8 0.5 collective-permute-start.14
  33.3 0.0 collective-permute-done.8.refs_1_
  33.4 0.0 collective-permute-done.10.refs_3_
  33.4 0.0 copy-done
  33.4 3.5 %shard_map.64 = (f32[8,256]{1,0:T(8,128)S(1)}, f32[2,256]{1,0:T(2,128)S(1)}) custom-call(s32[49]{0:T(128)S(1)} %concatenate.14.info_ref, s32[2]{0:T(128)S(1)} %pad_add_fusion.units_ref, bf16[8,256,512]{2,1,0:T(8,128)(2,1)S(1)} %copy-done, bf16[8,256,512]{2,1,0:T(8,128)(2,1)} %collective-permute-done.peer_ref, ...), custom_call_target="tpu_custom_call" | custom-call | tf_op jit(solution)/shard_map/pallas_call | solution.py:95
  36.9 8.9 %collective-permute-start.13 = (f32[2,256]{1,0:T(2,128)S(1)}, f32[2,256]{1,0:T(2,128)S(1)}, u32[]{:S(2)}, u32[]{:S(2)}) collective-permute-start(f32[2,256]{1,0:T(2,128)S(1)} %get-tuple-element.29), channel_id=1, source_target_pairs={{4,0},{8,4},{12,8},{0,12},{24,28},{20,24},{16,20},{28,16},{5,1},{9... | collective-permute-start | bytes 6152 | tf_op jit(solution)/shard_map/ppermute | solution.py:232
  45.8 0.7 %slice_bitcast_fusion = bf16[2,4,8,128]{3,2,1,0:T(8,128)(2,1)S(1)} fusion(bf16[272,512]{1,0:T(8,128)(2,1)} %collective-permute-done.6), kind=kLoop, calls=%fused_computation.1 | loop fusion | bytes 32768
  46.5 0.3 collective-permute-start.16
  46.8 0.7 %slice_convert_fusion = f32[4,512]{1,0:T(4,128)S(1)} fusion(bf16[272,512]{1,0:T(8,128)(2,1)} %collective-permute-done.6), kind=kLoop, calls=%fused_computation.7 | loop fusion | flops 2048 | bytes 12288 | tf_op jit(solution)/shard_map/convert_element_type | solution.py:211
  47.5 0.1 dynamic-slice_convert_fusion
  47.6 0.1 concatenate.15.info_ref
  47.7 0.0 collective-permute-done.12.refs_0_
  47.7 0.6 collective-permute-done.13
  48.2 0.0 collective-permute-done.15.refs_2_
  48.2 0.0 collective-permute-done.14.refs_1_
  48.2 0.1 collective-permute-done.16.refs_3_
  48.4 1.5 %shard_map.65 = (f32[8,256]{1,0:T(8,128)S(1)}, f32[2,256]{1,0:T(2,128)S(1)}) custom-call(s32[49]{0:T(128)S(1)} %concatenate.15.info_ref, s32[2]{0:T(128)S(1)} %pad_add_fusion.units_ref, bf16[8,256,512]{2,1,0:T(8,128)(2,1)S(1)} %copy-done, bf16[8,256,512]{2,1,0:T(8,128)(2,1)} %collective-permute-done.peer_ref, ...), custom_call_target="tpu_custom_call" | custom-call | tf_op jit(solution)/shard_map/pallas_call | solution.py:95
  49.8 5.2 %collective-permute-start.17 = (f32[2,256]{1,0:T(2,128)S(1)}, f32[2,256]{1,0:T(2,128)S(1)}, u32[]{:S(2)}, u32[]{:S(2)}) collective-permute-start(f32[2,256]{1,0:T(2,128)S(1)} %get-tuple-element.34), channel_id=1, source_target_pairs={{8,0},{12,4},{0,8},{4,12},{20,28},{16,24},{28,20},{24,16},{9,1},{1... | collective-permute-start | bytes 6152 | tf_op jit(solution)/shard_map/ppermute | solution.py:232
  55.1 0.1 broadcast_and_fusion
  55.1 0.1 broadcast_in_dim.49
  55.2 1.4 %collective-permute-done.17 = f32[2,256]{1,0:T(2,128)S(1)} collective-permute-done((f32[2,256]{1,0:T(2,128)S(1)}, f32[2,256]{1,0:T(2,128)S(1)}, u32[]{:S(2)}, u32[]{:S(2)}) %collective-permute-start.17) | collective-permute-done | bytes 2080 | tf_op jit(solution)/shard_map/ppermute | solution.py:232
  56.6 0.1 select_add_fusion
  56.7 8.7 %psum.7 = f32[8,256]{1,0:T(8,128)S(1)} all-reduce(f32[8,256]{1,0:T(8,128)S(1)} %select_add_fusion), channel_id=1, replica_groups=mesh['groups'=2,'blocks'=4,'pairs'=2,'dims'=2] {'pairs','dims'}, use_global_device_ids=true, to_apply=%region_1.2 | all-reduce | flops 2048 | bytes 16384 | tf_op jit(solution)/shard_map/psum | solution.py:242
  65.4 0.6 log1p.3
  (26 shorter events, 0.2 us)
Async XLA Ops:
  0.0 33.4 %copy-start = (bf16[8,256,512]{2,1,0:T(8,128)(2,1)S(1)}, bf16[8,256,512]{2,1,0:T(8,128)(2,1)}, u32[]{:S(2)}) copy-start(bf16[8,256,512]{2,1,0:T(8,128)(2,1)} %own_ref.3) | copy-start | bytes 6291460
  0.0 7.8 %copy-start.1 = (bf16[8,256]{1,0:T(8,128)(2,1)S(1)}, bf16[8,256]{1,0:T(8,128)(2,1)}, u32[]{:S(2)}) copy-start(bf16[8,256]{1,0:T(8,128)(2,1)} %param.7) | copy-start | bytes 12292
  0.0 7.8 %copy-start.2 = (s32[8]{0:T(128)S(1)}, s32[8]{0:T(128)}, u32[]{:S(2)}) copy-start(s32[8]{0:T(128)} %param.8) | copy-start | bytes 100
  0.0 7.8 %copy-start.3 = (s32[8]{0:T(128)S(1)}, s32[8]{0:T(128)}, u32[]{:S(2)}) copy-start(s32[8]{0:T(128)} %param.9) | copy-start | bytes 100
  0.0 7.8 %copy-start.5 = (s32[1,1,12,1]{2,3,1,0:T(1,128)S(1)}, s32[1,1,12,1]{2,3,1,0:T(1,128)}, u32[]{:S(2)}) copy-start(s32[1,1,12,1]{2,3,1,0:T(1,128)} %param.10) | copy-start | bytes 148
  0.0 7.8 %copy-start.4 = (s32[1,1,12]{2,1,0:T(1,128)S(1)}, s32[1,1,12]{2,1,0:T(1,128)}, u32[]{:S(2)}) copy-start(s32[1,1,12]{2,1,0:T(1,128)} %param.11) | copy-start | bytes 148
  1.2 6.7 %collective-permute-start = (bf16[8,256,512]{2,1,0:T(8,128)(2,1)}, bf16[8,256,512]{2,1,0:T(8,128)(2,1)}, u32[]{:S(2)}, u32[]{:S(2)}) collective-permute-start(bf16[8,256,512]{2,1,0:T(8,128)(2,1)} %own_ref.3), channel_id=1, source_target_pairs={{0,1},{1,0},{2,3},{3,2},{4,5},{5,4},{6,7},{7,6},{8,9},{9,8},{10,11... | collective-permute-start | bytes 6291464 | tf_op jit(solution)/shard_map/ppermute | solution.py:166
  1.7 12.3 %collective-permute-start.3 = (bf16[256,512]{1,0:T(8,128)(2,1)S(1)}, bf16[256,512]{1,0:T(8,128)(2,1)}, u32[]{:S(2)}, u32[]{:S(2)}) collective-permute-start(bf16[256,512]{1,0:T(8,128)(2,1)S(1)} %constant_dynamic-slice_fusion.5), channel_id=1, source_target_pairs={{0,4},{4,8},{8,12},{12,0},{28,24},{24,20},{20,16},{16,28},{1,5},{5... | collective-permute-start | bytes 786440 | tf_op jit(solution)/shard_map/ppermute | solution.py:160
  6.2 12.9 %collective-permute-start.7 = (bf16[256,512]{1,0:T(8,128)(2,1)}, bf16[256,512]{1,0:T(8,128)(2,1)S(1)}, u32[]{:S(2)}, u32[]{:S(2)}) collective-permute-start(bf16[256,512]{1,0:T(8,128)(2,1)} %get-tuple-element.36), channel_id=1, source_target_pairs={{0,4},{4,8},{8,12},{12,0},{28,24},{24,20},{20,16},{16,28},{1,5},{5... | collective-permute-start | bytes 786440 | tf_op jit(solution)/shard_map/ppermute | solution.py:160
  8.0 3.6 %collective-permute-start.1 = (f32[32]{0:T(128)S(1)}, f32[32]{0:T(128)S(1)}, u32[]{:S(2)}, u32[]{:S(2)}) collective-permute-start(f32[32]{0:T(128)S(1)} %convert_reduce_fusion), channel_id=1, source_target_pairs={{0,2},{2,0},{1,3},{3,1},{4,6},{6,4},{5,7},{7,5},{8,10},{10,8},{9,1... | collective-permute-start | bytes 392 | tf_op jit(solution)/shard_map/ppermute | solution.py:176
  12.4 12.8 %collective-permute-start.2 = (bf16[272,512]{1,0:T(8,128)(2,1)}, bf16[272,512]{1,0:T(8,128)(2,1)}, u32[]{:S(2)}, u32[]{:S(2)}) collective-permute-start(bf16[272,512]{1,0:T(8,128)(2,1)} %pad_maximum_fusion), channel_id=1, source_target_pairs={{0,4},{4,8},{8,12},{12,0},{28,24},{24,20},{20,16},{16,28},{1,5},{5... | collective-permute-start | bytes 835592 | tf_op jit(solution)/shard_map/ppermute | solution.py:160
  14.0 6.6 %collective-permute-start.4 = (bf16[256,512]{1,0:T(8,128)(2,1)}, bf16[256,512]{1,0:T(8,128)(2,1)}, u32[]{:S(2)}, u32[]{:S(2)}) collective-permute-start(bf16[256,512]{1,0:T(8,128)(2,1)} %collective-permute-done.3), channel_id=1, source_target_pairs={{4,20},{8,24},{24,8},{20,4},{5,21},{9,25},{25,9},{21,5},{6,22},{10... | collective-permute-start | bytes 786440 | tf_op jit(solution)/shard_map/ppermute | solution.py:202
  15.4 15.2 %collective-permute-start.9 = (bf16[256,512]{1,0:T(8,128)(2,1)S(1)}, bf16[256,512]{1,0:T(8,128)(2,1)S(1)}, u32[]{:S(2)}, u32[]{:S(2)}) collective-permute-start(bf16[256,512]{1,0:T(8,128)(2,1)S(1)} %get-tuple-element.26), channel_id=1, source_target_pairs={{0,4},{4,8},{8,12},{12,0},{28,24},{24,20},{20,16},{16,28},{1,5},{5... | collective-permute-start | bytes 786440 | tf_op jit(solution)/shard_map/ppermute | solution.py:160
  18.9 14.4 %collective-permute-start.8 = (bf16[256,512]{1,0:T(8,128)(2,1)}, bf16[256,512]{1,0:T(8,128)(2,1)S(1)}, u32[]{:S(2)}, u32[]{:S(2)}) collective-permute-start(bf16[256,512]{1,0:T(8,128)(2,1)} %collective-permute-done.3), channel_id=1, source_target_pairs={{0,1},{1,0},{2,3},{3,2},{4,5},{5,4},{6,7},{7,6},{8,9},{9,8},{10,11... | collective-permute-start | bytes 786440 | tf_op jit(solution)/shard_map/ppermute | solution.py:222
  19.1 11.7 %collective-permute-start.11 = (bf16[256,512]{1,0:T(8,128)(2,1)S(1)}, bf16[256,512]{1,0:T(8,128)(2,1)}, u32[]{:S(2)}, u32[]{:S(2)}) collective-permute-start(bf16[256,512]{1,0:T(8,128)(2,1)S(1)} %collective-permute-done.7.refs_0_), channel_id=1, source_target_pairs={{4,20},{8,24},{24,8},{20,4},{5,21},{9,25},{25,9},{21,5},{6,22},{10... | collective-permute-start | bytes 786440 | tf_op jit(solution)/shard_map/ppermute | solution.py:203
  20.6 10.9 %collective-permute-start.5 = (bf16[256,512]{1,0:T(8,128)(2,1)}, bf16[256,512]{1,0:T(8,128)(2,1)}, u32[]{:S(2)}, u32[]{:S(2)}) collective-permute-start(bf16[256,512]{1,0:T(8,128)(2,1)} %collective-permute-done.4), channel_id=1, source_target_pairs={{20,8},{24,12},{8,20},{4,16},{21,9},{25,13},{9,21},{5,17},{22,10},... | collective-permute-start | bytes 786440 | tf_op jit(solution)/shard_map/ppermute | solution.py:160
  25.9 6.9 %collective-permute-start.6 = (bf16[272,512]{1,0:T(8,128)(2,1)}, bf16[272,512]{1,0:T(8,128)(2,1)}, u32[]{:S(2)}, u32[]{:S(2)}) collective-permute-start(bf16[272,512]{1,0:T(8,128)(2,1)} %collective-permute-done.2), channel_id=1, source_target_pairs={{4,8},{8,12},{24,20},{20,16},{5,9},{9,13},{25,21},{21,17},{6,10},{... | collective-permute-start | bytes 835592 | tf_op jit(solution)/shard_map/ppermute | solution.py:160
  30.6 2.7 %collective-permute-start.10 = (bf16[272,512]{1,0:T(8,128)(2,1)}, bf16[272,512]{1,0:T(8,128)(2,1)S(1)}, u32[]{:S(2)}, u32[]{:S(2)}) collective-permute-start(bf16[272,512]{1,0:T(8,128)(2,1)} %collective-permute-done.2), channel_id=1, source_target_pairs={{0,1},{1,0},{2,3},{3,2},{4,5},{5,4},{6,7},{7,6},{8,9},{9,8},{10,11... | collective-permute-start | bytes 835592 | tf_op jit(solution)/shard_map/ppermute | solution.py:222
  30.8 16.9 %collective-permute-start.12 = (bf16[256,512]{1,0:T(8,128)(2,1)}, bf16[256,512]{1,0:T(8,128)(2,1)S(1)}, u32[]{:S(2)}, u32[]{:S(2)}) collective-permute-start(bf16[256,512]{1,0:T(8,128)(2,1)} %collective-permute-done.11), channel_id=1, source_target_pairs={{20,8},{24,12},{8,20},{4,16},{21,9},{25,13},{9,21},{5,17},{22,10},... | collective-permute-start | bytes 786440 | tf_op jit(solution)/shard_map/ppermute | solution.py:160
  31.5 16.8 %collective-permute-start.15 = (bf16[256,512]{1,0:T(8,128)(2,1)S(1)}, bf16[256,512]{1,0:T(8,128)(2,1)}, u32[]{:S(2)}, u32[]{:S(2)}) collective-permute-start(bf16[256,512]{1,0:T(8,128)(2,1)S(1)} %collective-permute-done.9.refs_2_), channel_id=1, source_target_pairs={{4,8},{8,12},{24,20},{20,16},{5,9},{9,13},{25,21},{21,17},{6,10},{... | collective-permute-start | bytes 786440 | tf_op jit(solution)/shard_map/ppermute | solution.py:160
  32.8 15.4 %collective-permute-start.14 = (bf16[256,512]{1,0:T(8,128)(2,1)}, bf16[256,512]{1,0:T(8,128)(2,1)}, u32[]{:S(2)}, u32[]{:S(2)}) collective-permute-start(bf16[256,512]{1,0:T(8,128)(2,1)} %collective-permute-done.5), channel_id=1, source_target_pairs={{0,1},{1,0},{2,3},{3,2},{4,5},{5,4},{6,7},{7,6},{8,9},{9,8},{10,11... | collective-permute-start | bytes 786440 | tf_op jit(solution)/shard_map/ppermute | solution.py:224
  36.9 11.4 %collective-permute-start.13 = (f32[2,256]{1,0:T(2,128)S(1)}, f32[2,256]{1,0:T(2,128)S(1)}, u32[]{:S(2)}, u32[]{:S(2)}) collective-permute-start(f32[2,256]{1,0:T(2,128)S(1)} %get-tuple-element.29), channel_id=1, source_target_pairs={{4,0},{8,4},{12,8},{0,12},{24,28},{20,24},{16,20},{28,16},{5,1},{9... | collective-permute-start | bytes 6152 | tf_op jit(solution)/shard_map/ppermute | solution.py:232
  46.5 1.8 %collective-permute-start.16 = (bf16[272,512]{1,0:T(8,128)(2,1)}, bf16[272,512]{1,0:T(8,128)(2,1)S(1)}, u32[]{:S(2)}, u32[]{:S(2)}) collective-permute-start(bf16[272,512]{1,0:T(8,128)(2,1)} %collective-permute-done.6), channel_id=1, source_target_pairs={{0,1},{1,0},{2,3},{3,2},{4,5},{5,4},{6,7},{7,6},{8,9},{9,8},{10,11... | collective-permute-start | bytes 835592 | tf_op jit(solution)/shard_map/ppermute | solution.py:224
  49.8 6.8 %collective-permute-start.17 = (f32[2,256]{1,0:T(2,128)S(1)}, f32[2,256]{1,0:T(2,128)S(1)}, u32[]{:S(2)}, u32[]{:S(2)}) collective-permute-start(f32[2,256]{1,0:T(2,128)S(1)} %get-tuple-element.34), channel_id=1, source_target_pairs={{8,0},{12,4},{0,8},{4,12},{20,28},{16,24},{28,20},{24,16},{9,1},{1... | collective-permute-start | bytes 6152 | tf_op jit(solution)/shard_map/ppermute | solution.py:232

commit v4 on v3

--- a/solution.py
+++ b/solution.py
@@ -9,12 +9,14 @@
 
 NT = (((1,), (1,)), ((), ()))
 LANES = 128
+LOG2E = math.log2(math.e)
 
 
 def tile_kernel(info_ref, units_ref, own_ref, peer_ref, *refs):
-    count = len(refs) - 7
+    count = len(refs) - 8
     parts = refs[:count]
-    scale_ref, part_scale_ref, rows_ref, columns_ref, held_ref, total_ref, copied = refs[count:]
+    (scale_ref, part_scale_ref, rows_ref, columns_ref,
+     held_ref, total_ref, wide_ref, copied) = refs[count:]
     blocks, rows, _ = own_ref.shape
     segments, unit = columns_ref.shape
 
@@ -49,6 +51,11 @@
             for copy in copies(block):
                 copy.start()
 
+    for segment in range(segments):
+        part_scale = jnp.broadcast_to(part_scale_ref[pl.ds(units_ref[segment], 1), :], (LANES, unit))
+        wide_ref[0, segment] = jnp.transpose(part_scale)
+        row_ids = lax.broadcasted_iota(jnp.int32, (unit, LANES), 0)
+        wide_ref[1, segment] = (row_ids < valid[segment]).astype(jnp.float32)
     rows_ref[...] = jnp.zeros_like(rows_ref)
     total_ref[...] = jnp.zeros_like(total_ref)
     for block in range(blocks):
@@ -66,19 +73,24 @@
                     ) + lax.dot_general(
                         part(1, segment), held_ref[block, 1], NT, preferred_element_type=jnp.float32
                     )
-                    part_scale = jnp.transpose(jnp.broadcast_to(
-                        part_scale_ref[pl.ds(units_ref[segment], 1), :], (8, unit)
-                    ))[:, 0:1]
-                    kern = jnp.exp(gram * (part_scale * scale_ref[block : block + 1, :]))
-                    row_valid = lax.broadcasted_iota(jnp.int32, (1, rows), 1) < info_ref[blocks + block]
-                    part_valid = lax.broadcasted_iota(jnp.int32, (unit, 1), 0) < valid[segment]
-                    kern = jnp.where(row_valid & part_valid, kern, 0.0)
                     factor = weights[segment][block].astype(jnp.float32)
-                    rows_ref[block : block + 1, :] += factor * jnp.sum(kern, axis=0, keepdims=True)
-                    folded = kern[:, 0:LANES]
-                    for start in range(LANES, rows, LANES):
-                        folded = folded + kern[:, start : start + LANES]
-                    total_ref[segment] += factor * folded
+                    row_ids = lax.broadcasted_iota(jnp.int32, (1, LANES), 1)
+                    for start in range(0, rows, LANES):
+                        own_scale = scale_ref[block : block + 1, start : start + LANES] * LOG2E
+                        own_valid = jnp.where(
+                            row_ids + start < info_ref[blocks + block], factor, 0.0
+                        )
+                        summed = jnp.zeros((8, LANES), jnp.float32)
+                        for at in range(0, unit, 64):
+                            scaled = gram[at : at + 64, start : start + LANES] * (
+                                wide_ref[0, segment, at : at + 64, :] * own_scale
+                            )
+                            kern = jnp.exp2(scaled) * wide_ref[1, segment, at : at + 64, :]
+                            summed = summed + jnp.sum(kern.reshape(-1, 8, LANES), axis=0)
+                            total_ref[segment, at : at + 64, :] += kern * own_valid
+                        rows_ref[block : block + 1, start : start + LANES] += own_valid * jnp.sum(
+                            summed, axis=0, keepdims=True
+                        )
 
     for segment in range(segments):
         columns_ref[segment : segment + 1, :] = jnp.sum(
@@ -103,6 +115,7 @@
         scratch_shapes=[
             pltpu.VMEM((blocks, 2, rows, width), own.dtype),
             pltpu.VMEM((segments, unit, LANES), jnp.float32),
+            pltpu.VMEM((2, segments, unit, LANES), jnp.float32),
             pltpu.SemaphoreType.DMA((blocks, 2)),
         ],
         compiler_params=pltpu.CompilerParams(vmem_limit_bytes=32 * 1024 * 1024),
@@ -163,10 +176,11 @@
     flat = follow(flat, first[0])
     first.append(quarter(core))
     second = [quarter(3 - core), quarter(2 + core)]
-    peer_codes = lax.ppermute(follow(codes, first[0]), "dims", swap)
+    peer_codes = lax.ppermute(codes, "dims", swap)
+    sliced = first[0]
+    first = send(first, moves(1, 0, 1))
+
     route_offsets = follow(route_offsets, peer_codes)
-    first = send(first, moves(1, 0, 1))
-
     targets = (owner + 1 + route_offsets.reshape(-1)) % owners
     named = targets * blocks + partner_local.reshape(-1)
     block_ids = jnp.arange(owners * blocks, dtype=jnp.int32)
@@ -190,8 +204,11 @@
     scale_root = scales.astype(jnp.float32) * inverse_root
     units = jnp.stack([pair * 4 + core, pair * 4 + core + 2]).astype(jnp.int32)
 
+    def exchanged(part):
+        return lax.ppermute(part, "dims", swap)
+
     row_parts, column_parts = [], []
-    given = None
+    others = [None, None]
     for step in range(1, rounds + 1):
         held, held_second = list(first), list(second)
         if step < rounds:
@@ -202,9 +219,10 @@
                 one = lax.ppermute(follow(held[0], ready), line, aside)
                 two = lax.ppermute(held[1], line, aside)
                 first = send([one, two], home)
-                second = send([follow(held_second[0], one), held_second[1]], perm)
             else:
-                first, second = send(held, perm), send(held_second, perm)
+                one, two = held
+                first = send(held, perm)
+            second[0] = lax.ppermute(follow(held_second[0], one), line, perm)
         note = held_second[0][unit:].reshape(-1)
         scale_end = blocks * rows
         cluster_end, count_end = scale_end + blocks, scale_end + 2 * blocks
@@ -219,28 +237,59 @@
             lax.dynamic_slice_in_dim(note, count_end + owner * blocks, blocks, 0).astype(jnp.int32),
             active.astype(jnp.int32)[None],
         ])
-        others = given or [lax.ppermute(part, "dims", swap) for part in (held[0], held_second[0])]
+        if others[0] is None:
+            others[0] = exchanged(held[0])
+        if others[1] is None:
+            others[1] = exchanged(held_second[0])
+        chunks = [held[1], others[0], follow(held_second[1], others[0], others[1], info), others[1]]
+        others = [None, None]
         if step < rounds:
-            given = [lax.ppermute(part, "dims", swap) for part in (first[0], second[0])]
-            info = follow(info, first[0], second[0])
+            others[1] = exchanged(second[0])
+            info = follow(info, one)
+            second[1] = lax.ppermute(held_second[1], line, perm)
         row_sums, columns = tile_sums(
-            info, units, codes, peer_codes,
-            [held[1], others[0], follow(held_second[1], others[0], others[1], info), others[1]],
-            scale_root, part_scale,
+            info, units, codes, peer_codes, chunks, scale_root, part_scale
         )
         row_parts.append(row_sums)
-        columns = lax.ppermute(
-            columns, line,
-            [(place(g, o + step), place(g, o)) for g in range(groups) for o in range(owners)],
-        )
-        column_parts.append(columns)
         if step < rounds:
+            columns = follow(columns, row_sums)
+        if step < rounds or pairs != 2:
+            columns = lax.ppermute(
+                columns, line,
+                [(place(g, o + step), place(g, o)) for g in range(groups) for o in range(owners)],
+            )
+            column_parts.append(columns)
+        if step < rounds:
+            first[0] = follow(first[0], row_sums)
             first[1], second[1] = follow(first[1], columns), follow(second[1], columns)
-    here = (jnp.arange(pairs)[:, None] == pair) & (jnp.arange(2)[None, :] == core)
-    column_total = jnp.where(here[:, None, :, None], sum(column_parts)[None, :, None, :], 0.0)
-    density = sum(row_parts) + column_total.reshape(blocks, rows)
-    density = lax.psum(density, ("pairs", "dims"))
-    return jnp.log1p(density)
+    cores = jnp.arange(2)[None, :] == core
+    here = (jnp.arange(pairs)[:, None] == pair) & cores
+    density = sum(row_parts)
+    if column_parts:
+        density = density + jnp.where(
+            here[:, None, :, None], sum(column_parts)[None, :, None, :], 0.0
+        ).reshape(blocks, rows)
+    if pairs != 2:
+        return jnp.log1p(lax.psum(density, ("pairs", "dims")))
+    outgoing = jnp.where(cores[:, :, None], columns[:, None, :], 0.0).reshape(-1, rows)
+    both = jnp.concatenate([density, outgoing], axis=0)
+    both = both + lax.ppermute(both, "dims", swap)
+    density, outgoing = both[:blocks], both[blocks:]
+    across = [(0, 1), (1, 0)]
+    joint = ("groups", "blocks", "pairs")
+    back = [
+        (place(g, o + rounds) * 2 + p, place(g, o) * 2, p)
+        for g in range(groups) for o in range(owners) for p in range(2)
+    ]
+    parts = [
+        lax.ppermute(density, "pairs", across),
+        lax.ppermute(outgoing, joint, [(s, t + p) for s, t, p in back]),
+        lax.ppermute(outgoing, joint, [(s, t + 1 - p) for s, t, p in back]),
+    ]
+    straight, crossed = parts[1].reshape(1, -1, rows), parts[2].reshape(1, -1, rows)
+    own_pair = (jnp.arange(2) == pair)[:, None, None]
+    columns = jnp.where(own_pair, straight, crossed).reshape(blocks, rows)
+    return jnp.log1p(density + parts[0] + columns)
 
 
 def solution(mesh):

time: 66 us -> 61.7 us (0.935)
  blocking collectives: 8.72 us -> 0 us
  waiting for transfers between devices: 10.2 us -> 17.1 us
  starting transfers between devices: 33.8 us -> 30.1 us
  local copies, waits for them, and re-layouts: 5.57 us -> 6.77 us
  Pallas kernels: 4.97 us -> 4.03 us
  other arithmetic: 2.64 us -> 3.43 us
    ppermute x2 -> x1, starting transfers between devices: 14.1 us -> 2.87 us  [per_device(): lax.ppermute(columns, line, [(place(g, o + step), place(g, o)) for g in r...]
    ppermute x5 -> x11, starting transfers between devices: 1.3 us -> 11.5 us  [the longest x1 7.01 us: per_device(): lax.ppermute(outgoing, joint, [(s, t + p) for s, t, p in back])]
    psum x1 -> x0, blocking collectives: 8.72 us -> none  [per_device(): density = lax.psum(density, ('pairs', 'dims'))]
    ppermute x5 -> x11, waiting for transfers between devices: 0.12 us -> 6.42 us  [the longest x1 3.81 us: per_device(): lax.ppermute(outgoing, joint, [(s, t + 1 - p) for s, t, p in back])]
    ppermute x8 -> x6, starting transfers between devices: 14.1 us -> 11.4 us  [send(): return [lax.ppermute(array, line, to) for array in arrays]]
    unnamed x17 -> x21, local copies, waits for them, and re-layouts: 1.48 us -> 3.12 us
    pallas_call x2, Pallas kernels: 4.97 us -> 4.03 us  [tile_sums(): pl.pallas_call(tile_kernel, out_shape=(jax.ShapeDtypeStruct((blocks, rows...]
    log1p x0 -> x1, other arithmetic: none -> 0.68 us  [per_device(): return jnp.log1p(density + parts[0] + columns)]
  transfers between devices with their start and end apart: 18 -> 21, of which waited for: 7 -> 7; matrix products, arithmetic and copies ran while one was open for 10% -> 12% of each run, Pallas kernels for 5% -> 5%
where the time goes in v4:
time: 61.7 us; the launch traced here: 61.6 us
  starting transfers between devices  30.1 us (49%)
  waiting for transfers between devices  17.1 us (28%)
  local copies, waits for them, and re-layouts  6.77 us (11%)
  Pallas kernels  4.03 us (7%)
  other arithmetic  3.43 us (6%)
    ppermute x6, starting transfers between devices, send(): return [lax.ppermute(array, line, to) for array in arrays]  11.4 us
    ppermute x1, starting transfers between devices, per_device(): lax.ppermute(outgoing, joint, [(s, t + p) for s, t, p in back])  7.01 us
    ppermute x6, waiting for transfers between devices, send(): return [lax.ppermute(array, line, to) for array in arrays]  6.39 us
    pallas_call x2, Pallas kernels, tile_sums(): pl.pallas_call(tile_kernel, out_shape=(jax.ShapeDtypeStruct((blocks, rows...  4.03 us
    ppermute x1, waiting for transfers between devices, per_device(): lax.ppermute(outgoing, joint, [(s, t + 1 - p) for s, t, p in back])  3.81 us
    unnamed x21, local copies, waits for them, and re-layouts  3.12 us
    ppermute x1, starting transfers between devices, per_device(): lax.ppermute(columns, line, [(place(g, o + step), place(g, o)) for g in r...  2.87 us
    dynamic_slice x2, local copies, waits for them, and re-layouts, quarter(): return lax.dynamic_slice_in_dim(flat, pair * share + number * unit, unit, 0)  2.84 us
  transfers between devices with their start and end apart: 21, of which 7 were waited for; matrix products, arithmetic and copies ran while one was open for 12% of the time, Pallas kernels for 5%

profile of v4, /device:TPU:0, one launch (start us, length us, event | category | flops | bytes accessed | tf_op | source)
XLA Modules:
  0.0 61.6 jit_solution(1242272788055496760)
XLA Ops:
  0.0 0.5 collective-permute-start
  0.6 1.0 %constant_dynamic-slice_fusion.4 = bf16[256,512]{1,0:T(8,128)(2,1)S(1)} fusion(bf16[2048,512]{1,0:T(8,128)(2,1)} %bitcast.21, s32[]{:T(128)S(6)} %select_n.85), kind=kLoop, calls=%fused_computation.19 | loop fusion | bytes 524292 | tf_op jit(solution)/shard_map/dynamic_slice | solution.py:167
  1.5 2.8 %collective-permute-start.3 = (bf16[256,512]{1,0:T(8,128)(2,1)S(1)}, bf16[256,512]{1,0:T(8,128)(2,1)}, u32[]{:S(2)}, u32[]{:S(2)}) collective-permute-start(bf16[256,512]{1,0:T(8,128)(2,1)S(1)} %constant_dynamic-slice_fusion.4), channel_id=1, source_target_pairs={{0,4},{4,8},{8,12},{12,0},{28,24},{24,20},{20,16},{16,28},{1,5},{5... | collective-permute-start | bytes 786440 | tf_op jit(solution)/shard_map/ppermute | solution.py:173
  4.3 1.9 %constant_dynamic-slice_fusion.1 = (bf16[256,512]{1,0:T(8,128)(2,1)S(1)}, bf16[256,512]{1,0:T(8,128)(2,1)}, bf16[256,512]{1,0:T(8,128)(2,1)S(1)}) fusion(bf16[2048,512]{1,0:T(8,128)(2,1)} %bitcast.22, s32[]{:T(128)S(6)} %select_n.91, s32[]{:T(128)S(6)} %select_n.90, s32[]{:T(128)S(6)} %select_n.86), kind=kLoop, calls=%fused_computation.16 | loop fusion | bytes 1572876 | tf_op jit(solution)/shard_map/dynamic_slice | solution.py:167
  6.2 1.6 %collective-permute-start.5 = (bf16[256,512]{1,0:T(8,128)(2,1)}, bf16[256,512]{1,0:T(8,128)(2,1)S(1)}, u32[]{:S(2)}, u32[]{:S(2)}) collective-permute-start(bf16[256,512]{1,0:T(8,128)(2,1)} %get-tuple-element.38), channel_id=1, source_target_pairs={{0,4},{4,8},{8,12},{12,0},{28,24},{24,20},{20,16},{16,28},{1,5},{5... | collective-permute-start | bytes 786440 | tf_op jit(solution)/shard_map/ppermute | solution.py:173
  7.8 0.0 collective-permute-done.peer_ref
  7.8 0.1 convert_reduce_fusion
  7.9 1.6 %collective-permute-start.1 = (f32[32]{0:T(128)S(1)}, f32[32]{0:T(128)S(1)}, u32[]{:S(2)}, u32[]{:S(2)}) collective-permute-start(f32[32]{0:T(128)S(1)} %convert_reduce_fusion), channel_id=1, source_target_pairs={{0,2},{2,0},{1,3},{3,1},{4,6},{6,4},{5,7},{7,5},{8,10},{10,8},{9,1... | collective-permute-start | bytes 392 | tf_op jit(solution)/shard_map/ppermute | solution.py:190
  9.5 2.0 %collective-permute-done.1 = f32[32]{0:T(128)S(1)} collective-permute-done((f32[32]{0:T(128)S(1)}, f32[32]{0:T(128)S(1)}, u32[]{:S(2)}, u32[]{:S(2)}) %collective-permute-start.1) | collective-permute-done | bytes 160 | tf_op jit(solution)/shard_map/ppermute | solution.py:190
  11.5 0.1 concatenate.15
  11.7 0.7 %pad_maximum_fusion = bf16[272,512]{1,0:T(8,128)(2,1)} fusion(bf16[16,512]{1,0:T(8,128)(2,1)S(1)} %reshape.118, bf16[256,512]{1,0:T(8,128)(2,1)S(1)} %get-tuple-element.39), kind=kLoop, calls=%fused_computation | loop fusion | flops 557056 | bytes 557056 | tf_op jit(solution)/shard_map/concatenate | solution.py:199
  12.4 1.6 %collective-permute-start.2 = (bf16[272,512]{1,0:T(8,128)(2,1)}, bf16[272,512]{1,0:T(8,128)(2,1)}, u32[]{:S(2)}, u32[]{:S(2)}) collective-permute-start(bf16[272,512]{1,0:T(8,128)(2,1)} %pad_maximum_fusion), channel_id=1, source_target_pairs={{0,4},{4,8},{8,12},{12,0},{28,24},{24,20},{20,16},{16,28},{1,5},{5... | collective-permute-start | bytes 835592 | tf_op jit(solution)/shard_map/ppermute | solution.py:173
  14.0 0.0 collective-permute-done.3
  14.0 1.4 %collective-permute-start.4 = (bf16[256,512]{1,0:T(8,128)(2,1)}, bf16[256,512]{1,0:T(8,128)(2,1)}, u32[]{:S(2)}, u32[]{:S(2)}) collective-permute-start(bf16[256,512]{1,0:T(8,128)(2,1)} %collective-permute-done.3), channel_id=1, source_target_pairs={{4,20},{8,24},{24,8},{20,4},{5,21},{9,25},{25,9},{21,5},{6,22},{10... | collective-permute-start | bytes 786440 | tf_op jit(solution)/shard_map/ppermute | solution.py:219
  15.4 0.1 broadcast_and_fusion
  15.4 0.1 broadcast_in_dim.108
  15.5 0.1 broadcast_in_dim.113
  15.6 0.1 pad_add_fusion.units_ref
  15.7 3.4 %collective-permute-start.7 = (bf16[256,512]{1,0:T(8,128)(2,1)S(1)}, bf16[256,512]{1,0:T(8,128)(2,1)S(1)}, u32[]{:S(2)}, u32[]{:S(2)}) collective-permute-start(bf16[256,512]{1,0:T(8,128)(2,1)S(1)} %get-tuple-element.25), channel_id=1, source_target_pairs={{0,4},{4,8},{8,12},{12,0},{28,24},{24,20},{20,16},{16,28},{1,5},{5... | collective-permute-start | bytes 786440 | tf_op jit(solution)/shard_map/ppermute | solution.py:173
  19.1 0.0 collective-permute-start.6
  19.2 0.0 collective-permute-done.5.refs_0_
  19.2 1.4 %collective-permute-start.10 = (bf16[256,512]{1,0:T(8,128)(2,1)S(1)}, bf16[256,512]{1,0:T(8,128)(2,1)}, u32[]{:S(2)}, u32[]{:S(2)}) collective-permute-start(bf16[256,512]{1,0:T(8,128)(2,1)S(1)} %collective-permute-done.5.refs_0_), channel_id=1, source_target_pairs={{4,20},{8,24},{24,8},{20,4},{5,21},{9,25},{25,9},{21,5},{6,22},{10... | collective-permute-start | bytes 786440 | tf_op jit(solution)/shard_map/ppermute | solution.py:220
  20.5 0.1 convert_element_type.53
  20.6 0.0 collective-permute-done.4
  20.6 1.4 %collective-permute-start.13 = (bf16[256,512]{1,0:T(8,128)(2,1)}, bf16[256,512]{1,0:T(8,128)(2,1)}, u32[]{:S(2)}, u32[]{:S(2)}) collective-permute-start(bf16[256,512]{1,0:T(8,128)(2,1)} %collective-permute-done.4), channel_id=1, source_target_pairs={{20,8},{24,12},{8,20},{4,16},{21,9},{25,13},{9,21},{5,17},{22,10},... | collective-permute-start | bytes 786440 | tf_op jit(solution)/shard_map/ppermute | solution.py:173
  22.0 3.2 %collective-permute-done.2 = bf16[272,512]{1,0:T(8,128)(2,1)} collective-permute-done((bf16[272,512]{1,0:T(8,128)(2,1)}, bf16[272,512]{1,0:T(8,128)(2,1)}, u32[]{:S(2)}, u32[]{:S(2)}) %collective-permute-start.2) | collective-permute-done | bytes 278560 | tf_op jit(solution)/shard_map/ppermute | solution.py:173
  25.2 0.7 %slice_bitcast_fusion.1 = bf16[2,4,8,128]{3,2,1,0:T(8,128)(2,1)S(1)} fusion(bf16[272,512]{1,0:T(8,128)(2,1)} %collective-permute-done.2), kind=kLoop, calls=%fused_computation.2 | loop fusion | bytes 32768
  25.9 1.4 %collective-permute-start.9 = (bf16[272,512]{1,0:T(8,128)(2,1)}, bf16[272,512]{1,0:T(8,128)(2,1)}, u32[]{:S(2)}, u32[]{:S(2)}) collective-permute-start(bf16[272,512]{1,0:T(8,128)(2,1)} %collective-permute-done.2), channel_id=1, source_target_pairs={{4,8},{8,12},{24,20},{20,16},{5,9},{9,13},{25,21},{21,17},{6,10},{... | collective-permute-start | bytes 835592 | tf_op jit(solution)/shard_map/ppermute | solution.py:225
  27.3 3.2 %collective-permute-done.7.refs_2_ = bf16[256,512]{1,0:T(8,128)(2,1)S(1)} collective-permute-done((bf16[256,512]{1,0:T(8,128)(2,1)S(1)}, bf16[256,512]{1,0:T(8,128)(2,1)S(1)}, u32[]{:S(2)}, u32[]{:S(2)}) %collective-permute-start.7) | collective-permute-done | bytes 262176 | tf_op jit(solution)/shard_map/ppermute | solution.py:173
  30.5 0.1 dynamic-slice_convert_fusion.1
  30.6 0.1 concatenate.17.info_ref
  30.7 0.7 %slice_convert_fusion.1 = f32[4,512]{1,0:T(4,128)S(1)} fusion(bf16[272,512]{1,0:T(8,128)(2,1)} %collective-permute-done.2), kind=kLoop, calls=%fused_computation.10 | loop fusion | flops 2048 | bytes 12288 | tf_op jit(solution)/shard_map/convert_element_type | solution.py:229
  31.4 0.0 collective-permute-done.6.refs_1_
  31.4 0.7 %copy-done.1 = bf16[256,512]{1,0:T(8,128)(2,1)} copy-done((bf16[256,512]{1,0:T(8,128)(2,1)}, bf16[256,512]{1,0:T(8,128)(2,1)S(1)}, u32[]{:S(2)}) %copy-start.1) | copy-done | bytes 262168
  32.1 0.7 %collective-permute-start.15 = (bf16[256,512]{1,0:T(8,128)(2,1)S(1)}, bf16[256,512]{1,0:T(8,128)(2,1)S(1)}, u32[]{:S(2)}, u32[]{:S(2)}) collective-permute-start(bf16[256,512]{1,0:T(8,128)(2,1)S(1)} %collective-permute-done.7.refs_2_), channel_id=1, source_target_pairs={{4,8},{8,12},{24,20},{20,16},{5,9},{9,13},{25,21},{21,17},{6,10},{... | collective-permute-start | bytes 786440 | tf_op jit(solution)/shard_map/ppermute | solution.py:249
  32.8 0.7 %collective-permute-start.11 = (bf16[256,512]{1,0:T(8,128)(2,1)}, bf16[256,512]{1,0:T(8,128)(2,1)S(1)}, u32[]{:S(2)}, u32[]{:S(2)}) collective-permute-start(bf16[256,512]{1,0:T(8,128)(2,1)} %collective-permute-done.10), channel_id=1, source_target_pairs={{20,8},{24,12},{8,20},{4,16},{21,9},{25,13},{9,21},{5,17},{22,10},... | collective-permute-start | bytes 786440 | tf_op jit(solution)/shard_map/ppermute | solution.py:173
  33.4 0.0 collective-permute-done.8.refs_3_
  33.5 0.9 %copy-done.2 = bf16[256,512]{1,0:T(8,128)(2,1)S(1)} copy-done((bf16[256,512]{1,0:T(8,128)(2,1)S(1)}, bf16[256,512]{1,0:T(8,128)(2,1)}, u32[]{:S(2)}) %copy-start.2) | copy-done | bytes 262168
  34.4 2.9 %shard_map.64 = (f32[8,256]{1,0:T(8,128)S(1)}, f32[2,256]{1,0:T(2,128)S(1)}) custom-call(s32[49]{0:T(128)S(1)} %concatenate.17.info_ref, s32[2]{0:T(128)S(1)} %pad_add_fusion.units_ref, bf16[8,256,512]{2,1,0:T(8,128)(2,1)S(1)} %copy-done, bf16[8,256,512]{2,1,0:T(8,128)(2,1)} %collective-permute-done.peer_ref, ...), custom_call_target="tpu_custom_call" | custom-call | tf_op jit(solution)/shard_map/pallas_call | solution.py:107
  37.4 2.9 %collective-permute-start.12 = (f32[2,256]{1,0:T(2,128)S(1)}, f32[2,256]{1,0:T(2,128)S(1)}, u32[]{:S(2)}, u32[]{:S(2)}) collective-permute-start(f32[2,256]{1,0:T(2,128)S(1)} %get-tuple-element.30), channel_id=1, source_target_pairs={{4,0},{8,4},{12,8},{0,12},{24,28},{20,24},{16,20},{28,16},{5,1},{9... | collective-permute-start | bytes 6152 | tf_op jit(solution)/shard_map/ppermute | solution.py:257
  40.2 0.0 collective-permute-done.13
  40.2 0.6 collective-permute-start.14
  40.9 0.0 collective-permute-done.9
  40.9 0.7 %slice_bitcast_fusion = bf16[2,4,8,128]{3,2,1,0:T(8,128)(2,1)S(1)} fusion(bf16[272,512]{1,0:T(8,128)(2,1)} %collective-permute-done.9), kind=kLoop, calls=%fused_computation.1 | loop fusion | bytes 32768
  41.6 0.1 collective-permute-start.16
  41.7 0.7 %slice_convert_fusion = f32[4,512]{1,0:T(4,128)S(1)} fusion(bf16[272,512]{1,0:T(8,128)(2,1)} %collective-permute-done.9), kind=kLoop, calls=%fused_computation.9 | loop fusion | flops 2048 | bytes 12288 | tf_op jit(solution)/shard_map/convert_element_type | solution.py:229
  42.4 0.1 dynamic-slice_convert_fusion
  42.5 0.1 concatenate.18.info_ref
  42.6 2.2 %collective-permute-done.12 = f32[2,256]{1,0:T(2,128)S(1)} collective-permute-done((f32[2,256]{1,0:T(2,128)S(1)}, f32[2,256]{1,0:T(2,128)S(1)}, u32[]{:S(2)}, u32[]{:S(2)}) %collective-permute-start.12) | collective-permute-done | bytes 2080 | tf_op jit(solution)/shard_map/ppermute | solution.py:257
  44.8 0.0 collective-permute-done.14.refs_1_
  44.8 0.0 collective-permute-done.16.refs_3_
  44.8 1.1 %shard_map.65 = (f32[8,256]{1,0:T(8,128)S(1)}, f32[2,256]{1,0:T(2,128)S(1)}) custom-call(s32[49]{0:T(128)S(1)} %concatenate.18.info_ref, s32[2]{0:T(128)S(1)} %pad_add_fusion.units_ref, bf16[8,256,512]{2,1,0:T(8,128)(2,1)S(1)} %copy-done, bf16[8,256,512]{2,1,0:T(8,128)(2,1)} %collective-permute-done.peer_ref, ...), custom_call_target="tpu_custom_call" | custom-call | tf_op jit(solution)/shard_map/pallas_call | solution.py:107
  45.9 0.1 broadcast_select_fusion
  46.0 0.1 select_add_fusion
  46.1 0.0 collective-permute-start.17
  46.1 1.2 %collective-permute-done.17 = f32[12,256]{1,0:T(8,128)S(1)} collective-permute-done((f32[12,256]{1,0:T(8,128)S(1)}, f32[12,256]{1,0:T(8,128)S(1)}, u32[]{:S(2)}, u32[]{:S(2)}) %collective-permute-start.17) | collective-permute-done | bytes 12320 | tf_op jit(solution)/shard_map/ppermute | solution.py:276
  47.3 1.2 %collective-permute-start.18 = (f32[8,256]{1,0:T(8,128)S(1)}, f32[8,256]{1,0:T(8,128)S(1)}, u32[]{:S(2)}, u32[]{:S(2)}) collective-permute-start(f32[8,256]{1,0:T(8,128)S(1)} %slice.42), channel_id=1, source_target_pairs={{0,2},{2,0},{1,3},{3,1},{4,6},{6,4},{5,7},{7,5},{8,10},{10,8},{9,1... | collective-permute-start | bytes 24584 | tf_op jit(solution)/shard_map/ppermute | solution.py:285
  48.5 7.0 %collective-permute-start.19 = (f32[4,256]{1,0:T(4,128)S(1)}, f32[4,256]{1,0:T(4,128)S(1)}, u32[]{:S(2)}, u32[]{:S(2)}) collective-permute-start(f32[4,256]{1,0:T(4,128)S(1)} %slice.43), channel_id=1, source_target_pairs={{8,0},{10,2},{12,4},{14,6},{0,8},{2,10},{4,12},{6,14},{20,28},{22,... | collective-permute-start | bytes 12296 | tf_op jit(solution)/shard_map/ppermute | solution.py:286
  55.5 0.0 collective-permute-start.20
  55.5 0.1 broadcast_in_dim.118
  55.6 0.1 broadcast_in_dim.119
  55.7 1.4 %collective-permute-done.19 = f32[4,256]{1,0:T(4,128)S(1)} collective-permute-done((f32[4,256]{1,0:T(4,128)S(1)}, f32[4,256]{1,0:T(4,128)S(1)}, u32[]{:S(2)}, u32[]{:S(2)}) %collective-permute-start.19) | collective-permute-done | bytes 4128 | tf_op jit(solution)/shard_map/ppermute | solution.py:286
  57.1 3.8 %collective-permute-done.20 = f32[4,256]{1,0:T(4,128)S(1)} collective-permute-done((f32[4,256]{1,0:T(4,128)S(1)}, f32[4,256]{1,0:T(4,128)S(1)}, u32[]{:S(2)}, u32[]{:S(2)}) %collective-permute-start.20) | collective-permute-done | bytes 4128 | tf_op jit(solution)/shard_map/ppermute | solution.py:287
  60.9 0.7 %add_log-plus-one_fusion = f32[8,256]{1,0:T(8,128)} fusion(f32[8,256]{1,0:T(8,128)S(1)} %broadcast_in_dim.122, f32[8,256]{1,0:T(8,128)S(1)} %broadcast_in_dim.124, f32[8,256]{1,0:T(8,128)S(1)} %collective-permute-done.18, pred[8]{0:T(512)(128)(4,1)S(1)} %broadcast_in_dim.119, f32[12,256]{1,0:T(8,128)S(1)} %fusion.5), kind=kLoop, calls=%fused_computation.4 | loop fusion | flops 6144 | bytes 40968 | tf_op jit(solution)/shard_map/log1p | solution.py:292
  (49 shorter events, 0.3 us)
Async XLA Ops:
  0.0 33.5 %copy-start = (bf16[8,256,512]{2,1,0:T(8,128)(2,1)S(1)}, bf16[8,256,512]{2,1,0:T(8,128)(2,1)}, u32[]{:S(2)}) copy-start(bf16[8,256,512]{2,1,0:T(8,128)(2,1)} %own_ref.3) | copy-start | bytes 6291460
  0.0 7.7 %copy-start.3 = (bf16[8,256]{1,0:T(8,128)(2,1)S(1)}, bf16[8,256]{1,0:T(8,128)(2,1)}, u32[]{:S(2)}) copy-start(bf16[8,256]{1,0:T(8,128)(2,1)} %param.7) | copy-start | bytes 12292
  0.0 7.7 %copy-start.4 = (s32[8]{0:T(128)S(1)}, s32[8]{0:T(128)}, u32[]{:S(2)}) copy-start(s32[8]{0:T(128)} %param.8) | copy-start | bytes 100
  0.0 7.8 %copy-start.7 = (s32[1,1,12,1]{2,3,1,0:T(1,128)S(1)}, s32[1,1,12,1]{2,3,1,0:T(1,128)}, u32[]{:S(2)}) copy-start(s32[1,1,12,1]{2,3,1,0:T(1,128)} %param.10) | copy-start | bytes 148
  0.0 7.8 %copy-start.6 = (s32[1,1,12]{2,1,0:T(1,128)S(1)}, s32[1,1,12]{2,1,0:T(1,128)}, u32[]{:S(2)}) copy-start(s32[1,1,12]{2,1,0:T(1,128)} %param.11) | copy-start | bytes 148
  0.0 9.5 %copy-start.5 = (s32[8]{0:T(128)S(1)}, s32[8]{0:T(128)}, u32[]{:S(2)}) copy-start(s32[8]{0:T(128)} %param.9) | copy-start | bytes 100
  0.0 7.8 %collective-permute-start = (bf16[8,256,512]{2,1,0:T(8,128)(2,1)}, bf16[8,256,512]{2,1,0:T(8,128)(2,1)}, u32[]{:S(2)}, u32[]{:S(2)}) collective-permute-start(bf16[8,256,512]{2,1,0:T(8,128)(2,1)} %own_ref.3), channel_id=1, source_target_pairs={{0,1},{1,0},{2,3},{3,2},{4,5},{5,4},{6,7},{7,6},{8,9},{9,8},{10,11... | collective-permute-start | bytes 6291464 | tf_op jit(solution)/shard_map/ppermute | solution.py:179
  1.5 12.4 %collective-permute-start.3 = (bf16[256,512]{1,0:T(8,128)(2,1)S(1)}, bf16[256,512]{1,0:T(8,128)(2,1)}, u32[]{:S(2)}, u32[]{:S(2)}) collective-permute-start(bf16[256,512]{1,0:T(8,128)(2,1)S(1)} %constant_dynamic-slice_fusion.4), channel_id=1, source_target_pairs={{0,4},{4,8},{8,12},{12,0},{28,24},{24,20},{20,16},{16,28},{1,5},{5... | collective-permute-start | bytes 786440 | tf_op jit(solution)/shard_map/ppermute | solution.py:173
  6.2 13.0 %collective-permute-start.5 = (bf16[256,512]{1,0:T(8,128)(2,1)}, bf16[256,512]{1,0:T(8,128)(2,1)S(1)}, u32[]{:S(2)}, u32[]{:S(2)}) collective-permute-start(bf16[256,512]{1,0:T(8,128)(2,1)} %get-tuple-element.38), channel_id=1, source_target_pairs={{0,4},{4,8},{8,12},{12,0},{28,24},{24,20},{20,16},{16,28},{1,5},{5... | collective-permute-start | bytes 786440 | tf_op jit(solution)/shard_map/ppermute | solution.py:173
  7.9 3.6 %collective-permute-start.1 = (f32[32]{0:T(128)S(1)}, f32[32]{0:T(128)S(1)}, u32[]{:S(2)}, u32[]{:S(2)}) collective-permute-start(f32[32]{0:T(128)S(1)} %convert_reduce_fusion), channel_id=1, source_target_pairs={{0,2},{2,0},{1,3},{3,1},{4,6},{6,4},{5,7},{7,5},{8,10},{10,8},{9,1... | collective-permute-start | bytes 392 | tf_op jit(solution)/shard_map/ppermute | solution.py:190
  12.4 12.8 %collective-permute-start.2 = (bf16[272,512]{1,0:T(8,128)(2,1)}, bf16[272,512]{1,0:T(8,128)(2,1)}, u32[]{:S(2)}, u32[]{:S(2)}) collective-permute-start(bf16[272,512]{1,0:T(8,128)(2,1)} %pad_maximum_fusion), channel_id=1, source_target_pairs={{0,4},{4,8},{8,12},{12,0},{28,24},{24,20},{20,16},{16,28},{1,5},{5... | collective-permute-start | bytes 835592 | tf_op jit(solution)/shard_map/ppermute | solution.py:173
  14.0 6.6 %collective-permute-start.4 = (bf16[256,512]{1,0:T(8,128)(2,1)}, bf16[256,512]{1,0:T(8,128)(2,1)}, u32[]{:S(2)}, u32[]{:S(2)}) collective-permute-start(bf16[256,512]{1,0:T(8,128)(2,1)} %collective-permute-done.3), channel_id=1, source_target_pairs={{4,20},{8,24},{24,8},{20,4},{5,21},{9,25},{25,9},{21,5},{6,22},{10... | collective-permute-start | bytes 786440 | tf_op jit(solution)/shard_map/ppermute | solution.py:219
  15.7 14.8 %collective-permute-start.7 = (bf16[256,512]{1,0:T(8,128)(2,1)S(1)}, bf16[256,512]{1,0:T(8,128)(2,1)S(1)}, u32[]{:S(2)}, u32[]{:S(2)}) collective-permute-start(bf16[256,512]{1,0:T(8,128)(2,1)S(1)} %get-tuple-element.25), channel_id=1, source_target_pairs={{0,4},{4,8},{8,12},{12,0},{28,24},{24,20},{20,16},{16,28},{1,5},{5... | collective-permute-start | bytes 786440 | tf_op jit(solution)/shard_map/ppermute | solution.py:173
  19.1 12.2 %collective-permute-start.6 = (bf16[256,512]{1,0:T(8,128)(2,1)}, bf16[256,512]{1,0:T(8,128)(2,1)S(1)}, u32[]{:S(2)}, u32[]{:S(2)}) collective-permute-start(bf16[256,512]{1,0:T(8,128)(2,1)} %collective-permute-done.3), channel_id=1, source_target_pairs={{0,1},{1,0},{2,3},{3,2},{4,5},{5,4},{6,7},{7,6},{8,9},{9,8},{10,11... | collective-permute-start | bytes 786440 | tf_op jit(solution)/shard_map/ppermute | solution.py:208
  19.2 13.6 %collective-permute-start.10 = (bf16[256,512]{1,0:T(8,128)(2,1)S(1)}, bf16[256,512]{1,0:T(8,128)(2,1)}, u32[]{:S(2)}, u32[]{:S(2)}) collective-permute-start(bf16[256,512]{1,0:T(8,128)(2,1)S(1)} %collective-permute-done.5.refs_0_), channel_id=1, source_target_pairs={{4,20},{8,24},{24,8},{20,4},{5,21},{9,25},{25,9},{21,5},{6,22},{10... | collective-permute-start | bytes 786440 | tf_op jit(solution)/shard_map/ppermute | solution.py:220
  20.6 19.6 %collective-permute-start.13 = (bf16[256,512]{1,0:T(8,128)(2,1)}, bf16[256,512]{1,0:T(8,128)(2,1)}, u32[]{:S(2)}, u32[]{:S(2)}) collective-permute-start(bf16[256,512]{1,0:T(8,128)(2,1)} %collective-permute-done.4), channel_id=1, source_target_pairs={{20,8},{24,12},{8,20},{4,16},{21,9},{25,13},{9,21},{5,17},{22,10},... | collective-permute-start | bytes 786440 | tf_op jit(solution)/shard_map/ppermute | solution.py:173
  25.9 14.9 %collective-permute-start.9 = (bf16[272,512]{1,0:T(8,128)(2,1)}, bf16[272,512]{1,0:T(8,128)(2,1)}, u32[]{:S(2)}, u32[]{:S(2)}) collective-permute-start(bf16[272,512]{1,0:T(8,128)(2,1)} %collective-permute-done.2), channel_id=1, source_target_pairs={{4,8},{8,12},{24,20},{20,16},{5,9},{9,13},{25,21},{21,17},{6,10},{... | collective-permute-start | bytes 835592 | tf_op jit(solution)/shard_map/ppermute | solution.py:225
  30.5 2.9 %collective-permute-start.8 = (bf16[272,512]{1,0:T(8,128)(2,1)}, bf16[272,512]{1,0:T(8,128)(2,1)S(1)}, u32[]{:S(2)}, u32[]{:S(2)}) collective-permute-start(bf16[272,512]{1,0:T(8,128)(2,1)} %collective-permute-done.2), channel_id=1, source_target_pairs={{0,1},{1,0},{2,3},{3,2},{4,5},{5,4},{6,7},{7,6},{8,9},{9,8},{10,11... | collective-permute-start | bytes 835592 | tf_op jit(solution)/shard_map/ppermute | solution.py:208
  31.4 0.7 %copy-start.1 = (bf16[256,512]{1,0:T(8,128)(2,1)}, bf16[256,512]{1,0:T(8,128)(2,1)S(1)}, u32[]{:S(2)}) copy-start(bf16[256,512]{1,0:T(8,128)(2,1)S(1)} %collective-permute-done.6.refs_1_) | copy-start | bytes 786436
  32.1 10.5 %collective-permute-start.15 = (bf16[256,512]{1,0:T(8,128)(2,1)S(1)}, bf16[256,512]{1,0:T(8,128)(2,1)S(1)}, u32[]{:S(2)}, u32[]{:S(2)}) collective-permute-start(bf16[256,512]{1,0:T(8,128)(2,1)S(1)} %collective-permute-done.7.refs_2_), channel_id=1, source_target_pairs={{4,8},{8,12},{24,20},{20,16},{5,9},{9,13},{25,21},{21,17},{6,10},{... | collective-permute-start | bytes 786440 | tf_op jit(solution)/shard_map/ppermute | solution.py:249
  32.8 12.0 %collective-permute-start.11 = (bf16[256,512]{1,0:T(8,128)(2,1)}, bf16[256,512]{1,0:T(8,128)(2,1)S(1)}, u32[]{:S(2)}, u32[]{:S(2)}) collective-permute-start(bf16[256,512]{1,0:T(8,128)(2,1)} %collective-permute-done.10), channel_id=1, source_target_pairs={{20,8},{24,12},{8,20},{4,16},{21,9},{25,13},{9,21},{5,17},{22,10},... | collective-permute-start | bytes 786440 | tf_op jit(solution)/shard_map/ppermute | solution.py:173
  33.5 1.0 %copy-start.2 = (bf16[256,512]{1,0:T(8,128)(2,1)S(1)}, bf16[256,512]{1,0:T(8,128)(2,1)}, u32[]{:S(2)}) copy-start(bf16[256,512]{1,0:T(8,128)(2,1)} %copy-done.1) | copy-start | bytes 786436
  37.4 7.4 %collective-permute-start.12 = (f32[2,256]{1,0:T(2,128)S(1)}, f32[2,256]{1,0:T(2,128)S(1)}, u32[]{:S(2)}, u32[]{:S(2)}) collective-permute-start(f32[2,256]{1,0:T(2,128)S(1)} %get-tuple-element.30), channel_id=1, source_target_pairs={{4,0},{8,4},{12,8},{0,12},{24,28},{20,24},{16,20},{28,16},{5,1},{9... | collective-permute-start | bytes 6152 | tf_op jit(solution)/shard_map/ppermute | solution.py:257
  40.2 4.6 %collective-permute-start.14 = (bf16[256,512]{1,0:T(8,128)(2,1)}, bf16[256,512]{1,0:T(8,128)(2,1)S(1)}, u32[]{:S(2)}, u32[]{:S(2)}) collective-permute-start(bf16[256,512]{1,0:T(8,128)(2,1)} %collective-permute-done.13), channel_id=1, source_target_pairs={{0,1},{1,0},{2,3},{3,2},{4,5},{5,4},{6,7},{7,6},{8,9},{9,8},{10,11... | collective-permute-start | bytes 786440 | tf_op jit(solution)/shard_map/ppermute | solution.py:208
  41.6 3.2 %collective-permute-start.16 = (bf16[272,512]{1,0:T(8,128)(2,1)}, bf16[272,512]{1,0:T(8,128)(2,1)S(1)}, u32[]{:S(2)}, u32[]{:S(2)}) collective-permute-start(bf16[272,512]{1,0:T(8,128)(2,1)} %collective-permute-done.9), channel_id=1, source_target_pairs={{0,1},{1,0},{2,3},{3,2},{4,5},{5,4},{6,7},{7,6},{8,9},{9,8},{10,11... | collective-permute-start | bytes 835592 | tf_op jit(solution)/shard_map/ppermute | solution.py:208
  46.1 1.2 %collective-permute-start.17 = (f32[12,256]{1,0:T(8,128)S(1)}, f32[12,256]{1,0:T(8,128)S(1)}, u32[]{:S(2)}, u32[]{:S(2)}) collective-permute-start(f32[12,256]{1,0:T(8,128)S(1)} %pad_maximum_fusion.1), channel_id=1, source_target_pairs={{0,1},{1,0},{2,3},{3,2},{4,5},{5,4},{6,7},{7,6},{8,9},{9,8},{10,11... | collective-permute-start | bytes 36872 | tf_op jit(solution)/shard_map/ppermute | solution.py:276
  47.3 13.6 %collective-permute-start.18 = (f32[8,256]{1,0:T(8,128)S(1)}, f32[8,256]{1,0:T(8,128)S(1)}, u32[]{:S(2)}, u32[]{:S(2)}) collective-permute-start(f32[8,256]{1,0:T(8,128)S(1)} %slice.42), channel_id=1, source_target_pairs={{0,2},{2,0},{1,3},{3,1},{4,6},{6,4},{5,7},{7,5},{8,10},{10,8},{9,1... | collective-permute-start | bytes 24584 | tf_op jit(solution)/shard_map/ppermute | solution.py:285
  48.5 8.6 %collective-permute-start.19 = (f32[4,256]{1,0:T(4,128)S(1)}, f32[4,256]{1,0:T(4,128)S(1)}, u32[]{:S(2)}, u32[]{:S(2)}) collective-permute-start(f32[4,256]{1,0:T(4,128)S(1)} %slice.43), channel_id=1, source_target_pairs={{8,0},{10,2},{12,4},{14,6},{0,8},{2,10},{4,12},{6,14},{20,28},{22,... | collective-permute-start | bytes 12296 | tf_op jit(solution)/shard_map/ppermute | solution.py:286
  55.5 5.4 %collective-permute-start.20 = (f32[4,256]{1,0:T(4,128)S(1)}, f32[4,256]{1,0:T(4,128)S(1)}, u32[]{:S(2)}, u32[]{:S(2)}) collective-permute-start(f32[4,256]{1,0:T(4,128)S(1)} %slice.43), channel_id=1, source_target_pairs={{8,2},{10,0},{12,6},{14,4},{0,10},{2,8},{4,14},{6,12},{20,30},{22,... | collective-permute-start | bytes 12296 | tf_op jit(solution)/shard_map/ppermute | solution.py:287

commit v5 on v4

--- a/solution.py
+++ b/solution.py
@@ -1,3 +1,4 @@
+import functools
 import math
 
 import jax
@@ -13,15 +14,12 @@
 
 
 def tile_kernel(info_ref, units_ref, own_ref, peer_ref, *refs):
-    count = len(refs) - 8
+    count = len(refs) - 11
     parts = refs[:count]
-    (scale_ref, part_scale_ref, rows_ref, columns_ref,
-     held_ref, total_ref, wide_ref, copied) = refs[count:]
-    blocks, rows, _ = own_ref.shape
+    (scale_ref, rows_ref, columns_ref, held_ref, total_ref, wide_ref, part_ref, raw_ref, note_ref,
+     copied, part_copied) = refs[count:]
+    blocks, rows, width = own_ref.shape
     segments, unit = columns_ref.shape
-
-    def part(half, segment):
-        return parts[2 * segment + half][:unit, :]
 
     def copies(block):
         return [
@@ -29,6 +27,18 @@
             for half, whole in enumerate((own_ref, peer_ref))
         ]
 
+    note_rows = parts[-1].shape[0] - unit
+    part_copies = [
+        pltpu.make_async_copy(
+            part.at[pl.ds(0, unit)], part_ref.at[i % 2, pl.ds(i // 2 * unit, unit)], part_copied.at[i]
+        )
+        for i, part in enumerate(parts)
+    ]
+    part_copies.append(pltpu.make_async_copy(
+        parts[-1].at[pl.ds(unit, note_rows)], raw_ref, part_copied.at[count]
+    ))
+    for copy in part_copies:
+        copy.start()
     valid, weights = [], []
     for segment in range(segments):
         first_row = units_ref[segment] * unit
@@ -51,46 +61,70 @@
             for copy in copies(block):
                 copy.start()
 
+    rows_ref[...] = jnp.zeros_like(rows_ref)
+    total_ref[...] = jnp.zeros_like(total_ref)
+    for copy in part_copies:
+        copy.wait()
+    note_ref[...] = raw_ref[...].astype(jnp.float32)
+    in_row = width // unit
     for segment in range(segments):
-        part_scale = jnp.broadcast_to(part_scale_ref[pl.ds(units_ref[segment], 1), :], (LANES, unit))
-        wide_ref[0, segment] = jnp.transpose(part_scale)
+        line = note_ref[pl.ds(units_ref[segment] // in_row, 1), :]
+        at = units_ref[segment] % in_row
+        part_scale = line[:, :unit]
+        for i in range(1, in_row):
+            part_scale = jnp.where(at == i, line[:, i * unit : (i + 1) * unit], part_scale)
+        wide_ref[0, segment] = jnp.transpose(jnp.broadcast_to(part_scale, (LANES, unit)))
         row_ids = lax.broadcasted_iota(jnp.int32, (unit, LANES), 0)
         wide_ref[1, segment] = (row_ids < valid[segment]).astype(jnp.float32)
-    rows_ref[...] = jnp.zeros_like(rows_ref)
-    total_ref[...] = jnp.zeros_like(total_ref)
+
+    def product(block, first, length):
+        return sum(
+            lax.dot_general(
+                part_ref[half, first : first + length, :], held_ref[block, half], NT,
+                preferred_element_type=jnp.float32,
+            )
+            for half in range(2)
+        )
+
+    def tile(segment, block, gram):
+        factor = weights[segment][block].astype(jnp.float32)
+        row_ids = lax.broadcasted_iota(jnp.int32, (1, LANES), 1)
+        for start in range(0, rows, LANES):
+            own_scale = scale_ref[block : block + 1, start : start + LANES] * LOG2E
+            own_valid = jnp.where(row_ids + start < info_ref[blocks + block], factor, 0.0)
+            summed = jnp.zeros((8, LANES), jnp.float32)
+            for at in range(0, unit, 64):
+                here = pl.ds(at, 64)
+                scaled = gram[at : at + 64, start : start + LANES] * (
+                    wide_ref[0, segment, here, :] * own_scale
+                )
+                kern = jnp.exp2(scaled) * wide_ref[1, segment, here, :]
+                summed = summed + jnp.sum(kern.reshape(-1, 8, LANES), axis=0)
+                total_ref[segment, here, :] += kern * own_valid
+            rows_ref[block : block + 1, start : start + LANES] += own_valid * jnp.sum(
+                summed, axis=0, keepdims=True
+            )
+
     for block in range(blocks):
 
         @pl.when(needed[block] != 0)
         def _(block=block):
             for copy in copies(block):
                 copy.wait()
+            wanted = [weights[segment][block] != 0 for segment in range(segments)]
+            every = functools.reduce(jnp.logical_and, wanted)
+
+            @pl.when(every)
+            def _():
+                gram = product(block, 0, segments * unit)
+                for segment in range(segments):
+                    tile(segment, block, gram[segment * unit : (segment + 1) * unit])
+
             for segment in range(segments):
 
-                @pl.when(weights[segment][block] != 0)
+                @pl.when(wanted[segment] & jnp.logical_not(every))
                 def _(segment=segment):
-                    gram = lax.dot_general(
-                        part(0, segment), held_ref[block, 0], NT, preferred_element_type=jnp.float32
-                    ) + lax.dot_general(
-                        part(1, segment), held_ref[block, 1], NT, preferred_element_type=jnp.float32
-                    )
-                    factor = weights[segment][block].astype(jnp.float32)
-                    row_ids = lax.broadcasted_iota(jnp.int32, (1, LANES), 1)
-                    for start in range(0, rows, LANES):
-                        own_scale = scale_ref[block : block + 1, start : start + LANES] * LOG2E
-                        own_valid = jnp.where(
-                            row_ids + start < info_ref[blocks + block], factor, 0.0
-                        )
-                        summed = jnp.zeros((8, LANES), jnp.float32)
-                        for at in range(0, unit, 64):
-                            scaled = gram[at : at + 64, start : start + LANES] * (
-                                wide_ref[0, segment, at : at + 64, :] * own_scale
-                            )
-                            kern = jnp.exp2(scaled) * wide_ref[1, segment, at : at + 64, :]
-                            summed = summed + jnp.sum(kern.reshape(-1, 8, LANES), axis=0)
-                            total_ref[segment, at : at + 64, :] += kern * own_valid
-                        rows_ref[block : block + 1, start : start + LANES] += own_valid * jnp.sum(
-                            summed, axis=0, keepdims=True
-                        )
+                    tile(segment, block, product(block, segment * unit, unit))
 
     for segment in range(segments):
         columns_ref[segment : segment + 1, :] = jnp.sum(
@@ -98,9 +132,9 @@
         )
 
 
-def tile_sums(info, units, own, peer, parts, scale, part_scale):
+def tile_sums(info, units, own, peer, parts, scale):
     blocks, rows, width = own.shape
-    segments, unit = len(parts) // 2, part_scale.shape[1]
+    segments, unit = len(parts) // 2, parts[0].shape[0]
     smem = pl.BlockSpec(memory_space=pltpu.SMEM)
     vmem = pl.BlockSpec(memory_space=pltpu.VMEM)
     held = pl.BlockSpec(memory_space=pl.ANY)
@@ -110,17 +144,21 @@
             jax.ShapeDtypeStruct((blocks, rows), jnp.float32),
             jax.ShapeDtypeStruct((segments, unit), jnp.float32),
         ),
-        in_specs=[smem, smem, held, held] + [vmem] * (2 + len(parts)),
+        in_specs=[smem, smem, held, held] + [held] * len(parts) + [vmem],
         out_specs=(vmem, vmem),
         scratch_shapes=[
             pltpu.VMEM((blocks, 2, rows, width), own.dtype),
             pltpu.VMEM((segments, unit, LANES), jnp.float32),
             pltpu.VMEM((2, segments, unit, LANES), jnp.float32),
+            pltpu.VMEM((2, segments * unit, width), own.dtype),
+            pltpu.VMEM((parts[-1].shape[0] - unit, width), own.dtype),
+            pltpu.VMEM((parts[-1].shape[0] - unit, width), jnp.float32),
             pltpu.SemaphoreType.DMA((blocks, 2)),
+            pltpu.SemaphoreType.DMA((len(parts) + 1,)),
         ],
         compiler_params=pltpu.CompilerParams(vmem_limit_bytes=32 * 1024 * 1024),
         cost_estimate=pl.CostEstimate(flops=0, bytes_accessed=0, transcendentals=0),
-    )(info, units, own, peer, *parts, scale, part_scale)
+    )(info, units, own, peer, *parts, scale)
 
 
 def per_device(codes, scales, cluster_ids, row_counts, route_offsets, partner_local):
@@ -226,7 +264,6 @@
         note = held_second[0][unit:].reshape(-1)
         scale_end = blocks * rows
         cluster_end, count_end = scale_end + blocks, scale_end + 2 * blocks
-        part_scale = note[:scale_end].astype(jnp.float32).reshape(-1, unit)
         from_owner = (owner - sign * step) % owners
         active = ((ring_place - step) % owners) < origins(step)
         info = jnp.concatenate([
@@ -248,7 +285,7 @@
             info = follow(info, one)
             second[1] = lax.ppermute(held_second[1], line, perm)
         row_sums, columns = tile_sums(
-            info, units, codes, peer_codes, chunks, scale_root, part_scale
+            info, units, codes, peer_codes, chunks, scale_root
         )
         row_parts.append(row_sums)
         if step < rounds:

time: 61.7 us -> 61 us (0.989); the launches traced: 61.6 us -> 60.1 us
  starting transfers between devices: 30.1 us -> 27.6 us
  Pallas kernels: 4.03 us -> 6.35 us
  other arithmetic: 3.43 us -> 2.04 us
    pallas_call x2, Pallas kernels: 4.03 us -> 6.35 us  [tile_sums(): pl.pallas_call(tile_kernel, out_shape=(jax.ShapeDtypeStruct((blocks, rows...]
    ppermute x1, starting transfers between devices: 2.87 us -> 1.09 us  [per_device(): lax.ppermute(columns, line, [(place(g, o + step), place(g, o)) for g in r...]
    convert_element_type x2 -> x0, other arithmetic: 1.4 us -> none  [per_device(): part_scale = note[:scale_end].astype(jnp.float32).reshape(-1, unit)]
    ppermute x1, starting transfers between devices: 7.01 us -> 5.82 us  [per_device(): lax.ppermute(outgoing, joint, [(s, t + p) for s, t, p in back])]
  transfers between devices with their start and end apart: 21 -> 21, of which waited for: 7 -> 7; matrix products, arithmetic and copies ran while one was open for 12% -> 10% of each run, Pallas kernels for 5% -> 8%
where the time goes in v5:
time: 61 us; the launch traced here: 60.1 us
  starting transfers between devices  27.6 us (45%)
  waiting for transfers between devices  17.1 us (28%)
  local copies, waits for them, and re-layouts  6.76 us (11%)
  Pallas kernels  6.35 us (10%)
  other arithmetic  2.04 us (3%)
    ppermute x6, starting transfers between devices, send(): return [lax.ppermute(array, line, to) for array in arrays]  11.4 us
    ppermute x6, waiting for transfers between devices, send(): return [lax.ppermute(array, line, to) for array in arrays]  6.4 us
    pallas_call x2, Pallas kernels, tile_sums(): pl.pallas_call(tile_kernel, out_shape=(jax.ShapeDtypeStruct((blocks, rows...  6.35 us
    ppermute x1, starting transfers between devices, per_device(): lax.ppermute(outgoing, joint, [(s, t + p) for s, t, p in back])  5.82 us
    ppermute x1, waiting for transfers between devices, per_device(): lax.ppermute(outgoing, joint, [(s, t + 1 - p) for s, t, p in back])  3.81 us
    unnamed x21, local copies, waits for them, and re-layouts  3.13 us
    dynamic_slice x2, local copies, waits for them, and re-layouts, quarter(): return lax.dynamic_slice_in_dim(flat, pair * share + number * unit, unit, 0)  2.84 us
    ppermute x1, waiting for transfers between devices, per_device(): lax.ppermute(columns, line, [(place(g, o + step), place(g, o)) for g in r...  2.42 us
  transfers between devices with their start and end apart: 21, of which 7 were waited for; matrix products, arithmetic and copies ran while one was open for 10% of the time, Pallas kernels for 8%

profile of v5, /device:TPU:0, one launch (start us, length us, event | category | flops | bytes accessed | tf_op | source)
XLA Modules:
  0.0 60.1 jit_solution(16497045465885002415)
XLA Ops:
  0.0 0.5 collective-permute-start
  0.6 1.0 %constant_dynamic-slice_fusion.4 = bf16[256,512]{1,0:T(8,128)(2,1)S(1)} fusion(bf16[2048,512]{1,0:T(8,128)(2,1)} %bitcast.21, s32[]{:T(128)S(6)} %select_n.85), kind=kLoop, calls=%fused_computation.17 | loop fusion | bytes 524292 | tf_op jit(solution)/shard_map/dynamic_slice | solution.py:205
  1.5 2.8 %collective-permute-start.3 = (bf16[256,512]{1,0:T(8,128)(2,1)S(1)}, bf16[256,512]{1,0:T(8,128)(2,1)}, u32[]{:S(2)}, u32[]{:S(2)}) collective-permute-start(bf16[256,512]{1,0:T(8,128)(2,1)S(1)} %constant_dynamic-slice_fusion.4), channel_id=1, source_target_pairs={{0,4},{4,8},{8,12},{12,0},{28,24},{24,20},{20,16},{16,28},{1,5},{5... | collective-permute-start | bytes 786440 | tf_op jit(solution)/shard_map/ppermute | solution.py:211
  4.3 1.9 %constant_dynamic-slice_fusion.1 = (bf16[256,512]{1,0:T(8,128)(2,1)S(1)}, bf16[256,512]{1,0:T(8,128)(2,1)}, bf16[256,512]{1,0:T(8,128)(2,1)S(1)}) fusion(bf16[2048,512]{1,0:T(8,128)(2,1)} %bitcast.22, s32[]{:T(128)S(6)} %select_n.91, s32[]{:T(128)S(6)} %select_n.90, s32[]{:T(128)S(6)} %select_n.86), kind=kLoop, calls=%fused_computation.14 | loop fusion | bytes 1572876 | tf_op jit(solution)/shard_map/dynamic_slice | solution.py:205
  6.2 1.6 %collective-permute-start.5 = (bf16[256,512]{1,0:T(8,128)(2,1)}, bf16[256,512]{1,0:T(8,128)(2,1)S(1)}, u32[]{:S(2)}, u32[]{:S(2)}) collective-permute-start(bf16[256,512]{1,0:T(8,128)(2,1)} %get-tuple-element.38), channel_id=1, source_target_pairs={{0,4},{4,8},{8,12},{12,0},{28,24},{24,20},{20,16},{16,28},{1,5},{5... | collective-permute-start | bytes 786440 | tf_op jit(solution)/shard_map/ppermute | solution.py:211
  7.8 0.0 collective-permute-done.peer_ref
  7.8 0.1 convert_reduce_fusion
  7.9 1.6 %collective-permute-start.1 = (f32[32]{0:T(128)S(1)}, f32[32]{0:T(128)S(1)}, u32[]{:S(2)}, u32[]{:S(2)}) collective-permute-start(f32[32]{0:T(128)S(1)} %convert_reduce_fusion), channel_id=1, source_target_pairs={{0,2},{2,0},{1,3},{3,1},{4,6},{6,4},{5,7},{7,5},{8,10},{10,8},{9,1... | collective-permute-start | bytes 392 | tf_op jit(solution)/shard_map/ppermute | solution.py:228
  9.5 2.0 %collective-permute-done.1 = f32[32]{0:T(128)S(1)} collective-permute-done((f32[32]{0:T(128)S(1)}, f32[32]{0:T(128)S(1)}, u32[]{:S(2)}, u32[]{:S(2)}) %collective-permute-start.1) | collective-permute-done | bytes 160 | tf_op jit(solution)/shard_map/ppermute | solution.py:228
  11.5 0.1 concatenate.15
  11.7 0.7 %pad_maximum_fusion = bf16[272,512]{1,0:T(8,128)(2,1)} fusion(bf16[16,512]{1,0:T(8,128)(2,1)S(1)} %reshape.108, bf16[256,512]{1,0:T(8,128)(2,1)S(1)} %get-tuple-element.39), kind=kLoop, calls=%fused_computation | loop fusion | flops 557056 | bytes 557056 | tf_op jit(solution)/shard_map/concatenate | solution.py:237
  12.4 1.6 %collective-permute-start.2 = (bf16[272,512]{1,0:T(8,128)(2,1)}, bf16[272,512]{1,0:T(8,128)(2,1)}, u32[]{:S(2)}, u32[]{:S(2)}) collective-permute-start(bf16[272,512]{1,0:T(8,128)(2,1)} %pad_maximum_fusion), channel_id=1, source_target_pairs={{0,4},{4,8},{8,12},{12,0},{28,24},{24,20},{20,16},{16,28},{1,5},{5... | collective-permute-start | bytes 835592 | tf_op jit(solution)/shard_map/ppermute | solution.py:211
  14.0 0.0 collective-permute-done.3
  14.0 1.4 %collective-permute-start.4 = (bf16[256,512]{1,0:T(8,128)(2,1)}, bf16[256,512]{1,0:T(8,128)(2,1)}, u32[]{:S(2)}, u32[]{:S(2)}) collective-permute-start(bf16[256,512]{1,0:T(8,128)(2,1)} %collective-permute-done.3), channel_id=1, source_target_pairs={{4,20},{8,24},{24,8},{20,4},{5,21},{9,25},{25,9},{21,5},{6,22},{10... | collective-permute-start | bytes 786440 | tf_op jit(solution)/shard_map/ppermute | solution.py:257
  15.4 0.1 broadcast_and_fusion
  15.4 0.1 broadcast_in_dim.108
  15.5 0.1 broadcast_in_dim.113
  15.6 0.1 pad_add_fusion.units_ref
  15.7 3.4 %collective-permute-start.7 = (bf16[256,512]{1,0:T(8,128)(2,1)S(1)}, bf16[256,512]{1,0:T(8,128)(2,1)S(1)}, u32[]{:S(2)}, u32[]{:S(2)}) collective-permute-start(bf16[256,512]{1,0:T(8,128)(2,1)S(1)} %get-tuple-element.25), channel_id=1, source_target_pairs={{0,4},{4,8},{8,12},{12,0},{28,24},{24,20},{20,16},{16,28},{1,5},{5... | collective-permute-start | bytes 786440 | tf_op jit(solution)/shard_map/ppermute | solution.py:211
  19.1 0.0 collective-permute-start.6
  19.2 1.4 %collective-permute-start.10 = (bf16[256,512]{1,0:T(8,128)(2,1)S(1)}, bf16[256,512]{1,0:T(8,128)(2,1)}, u32[]{:S(2)}, u32[]{:S(2)}) collective-permute-start(bf16[256,512]{1,0:T(8,128)(2,1)S(1)} %collective-permute-done.5.refs_0_), channel_id=1, source_target_pairs={{4,20},{8,24},{24,8},{20,4},{5,21},{9,25},{25,9},{21,5},{6,22},{10... | collective-permute-start | bytes 786440 | tf_op jit(solution)/shard_map/ppermute | solution.py:258
  20.5 0.1 convert_element_type.39
  20.6 0.0 collective-permute-done.4
  20.6 1.4 %collective-permute-start.13 = (bf16[256,512]{1,0:T(8,128)(2,1)}, bf16[256,512]{1,0:T(8,128)(2,1)}, u32[]{:S(2)}, u32[]{:S(2)}) collective-permute-start(bf16[256,512]{1,0:T(8,128)(2,1)} %collective-permute-done.4), channel_id=1, source_target_pairs={{20,8},{24,12},{8,20},{4,16},{21,9},{25,13},{9,21},{5,17},{22,10},... | collective-permute-start | bytes 786440 | tf_op jit(solution)/shard_map/ppermute | solution.py:211
  22.0 3.2 %collective-permute-done.2 = bf16[272,512]{1,0:T(8,128)(2,1)} collective-permute-done((bf16[272,512]{1,0:T(8,128)(2,1)}, bf16[272,512]{1,0:T(8,128)(2,1)}, u32[]{:S(2)}, u32[]{:S(2)}) %collective-permute-start.2) | collective-permute-done | bytes 278560 | tf_op jit(solution)/shard_map/ppermute | solution.py:211
  25.2 0.7 %slice_bitcast_fusion.1 = bf16[2,4,8,128]{3,2,1,0:T(8,128)(2,1)S(1)} fusion(bf16[272,512]{1,0:T(8,128)(2,1)} %collective-permute-done.2), kind=kLoop, calls=%fused_computation.2 | loop fusion | bytes 32768
  25.9 1.4 %collective-permute-start.9 = (bf16[272,512]{1,0:T(8,128)(2,1)}, bf16[272,512]{1,0:T(8,128)(2,1)}, u32[]{:S(2)}, u32[]{:S(2)}) collective-permute-start(bf16[272,512]{1,0:T(8,128)(2,1)} %collective-permute-done.2), channel_id=1, source_target_pairs={{4,8},{8,12},{24,20},{20,16},{5,9},{9,13},{25,21},{21,17},{6,10},{... | collective-permute-start | bytes 835592 | tf_op jit(solution)/shard_map/ppermute | solution.py:263
  27.3 3.2 %collective-permute-done.7.refs_2_ = bf16[256,512]{1,0:T(8,128)(2,1)S(1)} collective-permute-done((bf16[256,512]{1,0:T(8,128)(2,1)S(1)}, bf16[256,512]{1,0:T(8,128)(2,1)S(1)}, u32[]{:S(2)}, u32[]{:S(2)}) %collective-permute-start.7) | collective-permute-done | bytes 262176 | tf_op jit(solution)/shard_map/ppermute | solution.py:211
  30.5 0.0 collective-permute-start.8
  30.5 0.1 dynamic-slice_convert_fusion.1
  30.6 0.1 concatenate.17.info_ref
  30.7 0.0 collective-permute-done.6.refs_1_
  30.7 0.7 %copy-done.1 = bf16[256,512]{1,0:T(8,128)(2,1)} copy-done((bf16[256,512]{1,0:T(8,128)(2,1)}, bf16[256,512]{1,0:T(8,128)(2,1)S(1)}, u32[]{:S(2)}) %copy-start.1) | copy-done | bytes 262168
  31.4 0.7 %collective-permute-start.15 = (bf16[256,512]{1,0:T(8,128)(2,1)S(1)}, bf16[256,512]{1,0:T(8,128)(2,1)S(1)}, u32[]{:S(2)}, u32[]{:S(2)}) collective-permute-start(bf16[256,512]{1,0:T(8,128)(2,1)S(1)} %collective-permute-done.7.refs_2_), channel_id=1, source_target_pairs={{4,8},{8,12},{24,20},{20,16},{5,9},{9,13},{25,21},{21,17},{6,10},{... | collective-permute-start | bytes 786440 | tf_op jit(solution)/shard_map/ppermute | solution.py:286
  32.0 0.0 collective-permute-done.10
  32.1 0.7 %collective-permute-start.11 = (bf16[256,512]{1,0:T(8,128)(2,1)}, bf16[256,512]{1,0:T(8,128)(2,1)S(1)}, u32[]{:S(2)}, u32[]{:S(2)}) collective-permute-start(bf16[256,512]{1,0:T(8,128)(2,1)} %collective-permute-done.10), channel_id=1, source_target_pairs={{20,8},{24,12},{8,20},{4,16},{21,9},{25,13},{9,21},{5,17},{22,10},... | collective-permute-start | bytes 786440 | tf_op jit(solution)/shard_map/ppermute | solution.py:211
  32.8 0.9 %copy-done.2 = bf16[256,512]{1,0:T(8,128)(2,1)S(1)} copy-done((bf16[256,512]{1,0:T(8,128)(2,1)S(1)}, bf16[256,512]{1,0:T(8,128)(2,1)}, u32[]{:S(2)}) %copy-start.2) | copy-done | bytes 262168
  33.7 4.9 %shard_map.64 = (f32[8,256]{1,0:T(8,128)S(1)}, f32[2,256]{1,0:T(2,128)S(1)}) custom-call(s32[49]{0:T(128)S(1)} %concatenate.17.info_ref, s32[2]{0:T(128)S(1)} %pad_add_fusion.units_ref, bf16[8,256,512]{2,1,0:T(8,128)(2,1)S(1)} %copy-done, bf16[8,256,512]{2,1,0:T(8,128)(2,1)} %collective-permute-done.peer_ref, ...), custom_call_target="tpu_custom_call" | custom-call | tf_op jit(solution)/shard_map/pallas_call | solution.py:141
  38.6 1.1 %collective-permute-start.12 = (f32[2,256]{1,0:T(2,128)S(1)}, f32[2,256]{1,0:T(2,128)S(1)}, u32[]{:S(2)}, u32[]{:S(2)}) collective-permute-start(f32[2,256]{1,0:T(2,128)S(1)} %get-tuple-element.30), channel_id=1, source_target_pairs={{4,0},{8,4},{12,8},{0,12},{24,28},{20,24},{16,20},{28,16},{5,1},{9... | collective-permute-start | bytes 6152 | tf_op jit(solution)/shard_map/ppermute | solution.py:294
  39.7 0.0 collective-permute-done.13
  39.7 0.6 collective-permute-start.14
  40.3 0.0 collective-permute-done.9
  40.3 0.7 %slice_bitcast_fusion = bf16[2,4,8,128]{3,2,1,0:T(8,128)(2,1)S(1)} fusion(bf16[272,512]{1,0:T(8,128)(2,1)} %collective-permute-done.9), kind=kLoop, calls=%fused_computation.1 | loop fusion | bytes 32768
  41.0 0.1 collective-permute-start.16
  41.1 0.1 dynamic-slice_convert_fusion
  41.2 0.1 concatenate.18.info_ref
  41.3 2.4 %collective-permute-done.12 = f32[2,256]{1,0:T(2,128)S(1)} collective-permute-done((f32[2,256]{1,0:T(2,128)S(1)}, f32[2,256]{1,0:T(2,128)S(1)}, u32[]{:S(2)}, u32[]{:S(2)}) %collective-permute-start.12) | collective-permute-done | bytes 2080 | tf_op jit(solution)/shard_map/ppermute | solution.py:294
  43.7 0.0 collective-permute-done.11.refs_0_
  43.7 0.0 collective-permute-done.14.refs_1_
  43.7 0.0 collective-permute-done.16.refs_3_
  43.7 1.5 %shard_map.65 = (f32[8,256]{1,0:T(8,128)S(1)}, f32[2,256]{1,0:T(2,128)S(1)}) custom-call(s32[49]{0:T(128)S(1)} %concatenate.18.info_ref, s32[2]{0:T(128)S(1)} %pad_add_fusion.units_ref, bf16[8,256,512]{2,1,0:T(8,128)(2,1)S(1)} %copy-done, bf16[8,256,512]{2,1,0:T(8,128)(2,1)} %collective-permute-done.peer_ref, ...), custom_call_target="tpu_custom_call" | custom-call | tf_op jit(solution)/shard_map/pallas_call | solution.py:141
  45.2 0.1 broadcast_select_fusion
  45.3 0.1 select_add_fusion
  45.4 0.0 collective-permute-start.17
  45.4 1.2 %collective-permute-done.17 = f32[12,256]{1,0:T(8,128)S(1)} collective-permute-done((f32[12,256]{1,0:T(8,128)S(1)}, f32[12,256]{1,0:T(8,128)S(1)}, u32[]{:S(2)}, u32[]{:S(2)}) %collective-permute-start.17) | collective-permute-done | bytes 12320 | tf_op jit(solution)/shard_map/ppermute | solution.py:313
  46.6 1.6 %collective-permute-start.18 = (f32[8,256]{1,0:T(8,128)S(1)}, f32[8,256]{1,0:T(8,128)S(1)}, u32[]{:S(2)}, u32[]{:S(2)}) collective-permute-start(f32[8,256]{1,0:T(8,128)S(1)} %slice.28), channel_id=1, source_target_pairs={{0,2},{2,0},{1,3},{3,1},{4,6},{6,4},{5,7},{7,5},{8,10},{10,8},{9,1... | collective-permute-start | bytes 24584 | tf_op jit(solution)/shard_map/ppermute | solution.py:322
  48.1 5.8 %collective-permute-start.19 = (f32[4,256]{1,0:T(4,128)S(1)}, f32[4,256]{1,0:T(4,128)S(1)}, u32[]{:S(2)}, u32[]{:S(2)}) collective-permute-start(f32[4,256]{1,0:T(4,128)S(1)} %slice.29), channel_id=1, source_target_pairs={{8,0},{10,2},{12,4},{14,6},{0,8},{2,10},{4,12},{6,14},{20,28},{22,... | collective-permute-start | bytes 12296 | tf_op jit(solution)/shard_map/ppermute | solution.py:323
  54.0 0.1 collective-permute-start.20
  54.1 0.1 broadcast_in_dim.118
  54.2 0.1 broadcast_in_dim.119
  54.3 1.3 %collective-permute-done.19 = f32[4,256]{1,0:T(4,128)S(1)} collective-permute-done((f32[4,256]{1,0:T(4,128)S(1)}, f32[4,256]{1,0:T(4,128)S(1)}, u32[]{:S(2)}, u32[]{:S(2)}) %collective-permute-start.19) | collective-permute-done | bytes 4128 | tf_op jit(solution)/shard_map/ppermute | solution.py:323
  55.6 3.8 %collective-permute-done.20 = f32[4,256]{1,0:T(4,128)S(1)} collective-permute-done((f32[4,256]{1,0:T(4,128)S(1)}, f32[4,256]{1,0:T(4,128)S(1)}, u32[]{:S(2)}, u32[]{:S(2)}) %collective-permute-start.20) | collective-permute-done | bytes 4128 | tf_op jit(solution)/shard_map/ppermute | solution.py:324
  59.4 0.0 collective-permute-done.18
  59.4 0.7 %add_log-plus-one_fusion = f32[8,256]{1,0:T(8,128)} fusion(f32[8,256]{1,0:T(8,128)S(1)} %broadcast_in_dim.122, f32[8,256]{1,0:T(8,128)S(1)} %broadcast_in_dim.124, f32[8,256]{1,0:T(8,128)S(1)} %collective-permute-done.18, pred[8]{0:T(512)(128)(4,1)S(1)} %broadcast_in_dim.119, f32[12,256]{1,0:T(8,128)S(1)} %fusion.5), kind=kLoop, calls=%fused_computation.4 | loop fusion | flops 6144 | bytes 40968 | tf_op jit(solution)/shard_map/log1p | solution.py:329
  (45 shorter events, 0.3 us)
Async XLA Ops:
  0.0 32.8 %copy-start = (bf16[8,256,512]{2,1,0:T(8,128)(2,1)S(1)}, bf16[8,256,512]{2,1,0:T(8,128)(2,1)}, u32[]{:S(2)}) copy-start(bf16[8,256,512]{2,1,0:T(8,128)(2,1)} %own_ref.3) | copy-start | bytes 6291460
  0.0 7.7 %copy-start.3 = (bf16[8,256]{1,0:T(8,128)(2,1)S(1)}, bf16[8,256]{1,0:T(8,128)(2,1)}, u32[]{:S(2)}) copy-start(bf16[8,256]{1,0:T(8,128)(2,1)} %param.7) | copy-start | bytes 12292
  0.0 7.7 %copy-start.4 = (s32[8]{0:T(128)S(1)}, s32[8]{0:T(128)}, u32[]{:S(2)}) copy-start(s32[8]{0:T(128)} %param.8) | copy-start | bytes 100
  0.0 7.8 %copy-start.7 = (s32[1,1,12,1]{2,3,1,0:T(1,128)S(1)}, s32[1,1,12,1]{2,3,1,0:T(1,128)}, u32[]{:S(2)}) copy-start(s32[1,1,12,1]{2,3,1,0:T(1,128)} %param.10) | copy-start | bytes 148
  0.0 7.8 %copy-start.6 = (s32[1,1,12]{2,1,0:T(1,128)S(1)}, s32[1,1,12]{2,1,0:T(1,128)}, u32[]{:S(2)}) copy-start(s32[1,1,12]{2,1,0:T(1,128)} %param.11) | copy-start | bytes 148
  0.0 9.5 %copy-start.5 = (s32[8]{0:T(128)S(1)}, s32[8]{0:T(128)}, u32[]{:S(2)}) copy-start(s32[8]{0:T(128)} %param.9) | copy-start | bytes 100
  0.0 7.8 %collective-permute-start = (bf16[8,256,512]{2,1,0:T(8,128)(2,1)}, bf16[8,256,512]{2,1,0:T(8,128)(2,1)}, u32[]{:S(2)}, u32[]{:S(2)}) collective-permute-start(bf16[8,256,512]{2,1,0:T(8,128)(2,1)} %own_ref.3), channel_id=1, source_target_pairs={{0,1},{1,0},{2,3},{3,2},{4,5},{5,4},{6,7},{7,6},{8,9},{9,8},{10,11... | collective-permute-start | bytes 6291464 | tf_op jit(solution)/shard_map/ppermute | solution.py:217
  1.5 12.4 %collective-permute-start.3 = (bf16[256,512]{1,0:T(8,128)(2,1)S(1)}, bf16[256,512]{1,0:T(8,128)(2,1)}, u32[]{:S(2)}, u32[]{:S(2)}) collective-permute-start(bf16[256,512]{1,0:T(8,128)(2,1)S(1)} %constant_dynamic-slice_fusion.4), channel_id=1, source_target_pairs={{0,4},{4,8},{8,12},{12,0},{28,24},{24,20},{20,16},{16,28},{1,5},{5... | collective-permute-start | bytes 786440 | tf_op jit(solution)/shard_map/ppermute | solution.py:211
  6.2 13.0 %collective-permute-start.5 = (bf16[256,512]{1,0:T(8,128)(2,1)}, bf16[256,512]{1,0:T(8,128)(2,1)S(1)}, u32[]{:S(2)}, u32[]{:S(2)}) collective-permute-start(bf16[256,512]{1,0:T(8,128)(2,1)} %get-tuple-element.38), channel_id=1, source_target_pairs={{0,4},{4,8},{8,12},{12,0},{28,24},{24,20},{20,16},{16,28},{1,5},{5... | collective-permute-start | bytes 786440 | tf_op jit(solution)/shard_map/ppermute | solution.py:211
  7.9 3.6 %collective-permute-start.1 = (f32[32]{0:T(128)S(1)}, f32[32]{0:T(128)S(1)}, u32[]{:S(2)}, u32[]{:S(2)}) collective-permute-start(f32[32]{0:T(128)S(1)} %convert_reduce_fusion), channel_id=1, source_target_pairs={{0,2},{2,0},{1,3},{3,1},{4,6},{6,4},{5,7},{7,5},{8,10},{10,8},{9,1... | collective-permute-start | bytes 392 | tf_op jit(solution)/shard_map/ppermute | solution.py:228
  12.4 12.8 %collective-permute-start.2 = (bf16[272,512]{1,0:T(8,128)(2,1)}, bf16[272,512]{1,0:T(8,128)(2,1)}, u32[]{:S(2)}, u32[]{:S(2)}) collective-permute-start(bf16[272,512]{1,0:T(8,128)(2,1)} %pad_maximum_fusion), channel_id=1, source_target_pairs={{0,4},{4,8},{8,12},{12,0},{28,24},{24,20},{20,16},{16,28},{1,5},{5... | collective-permute-start | bytes 835592 | tf_op jit(solution)/shard_map/ppermute | solution.py:211
  14.0 6.6 %collective-permute-start.4 = (bf16[256,512]{1,0:T(8,128)(2,1)}, bf16[256,512]{1,0:T(8,128)(2,1)}, u32[]{:S(2)}, u32[]{:S(2)}) collective-permute-start(bf16[256,512]{1,0:T(8,128)(2,1)} %collective-permute-done.3), channel_id=1, source_target_pairs={{4,20},{8,24},{24,8},{20,4},{5,21},{9,25},{25,9},{21,5},{6,22},{10... | collective-permute-start | bytes 786440 | tf_op jit(solution)/shard_map/ppermute | solution.py:257
  15.7 14.8 %collective-permute-start.7 = (bf16[256,512]{1,0:T(8,128)(2,1)S(1)}, bf16[256,512]{1,0:T(8,128)(2,1)S(1)}, u32[]{:S(2)}, u32[]{:S(2)}) collective-permute-start(bf16[256,512]{1,0:T(8,128)(2,1)S(1)} %get-tuple-element.25), channel_id=1, source_target_pairs={{0,4},{4,8},{8,12},{12,0},{28,24},{24,20},{20,16},{16,28},{1,5},{5... | collective-permute-start | bytes 786440 | tf_op jit(solution)/shard_map/ppermute | solution.py:211
  19.1 11.5 %collective-permute-start.6 = (bf16[256,512]{1,0:T(8,128)(2,1)}, bf16[256,512]{1,0:T(8,128)(2,1)S(1)}, u32[]{:S(2)}, u32[]{:S(2)}) collective-permute-start(bf16[256,512]{1,0:T(8,128)(2,1)} %collective-permute-done.3), channel_id=1, source_target_pairs={{0,1},{1,0},{2,3},{3,2},{4,5},{5,4},{6,7},{7,6},{8,9},{9,8},{10,11... | collective-permute-start | bytes 786440 | tf_op jit(solution)/shard_map/ppermute | solution.py:246
  19.2 12.9 %collective-permute-start.10 = (bf16[256,512]{1,0:T(8,128)(2,1)S(1)}, bf16[256,512]{1,0:T(8,128)(2,1)}, u32[]{:S(2)}, u32[]{:S(2)}) collective-permute-start(bf16[256,512]{1,0:T(8,128)(2,1)S(1)} %collective-permute-done.5.refs_0_), channel_id=1, source_target_pairs={{4,20},{8,24},{24,8},{20,4},{5,21},{9,25},{25,9},{21,5},{6,22},{10... | collective-permute-start | bytes 786440 | tf_op jit(solution)/shard_map/ppermute | solution.py:258
  20.6 19.1 %collective-permute-start.13 = (bf16[256,512]{1,0:T(8,128)(2,1)}, bf16[256,512]{1,0:T(8,128)(2,1)}, u32[]{:S(2)}, u32[]{:S(2)}) collective-permute-start(bf16[256,512]{1,0:T(8,128)(2,1)} %collective-permute-done.4), channel_id=1, source_target_pairs={{20,8},{24,12},{8,20},{4,16},{21,9},{25,13},{9,21},{5,17},{22,10},... | collective-permute-start | bytes 786440 | tf_op jit(solution)/shard_map/ppermute | solution.py:211
  25.9 14.4 %collective-permute-start.9 = (bf16[272,512]{1,0:T(8,128)(2,1)}, bf16[272,512]{1,0:T(8,128)(2,1)}, u32[]{:S(2)}, u32[]{:S(2)}) collective-permute-start(bf16[272,512]{1,0:T(8,128)(2,1)} %collective-permute-done.2), channel_id=1, source_target_pairs={{4,8},{8,12},{24,20},{20,16},{5,9},{9,13},{25,21},{21,17},{6,10},{... | collective-permute-start | bytes 835592 | tf_op jit(solution)/shard_map/ppermute | solution.py:263
  30.5 2.2 %collective-permute-start.8 = (bf16[272,512]{1,0:T(8,128)(2,1)}, bf16[272,512]{1,0:T(8,128)(2,1)S(1)}, u32[]{:S(2)}, u32[]{:S(2)}) collective-permute-start(bf16[272,512]{1,0:T(8,128)(2,1)} %collective-permute-done.2), channel_id=1, source_target_pairs={{0,1},{1,0},{2,3},{3,2},{4,5},{5,4},{6,7},{7,6},{8,9},{9,8},{10,11... | collective-permute-start | bytes 835592 | tf_op jit(solution)/shard_map/ppermute | solution.py:246
  30.7 0.7 %copy-start.1 = (bf16[256,512]{1,0:T(8,128)(2,1)}, bf16[256,512]{1,0:T(8,128)(2,1)S(1)}, u32[]{:S(2)}) copy-start(bf16[256,512]{1,0:T(8,128)(2,1)S(1)} %collective-permute-done.6.refs_1_) | copy-start | bytes 786436
  31.4 9.9 %collective-permute-start.15 = (bf16[256,512]{1,0:T(8,128)(2,1)S(1)}, bf16[256,512]{1,0:T(8,128)(2,1)S(1)}, u32[]{:S(2)}, u32[]{:S(2)}) collective-permute-start(bf16[256,512]{1,0:T(8,128)(2,1)S(1)} %collective-permute-done.7.refs_2_), channel_id=1, source_target_pairs={{4,8},{8,12},{24,20},{20,16},{5,9},{9,13},{25,21},{21,17},{6,10},{... | collective-permute-start | bytes 786440 | tf_op jit(solution)/shard_map/ppermute | solution.py:286
  32.1 11.6 %collective-permute-start.11 = (bf16[256,512]{1,0:T(8,128)(2,1)}, bf16[256,512]{1,0:T(8,128)(2,1)S(1)}, u32[]{:S(2)}, u32[]{:S(2)}) collective-permute-start(bf16[256,512]{1,0:T(8,128)(2,1)} %collective-permute-done.10), channel_id=1, source_target_pairs={{20,8},{24,12},{8,20},{4,16},{21,9},{25,13},{9,21},{5,17},{22,10},... | collective-permute-start | bytes 786440 | tf_op jit(solution)/shard_map/ppermute | solution.py:211
  32.8 1.0 %copy-start.2 = (bf16[256,512]{1,0:T(8,128)(2,1)S(1)}, bf16[256,512]{1,0:T(8,128)(2,1)}, u32[]{:S(2)}) copy-start(bf16[256,512]{1,0:T(8,128)(2,1)} %copy-done.1) | copy-start | bytes 786436
  38.6 5.1 %collective-permute-start.12 = (f32[2,256]{1,0:T(2,128)S(1)}, f32[2,256]{1,0:T(2,128)S(1)}, u32[]{:S(2)}, u32[]{:S(2)}) collective-permute-start(f32[2,256]{1,0:T(2,128)S(1)} %get-tuple-element.30), channel_id=1, source_target_pairs={{4,0},{8,4},{12,8},{0,12},{24,28},{20,24},{16,20},{28,16},{5,1},{9... | collective-permute-start | bytes 6152 | tf_op jit(solution)/shard_map/ppermute | solution.py:294
  39.7 4.0 %collective-permute-start.14 = (bf16[256,512]{1,0:T(8,128)(2,1)}, bf16[256,512]{1,0:T(8,128)(2,1)S(1)}, u32[]{:S(2)}, u32[]{:S(2)}) collective-permute-start(bf16[256,512]{1,0:T(8,128)(2,1)} %collective-permute-done.13), channel_id=1, source_target_pairs={{0,1},{1,0},{2,3},{3,2},{4,5},{5,4},{6,7},{7,6},{8,9},{9,8},{10,11... | collective-permute-start | bytes 786440 | tf_op jit(solution)/shard_map/ppermute | solution.py:246
  41.0 2.7 %collective-permute-start.16 = (bf16[272,512]{1,0:T(8,128)(2,1)}, bf16[272,512]{1,0:T(8,128)(2,1)S(1)}, u32[]{:S(2)}, u32[]{:S(2)}) collective-permute-start(bf16[272,512]{1,0:T(8,128)(2,1)} %collective-permute-done.9), channel_id=1, source_target_pairs={{0,1},{1,0},{2,3},{3,2},{4,5},{5,4},{6,7},{7,6},{8,9},{9,8},{10,11... | collective-permute-start | bytes 835592 | tf_op jit(solution)/shard_map/ppermute | solution.py:246
  45.4 1.2 %collective-permute-start.17 = (f32[12,256]{1,0:T(8,128)S(1)}, f32[12,256]{1,0:T(8,128)S(1)}, u32[]{:S(2)}, u32[]{:S(2)}) collective-permute-start(f32[12,256]{1,0:T(8,128)S(1)} %pad_maximum_fusion.1), channel_id=1, source_target_pairs={{0,1},{1,0},{2,3},{3,2},{4,5},{5,4},{6,7},{7,6},{8,9},{9,8},{10,11... | collective-permute-start | bytes 36872 | tf_op jit(solution)/shard_map/ppermute | solution.py:313
  46.6 12.8 %collective-permute-start.18 = (f32[8,256]{1,0:T(8,128)S(1)}, f32[8,256]{1,0:T(8,128)S(1)}, u32[]{:S(2)}, u32[]{:S(2)}) collective-permute-start(f32[8,256]{1,0:T(8,128)S(1)} %slice.28), channel_id=1, source_target_pairs={{0,2},{2,0},{1,3},{3,1},{4,6},{6,4},{5,7},{7,5},{8,10},{10,8},{9,1... | collective-permute-start | bytes 24584 | tf_op jit(solution)/shard_map/ppermute | solution.py:322
  48.1 7.4 %collective-permute-start.19 = (f32[4,256]{1,0:T(4,128)S(1)}, f32[4,256]{1,0:T(4,128)S(1)}, u32[]{:S(2)}, u32[]{:S(2)}) collective-permute-start(f32[4,256]{1,0:T(4,128)S(1)} %slice.29), channel_id=1, source_target_pairs={{8,0},{10,2},{12,4},{14,6},{0,8},{2,10},{4,12},{6,14},{20,28},{22,... | collective-permute-start | bytes 12296 | tf_op jit(solution)/shard_map/ppermute | solution.py:323
  54.0 5.4 %collective-permute-start.20 = (f32[4,256]{1,0:T(4,128)S(1)}, f32[4,256]{1,0:T(4,128)S(1)}, u32[]{:S(2)}, u32[]{:S(2)}) collective-permute-start(f32[4,256]{1,0:T(4,128)S(1)} %slice.29), channel_id=1, source_target_pairs={{8,2},{10,0},{12,6},{14,4},{0,10},{2,8},{4,14},{6,12},{20,30},{22,... | collective-permute-start | bytes 12296 | tf_op jit(solution)/shard_map/ppermute | solution.py:324

commit v6 on v5

--- a/solution.py
+++ b/solution.py
@@ -187,10 +187,10 @@
     def origins(step):
         return owners // 2 if 2 * step == owners else owners
 
-    def moves(step, start, stop):
+    def moves(step, start, stop, every=False):
         return [
             (place(g, o + start), place(g, o + stop))
-            for g in range(groups) for o in range(origins(step))
+            for g in range(groups) for o in range(owners if every else origins(step))
         ]
 
     def beside(at):
@@ -275,10 +275,11 @@
             active.astype(jnp.int32)[None],
         ])
         if others[0] is None:
-            others[0] = exchanged(held[0])
+            others[0] = exchanged(follow(held[0], info) if step == 1 else held[0])
         if others[1] is None:
             others[1] = exchanged(held_second[0])
-        chunks = [held[1], others[0], follow(held_second[1], others[0], others[1], info), others[1]]
+        last = held_second[1] if step == 1 else follow(held_second[1], others[0], others[1], info)
+        chunks = [held[1], others[0], last, others[1]]
         others = [None, None]
         if step < rounds:
             others[1] = exchanged(second[0])
@@ -313,20 +314,15 @@
     both = both + lax.ppermute(both, "dims", swap)
     density, outgoing = both[:blocks], both[blocks:]
     across = [(0, 1), (1, 0)]
-    joint = ("groups", "blocks", "pairs")
-    back = [
-        (place(g, o + rounds) * 2 + p, place(g, o) * 2, p)
-        for g in range(groups) for o in range(owners) for p in range(2)
-    ]
-    parts = [
-        lax.ppermute(density, "pairs", across),
-        lax.ppermute(outgoing, joint, [(s, t + p) for s, t, p in back]),
-        lax.ppermute(outgoing, joint, [(s, t + 1 - p) for s, t, p in back]),
-    ]
-    straight, crossed = parts[1].reshape(1, -1, rows), parts[2].reshape(1, -1, rows)
+    both = lax.ppermute(both, "pairs", across)
+    density = density + both[:blocks]
+    other = both[blocks:].reshape(1, -1, rows)
+    outgoing = outgoing.reshape(1, -1, rows)
     own_pair = (jnp.arange(2) == pair)[:, None, None]
-    columns = jnp.where(own_pair, straight, crossed).reshape(blocks, rows)
-    return jnp.log1p(density + parts[0] + columns)
+    columns = lax.ppermute(
+        jnp.where(own_pair, outgoing, other), line, moves(rounds, rounds, 0, True)
+    )
+    return jnp.log1p(density + columns.reshape(blocks, rows))
 
 
 def solution(mesh):

time: 61 us -> 59.1 us (0.969)
  local copies, waits for them, and re-layouts: 6.76 us -> 4.94 us
  waiting for transfers between devices: 17.1 us -> 18.6 us
  other arithmetic: 2.04 us -> 1.32 us
    unnamed x21 -> x17, local copies, waits for them, and re-layouts: 3.13 us -> 1.49 us
    ppermute x1, waiting for transfers between devices: 2.42 us -> 3.94 us  [per_device(): lax.ppermute(columns, line, [(place(g, o + step), place(g, o)) for g in r...]
    ppermute x3 -> x2, starting transfers between devices: 7.52 us -> 6.2 us  [the longest x1 4.84 us: per_device(): lax.ppermute(jnp.where(own_pair, outgoing, other), line, moves(rounds, ro...]
    ppermute x3 -> x2, waiting for transfers between devices: 5.09 us -> 4 us  [the longest x1 2.37 us: per_device(): both = lax.ppermute(both, 'pairs', across)]
    ppermute x6, waiting for transfers between devices: 6.4 us -> 7.41 us  [send(): return [lax.ppermute(array, line, to) for array in arrays]]
    concatenate x1, other arithmetic: 0.74 us -> 0.02 us  [per_device(): second[0] = jnp.concatenate([second[0], note], axis=0)]
  transfers between devices with their start and end apart: 21 -> 20, of which waited for: 7 -> 9; matrix products, arithmetic and copies ran while one was open for 10% -> 9% of each run, Pallas kernels for 8% -> 7%
where the time goes in v6:
time: 59.1 us; the launch traced here: 58.3 us
  starting transfers between devices  27.2 us (46%)
  waiting for transfers between devices  18.6 us (31%)
  Pallas kernels  6.02 us (10%)
  local copies, waits for them, and re-layouts  4.94 us (8%)
  other arithmetic  1.32 us (2%)
    ppermute x6, starting transfers between devices, send(): return [lax.ppermute(array, line, to) for array in arrays]  11.9 us
    ppermute x6, waiting for transfers between devices, send(): return [lax.ppermute(array, line, to) for array in arrays]  7.41 us
    pallas_call x2, Pallas kernels, tile_sums(): pl.pallas_call(tile_kernel, out_shape=(jax.ShapeDtypeStruct((blocks, rows...  6.02 us
    ppermute x1, starting transfers between devices, per_device(): lax.ppermute(jnp.where(own_pair, outgoing, other), line, moves(rounds, ro...  4.84 us
    ppermute x1, waiting for transfers between devices, per_device(): lax.ppermute(columns, line, [(place(g, o + step), place(g, o)) for g in r...  3.94 us
    dynamic_slice x2, local copies, waits for them, and re-layouts, quarter(): return lax.dynamic_slice_in_dim(flat, pair * share + number * unit, unit, 0)  2.85 us
    ppermute x1, waiting for transfers between devices, per_device(): both = lax.ppermute(both, 'pairs', across)  2.37 us
    ppermute x1, waiting for transfers between devices, per_device(): lax.ppermute(counted, 'pairs', [(i, (i + step) % pairs) for i in range(pa...  2.05 us
  transfers between devices with their start and end apart: 20, of which 9 were waited for; matrix products, arithmetic and copies ran while one was open for 9% of the time, Pallas kernels for 7%

profile of v6, /device:TPU:0, one launch (start us, length us, event | category | flops | bytes accessed | tf_op | source)
XLA Modules:
  0.0 58.3 jit_solution(3802481921678321306)
XLA Ops:
  0.0 0.5 collective-permute-start
  0.6 1.0 %constant_dynamic-slice_fusion.4 = bf16[256,512]{1,0:T(8,128)(2,1)S(1)} fusion(bf16[2048,512]{1,0:T(8,128)(2,1)} %bitcast.21, s32[]{:T(128)S(6)} %select_n.84), kind=kLoop, calls=%fused_computation.20 | loop fusion | bytes 524292 | tf_op jit(solution)/shard_map/dynamic_slice | solution.py:205
  1.5 2.8 %collective-permute-start.3 = (bf16[256,512]{1,0:T(8,128)(2,1)S(1)}, bf16[256,512]{1,0:T(8,128)(2,1)}, u32[]{:S(2)}, u32[]{:S(2)}) collective-permute-start(bf16[256,512]{1,0:T(8,128)(2,1)S(1)} %constant_dynamic-slice_fusion.4), channel_id=1, source_target_pairs={{0,4},{4,8},{8,12},{12,0},{28,24},{24,20},{20,16},{16,28},{1,5},{5... | collective-permute-start | bytes 786440 | tf_op jit(solution)/shard_map/ppermute | solution.py:211
  4.3 1.9 %constant_dynamic-slice_fusion.1 = (bf16[256,512]{1,0:T(8,128)(2,1)}, bf16[256,512]{1,0:T(8,128)(2,1)S(1)}, bf16[256,512]{1,0:T(8,128)(2,1)S(1)}) fusion(bf16[2048,512]{1,0:T(8,128)(2,1)} %bitcast.22, s32[]{:T(128)S(6)} %select_n.90, s32[]{:T(128)S(6)} %select_n.89, s32[]{:T(128)S(6)} %select_n.85), kind=kLoop, calls=%fused_computation.17 | loop fusion | bytes 1572876 | tf_op jit(solution)/shard_map/dynamic_slice | solution.py:205
  6.2 1.6 %collective-permute-start.5 = (bf16[256,512]{1,0:T(8,128)(2,1)S(1)}, bf16[256,512]{1,0:T(8,128)(2,1)S(1)}, u32[]{:S(2)}, u32[]{:S(2)}) collective-permute-start(bf16[256,512]{1,0:T(8,128)(2,1)S(1)} %get-tuple-element.38), channel_id=1, source_target_pairs={{0,4},{4,8},{8,12},{12,0},{28,24},{24,20},{20,16},{16,28},{1,5},{5... | collective-permute-start | bytes 786440 | tf_op jit(solution)/shard_map/ppermute | solution.py:211
  7.8 0.0 copy-done.1
  7.8 0.0 copy-done.3
  7.8 0.0 collective-permute-done.peer_ref
  7.8 0.0 copy-done.5
  7.9 0.1 convert_reduce_fusion
  8.0 1.6 %collective-permute-start.1 = (f32[32]{0:T(128)S(1)}, f32[32]{0:T(128)S(1)}, u32[]{:S(2)}, u32[]{:S(2)}) collective-permute-start(f32[32]{0:T(128)S(1)} %convert_reduce_fusion), channel_id=1, source_target_pairs={{0,2},{2,0},{1,3},{3,1},{4,6},{6,4},{5,7},{7,5},{8,10},{10,8},{9,1... | collective-permute-start | bytes 392 | tf_op jit(solution)/shard_map/ppermute | solution.py:228
  9.5 2.0 %collective-permute-done.1 = f32[32]{0:T(128)S(1)} collective-permute-done((f32[32]{0:T(128)S(1)}, f32[32]{0:T(128)S(1)}, u32[]{:S(2)}, u32[]{:S(2)}) %collective-permute-start.1) | collective-permute-done | bytes 160 | tf_op jit(solution)/shard_map/ppermute | solution.py:228
  11.6 0.1 concatenate.15
  11.7 1.6 %collective-permute-start.2 = (bf16[272,512]{1,0:T(8,128)(2,1)S(1)}, bf16[272,512]{1,0:T(8,128)(2,1)}, u32[]{:S(2)}, u32[]{:S(2)}) collective-permute-start(bf16[272,512]{1,0:T(8,128)(2,1)S(1)} %pad_maximum_fusion), channel_id=1, source_target_pairs={{0,4},{4,8},{8,12},{12,0},{28,24},{24,20},{20,16},{16,28},{1,5},{5... | collective-permute-start | bytes 835592 | tf_op jit(solution)/shard_map/ppermute | solution.py:211
  13.4 0.2 collective-permute-done.3
  13.6 1.3 %collective-permute-start.4 = (bf16[256,512]{1,0:T(8,128)(2,1)}, bf16[256,512]{1,0:T(8,128)(2,1)}, u32[]{:S(2)}, u32[]{:S(2)}) collective-permute-start(bf16[256,512]{1,0:T(8,128)(2,1)} %collective-permute-done.3), channel_id=1, source_target_pairs={{4,20},{8,24},{24,8},{20,4},{5,21},{9,25},{25,9},{21,5},{6,22},{10... | collective-permute-start | bytes 786440 | tf_op jit(solution)/shard_map/ppermute | solution.py:257
  14.9 0.1 broadcast_and_fusion
  15.0 3.2 %collective-permute-start.7 = (bf16[256,512]{1,0:T(8,128)(2,1)}, bf16[256,512]{1,0:T(8,128)(2,1)S(1)}, u32[]{:S(2)}, u32[]{:S(2)}) collective-permute-start(bf16[256,512]{1,0:T(8,128)(2,1)} %get-tuple-element.26), channel_id=1, source_target_pairs={{0,4},{4,8},{8,12},{12,0},{28,24},{24,20},{20,16},{16,28},{1,5},{5... | collective-permute-start | bytes 786440 | tf_op jit(solution)/shard_map/ppermute | solution.py:211
  18.2 0.9 %collective-permute-done.5.refs_0_ = bf16[256,512]{1,0:T(8,128)(2,1)S(1)} collective-permute-done((bf16[256,512]{1,0:T(8,128)(2,1)S(1)}, bf16[256,512]{1,0:T(8,128)(2,1)S(1)}, u32[]{:S(2)}, u32[]{:S(2)}) %collective-permute-start.5) | collective-permute-done | bytes 262176 | tf_op jit(solution)/shard_map/ppermute | solution.py:211
  19.1 1.4 %collective-permute-start.10 = (bf16[256,512]{1,0:T(8,128)(2,1)S(1)}, bf16[256,512]{1,0:T(8,128)(2,1)}, u32[]{:S(2)}, u32[]{:S(2)}) collective-permute-start(bf16[256,512]{1,0:T(8,128)(2,1)S(1)} %collective-permute-done.5.refs_0_), channel_id=1, source_target_pairs={{4,20},{8,24},{24,8},{20,4},{5,21},{9,25},{25,9},{21,5},{6,22},{10... | collective-permute-start | bytes 786440 | tf_op jit(solution)/shard_map/ppermute | solution.py:258
  20.5 0.1 convert_element_type.39
  20.6 0.0 collective-permute-done.4
  20.6 1.4 %collective-permute-start.13 = (bf16[256,512]{1,0:T(8,128)(2,1)}, bf16[256,512]{1,0:T(8,128)(2,1)}, u32[]{:S(2)}, u32[]{:S(2)}) collective-permute-start(bf16[256,512]{1,0:T(8,128)(2,1)} %collective-permute-done.4), channel_id=1, source_target_pairs={{20,8},{24,12},{8,20},{4,16},{21,9},{25,13},{9,21},{5,17},{22,10},... | collective-permute-start | bytes 786440 | tf_op jit(solution)/shard_map/ppermute | solution.py:211
  21.9 3.3 %collective-permute-done.2 = bf16[272,512]{1,0:T(8,128)(2,1)} collective-permute-done((bf16[272,512]{1,0:T(8,128)(2,1)S(1)}, bf16[272,512]{1,0:T(8,128)(2,1)}, u32[]{:S(2)}, u32[]{:S(2)}) %collective-permute-start.2) | collective-permute-done | bytes 278560 | tf_op jit(solution)/shard_map/ppermute | solution.py:211
  25.2 0.7 %slice_bitcast_fusion.1 = bf16[2,4,8,128]{3,2,1,0:T(8,128)(2,1)S(1)} fusion(bf16[272,512]{1,0:T(8,128)(2,1)} %collective-permute-done.2), kind=kLoop, calls=%fused_computation.2 | loop fusion | bytes 32768
  26.0 0.1 dynamic-slice_convert_fusion.1
  26.0 0.1 concatenate.17.info_ref
  26.1 0.0 collective-permute-start.6
  26.1 1.4 %collective-permute-start.9 = (bf16[272,512]{1,0:T(8,128)(2,1)}, bf16[272,512]{1,0:T(8,128)(2,1)}, u32[]{:S(2)}, u32[]{:S(2)}) collective-permute-start(bf16[272,512]{1,0:T(8,128)(2,1)} %collective-permute-done.2), channel_id=1, source_target_pairs={{4,8},{8,12},{24,20},{20,16},{5,9},{9,13},{25,21},{21,17},{6,10},{... | collective-permute-start | bytes 835592 | tf_op jit(solution)/shard_map/ppermute | solution.py:263
  27.5 3.0 %collective-permute-done.7.refs_2_ = bf16[256,512]{1,0:T(8,128)(2,1)S(1)} collective-permute-done((bf16[256,512]{1,0:T(8,128)(2,1)}, bf16[256,512]{1,0:T(8,128)(2,1)S(1)}, u32[]{:S(2)}, u32[]{:S(2)}) %collective-permute-start.7) | collective-permute-done | bytes 262176 | tf_op jit(solution)/shard_map/ppermute | solution.py:211
  30.5 0.0 collective-permute-start.8
  30.5 0.1 pad_add_fusion.units_ref
  30.6 0.1 broadcast_in_dim.100
  30.7 0.1 broadcast_in_dim.105
  30.8 0.0 collective-permute-done.10
  30.8 0.7 %collective-permute-start.15 = (bf16[256,512]{1,0:T(8,128)(2,1)S(1)}, bf16[256,512]{1,0:T(8,128)(2,1)S(1)}, u32[]{:S(2)}, u32[]{:S(2)}) collective-permute-start(bf16[256,512]{1,0:T(8,128)(2,1)S(1)} %collective-permute-done.7.refs_2_), channel_id=1, source_target_pairs={{4,8},{8,12},{24,20},{20,16},{5,9},{9,13},{25,21},{21,17},{6,10},{... | collective-permute-start | bytes 786440 | tf_op jit(solution)/shard_map/ppermute | solution.py:287
  31.5 0.0 collective-permute-done.6.refs_1_
  31.5 1.4 %collective-permute-start.11 = (bf16[256,512]{1,0:T(8,128)(2,1)}, bf16[256,512]{1,0:T(8,128)(2,1)}, u32[]{:S(2)}, u32[]{:S(2)}) collective-permute-start(bf16[256,512]{1,0:T(8,128)(2,1)} %collective-permute-done.10), channel_id=1, source_target_pairs={{20,8},{24,12},{8,20},{4,16},{21,9},{25,13},{9,21},{5,17},{22,10},... | collective-permute-start | bytes 786440 | tf_op jit(solution)/shard_map/ppermute | solution.py:211
  32.9 0.0 collective-permute-done.8.refs_3_
  32.9 3.8 %shard_map.64 = (f32[8,256]{1,0:T(8,128)S(1)}, f32[2,256]{1,0:T(2,128)S(1)}) custom-call(s32[49]{0:T(128)S(1)} %concatenate.17.info_ref, s32[2]{0:T(128)S(1)} %pad_add_fusion.units_ref, bf16[8,256,512]{2,1,0:T(8,128)(2,1)S(1)} %copy-done, bf16[8,256,512]{2,1,0:T(8,128)(2,1)} %collective-permute-done.peer_ref, ...), custom_call_target="tpu_custom_call" | custom-call | tf_op jit(solution)/shard_map/pallas_call | solution.py:141
  36.7 1.5 %collective-permute-start.12 = (f32[2,256]{1,0:T(2,128)S(1)}, f32[2,256]{1,0:T(2,128)S(1)}, u32[]{:S(2)}, u32[]{:S(2)}) collective-permute-start(f32[2,256]{1,0:T(2,128)S(1)} %get-tuple-element.30), channel_id=1, source_target_pairs={{4,0},{8,4},{12,8},{0,12},{24,28},{20,24},{16,20},{28,16},{5,1},{9... | collective-permute-start | bytes 6152 | tf_op jit(solution)/shard_map/ppermute | solution.py:295
  38.2 0.0 collective-permute-done.13
  38.2 0.7 %collective-permute-start.14 = (bf16[256,512]{1,0:T(8,128)(2,1)}, bf16[256,512]{1,0:T(8,128)(2,1)S(1)}, u32[]{:S(2)}, u32[]{:S(2)}) collective-permute-start(bf16[256,512]{1,0:T(8,128)(2,1)} %collective-permute-done.13), channel_id=1, source_target_pairs={{0,1},{1,0},{2,3},{3,2},{4,5},{5,4},{6,7},{7,6},{8,9},{9,8},{10,11... | collective-permute-start | bytes 786440 | tf_op jit(solution)/shard_map/ppermute | solution.py:246
  38.8 0.0 collective-permute-done.9
  38.8 0.7 %slice_bitcast_fusion = bf16[2,4,8,128]{3,2,1,0:T(8,128)(2,1)S(1)} fusion(bf16[272,512]{1,0:T(8,128)(2,1)} %collective-permute-done.9), kind=kLoop, calls=%fused_computation.1 | loop fusion | bytes 32768
  39.6 0.1 collective-permute-start.16
  39.6 0.1 dynamic-slice_convert_fusion
  39.7 0.1 concatenate.18.info_ref
  39.8 0.0 collective-permute-done.15.refs_2_
  39.8 3.9 %collective-permute-done.12 = f32[2,256]{1,0:T(2,128)S(1)} collective-permute-done((f32[2,256]{1,0:T(2,128)S(1)}, f32[2,256]{1,0:T(2,128)S(1)}, u32[]{:S(2)}, u32[]{:S(2)}) %collective-permute-start.12) | collective-permute-done | bytes 2080 | tf_op jit(solution)/shard_map/ppermute | solution.py:295
  43.8 0.0 collective-permute-done.11.refs_0_
  43.8 0.0 collective-permute-done.14.refs_1_
  43.8 0.0 collective-permute-done.16.refs_3_
  43.8 2.2 %shard_map.65 = (f32[8,256]{1,0:T(8,128)S(1)}, f32[2,256]{1,0:T(2,128)S(1)}) custom-call(s32[49]{0:T(128)S(1)} %concatenate.18.info_ref, s32[2]{0:T(128)S(1)} %pad_add_fusion.units_ref, bf16[8,256,512]{2,1,0:T(8,128)(2,1)S(1)} %copy-done, bf16[8,256,512]{2,1,0:T(8,128)(2,1)} %collective-permute-done.peer_ref, ...), custom_call_target="tpu_custom_call" | custom-call | tf_op jit(solution)/shard_map/pallas_call | solution.py:141
  46.0 0.1 broadcast_select_fusion.1
  46.1 0.1 select_add_fusion
  46.2 0.0 collective-permute-start.17
  46.2 1.2 %collective-permute-done.17 = f32[12,256]{1,0:T(8,128)S(1)} collective-permute-done((f32[12,256]{1,0:T(8,128)S(1)}, f32[12,256]{1,0:T(8,128)S(1)}, u32[]{:S(2)}, u32[]{:S(2)}) %collective-permute-start.17) | collective-permute-done | bytes 12320 | tf_op jit(solution)/shard_map/ppermute | solution.py:314
  47.4 1.4 %collective-permute-start.18 = (f32[12,256]{1,0:T(8,128)S(1)}, f32[12,256]{1,0:T(8,128)S(1)}, u32[]{:S(2)}, u32[]{:S(2)}) collective-permute-start(f32[12,256]{1,0:T(8,128)S(1)} %fusion.7), channel_id=1, source_target_pairs={{0,2},{2,0},{1,3},{3,1},{4,6},{6,4},{5,7},{7,5},{8,10},{10,8},{9,1... | collective-permute-start | bytes 36872 | tf_op jit(solution)/shard_map/ppermute | solution.py:317
  48.8 2.4 %collective-permute-done.18 = f32[12,256]{1,0:T(8,128)S(1)} collective-permute-done((f32[12,256]{1,0:T(8,128)S(1)}, f32[12,256]{1,0:T(8,128)S(1)}, u32[]{:S(2)}, u32[]{:S(2)}) %collective-permute-start.18) | collective-permute-done | bytes 12320 | tf_op jit(solution)/shard_map/ppermute | solution.py:317
  51.1 0.1 broadcast_select_fusion
  51.2 4.8 %collective-permute-start.19 = (f32[2,4,256]{2,1,0:T(4,128)S(1)}, f32[2,4,256]{2,1,0:T(4,128)S(1)}, u32[]{:S(2)}, u32[]{:S(2)}) collective-permute-start(f32[2,4,256]{2,1,0:T(4,128)S(1)} %broadcast_select_fusion), channel_id=1, source_target_pairs={{8,0},{12,4},{0,8},{4,12},{20,28},{16,24},{28,20},{24,16},{9,1},{1... | collective-permute-start | bytes 24584 | tf_op jit(solution)/shard_map/ppermute | solution.py:322
  56.0 1.6 %collective-permute-done.19 = f32[2,4,256]{2,1,0:T(4,128)S(1)} collective-permute-done((f32[2,4,256]{2,1,0:T(4,128)S(1)}, f32[2,4,256]{2,1,0:T(4,128)S(1)}, u32[]{:S(2)}, u32[]{:S(2)}) %collective-permute-start.19) | collective-permute-done | bytes 8224 | tf_op jit(solution)/shard_map/ppermute | solution.py:322
  57.7 0.6 %fusion.1 = f32[8,256]{1,0:T(8,128)} fusion(f32[8,256]{1,0:T(8,128)S(1)} %reshape.110, f32[12,256]{1,0:T(8,128)S(1)} %collective-permute-done.18, f32[12,256]{1,0:T(8,128)S(1)} %fusion.7), kind=kLoop, calls=%fused_computation.6 | loop fusion | flops 4096 | bytes 32768 | tf_op jit(solution)/shard_map/log1p | solution.py:325
  (35 shorter events, 0.2 us)
Async XLA Ops:
  0.0 32.9 %copy-start = (bf16[8,256,512]{2,1,0:T(8,128)(2,1)S(1)}, bf16[8,256,512]{2,1,0:T(8,128)(2,1)}, u32[]{:S(2)}) copy-start(bf16[8,256,512]{2,1,0:T(8,128)(2,1)} %own_ref.3) | copy-start | bytes 6291460
  0.0 7.8 %copy-start.1 = (bf16[8,256]{1,0:T(8,128)(2,1)S(1)}, bf16[8,256]{1,0:T(8,128)(2,1)}, u32[]{:S(2)}) copy-start(bf16[8,256]{1,0:T(8,128)(2,1)} %param.7) | copy-start | bytes 12292
  0.0 7.8 %copy-start.2 = (s32[8]{0:T(128)S(1)}, s32[8]{0:T(128)}, u32[]{:S(2)}) copy-start(s32[8]{0:T(128)} %param.8) | copy-start | bytes 100
  0.0 7.8 %copy-start.3 = (s32[8]{0:T(128)S(1)}, s32[8]{0:T(128)}, u32[]{:S(2)}) copy-start(s32[8]{0:T(128)} %param.9) | copy-start | bytes 100
  0.0 7.8 %copy-start.5 = (s32[1,1,12,1]{2,3,1,0:T(1,128)S(1)}, s32[1,1,12,1]{2,3,1,0:T(1,128)}, u32[]{:S(2)}) copy-start(s32[1,1,12,1]{2,3,1,0:T(1,128)} %param.10) | copy-start | bytes 148
  0.0 7.8 %copy-start.4 = (s32[1,1,12]{2,1,0:T(1,128)S(1)}, s32[1,1,12]{2,1,0:T(1,128)}, u32[]{:S(2)}) copy-start(s32[1,1,12]{2,1,0:T(1,128)} %param.11) | copy-start | bytes 148
  0.0 7.8 %collective-permute-start = (bf16[8,256,512]{2,1,0:T(8,128)(2,1)}, bf16[8,256,512]{2,1,0:T(8,128)(2,1)}, u32[]{:S(2)}, u32[]{:S(2)}) collective-permute-start(bf16[8,256,512]{2,1,0:T(8,128)(2,1)} %own_ref.3), channel_id=1, source_target_pairs={{0,1},{1,0},{2,3},{3,2},{4,5},{5,4},{6,7},{7,6},{8,9},{9,8},{10,11... | collective-permute-start | bytes 6291464 | tf_op jit(solution)/shard_map/ppermute | solution.py:217
  1.5 12.1 %collective-permute-start.3 = (bf16[256,512]{1,0:T(8,128)(2,1)S(1)}, bf16[256,512]{1,0:T(8,128)(2,1)}, u32[]{:S(2)}, u32[]{:S(2)}) collective-permute-start(bf16[256,512]{1,0:T(8,128)(2,1)S(1)} %constant_dynamic-slice_fusion.4), channel_id=1, source_target_pairs={{0,4},{4,8},{8,12},{12,0},{28,24},{24,20},{20,16},{16,28},{1,5},{5... | collective-permute-start | bytes 786440 | tf_op jit(solution)/shard_map/ppermute | solution.py:211
  6.2 12.9 %collective-permute-start.5 = (bf16[256,512]{1,0:T(8,128)(2,1)S(1)}, bf16[256,512]{1,0:T(8,128)(2,1)S(1)}, u32[]{:S(2)}, u32[]{:S(2)}) collective-permute-start(bf16[256,512]{1,0:T(8,128)(2,1)S(1)} %get-tuple-element.38), channel_id=1, source_target_pairs={{0,4},{4,8},{8,12},{12,0},{28,24},{24,20},{20,16},{16,28},{1,5},{5... | collective-permute-start | bytes 786440 | tf_op jit(solution)/shard_map/ppermute | solution.py:211
  8.0 3.6 %collective-permute-start.1 = (f32[32]{0:T(128)S(1)}, f32[32]{0:T(128)S(1)}, u32[]{:S(2)}, u32[]{:S(2)}) collective-permute-start(f32[32]{0:T(128)S(1)} %convert_reduce_fusion), channel_id=1, source_target_pairs={{0,2},{2,0},{1,3},{3,1},{4,6},{6,4},{5,7},{7,5},{8,10},{10,8},{9,1... | collective-permute-start | bytes 392 | tf_op jit(solution)/shard_map/ppermute | solution.py:228
  11.7 13.5 %collective-permute-start.2 = (bf16[272,512]{1,0:T(8,128)(2,1)S(1)}, bf16[272,512]{1,0:T(8,128)(2,1)}, u32[]{:S(2)}, u32[]{:S(2)}) collective-permute-start(bf16[272,512]{1,0:T(8,128)(2,1)S(1)} %pad_maximum_fusion), channel_id=1, source_target_pairs={{0,4},{4,8},{8,12},{12,0},{28,24},{24,20},{20,16},{16,28},{1,5},{5... | collective-permute-start | bytes 835592 | tf_op jit(solution)/shard_map/ppermute | solution.py:211
  13.6 7.0 %collective-permute-start.4 = (bf16[256,512]{1,0:T(8,128)(2,1)}, bf16[256,512]{1,0:T(8,128)(2,1)}, u32[]{:S(2)}, u32[]{:S(2)}) collective-permute-start(bf16[256,512]{1,0:T(8,128)(2,1)} %collective-permute-done.3), channel_id=1, source_target_pairs={{4,20},{8,24},{24,8},{20,4},{5,21},{9,25},{25,9},{21,5},{6,22},{10... | collective-permute-start | bytes 786440 | tf_op jit(solution)/shard_map/ppermute | solution.py:257
  15.0 15.5 %collective-permute-start.7 = (bf16[256,512]{1,0:T(8,128)(2,1)}, bf16[256,512]{1,0:T(8,128)(2,1)S(1)}, u32[]{:S(2)}, u32[]{:S(2)}) collective-permute-start(bf16[256,512]{1,0:T(8,128)(2,1)} %get-tuple-element.26), channel_id=1, source_target_pairs={{0,4},{4,8},{8,12},{12,0},{28,24},{24,20},{20,16},{16,28},{1,5},{5... | collective-permute-start | bytes 786440 | tf_op jit(solution)/shard_map/ppermute | solution.py:211
  19.1 11.7 %collective-permute-start.10 = (bf16[256,512]{1,0:T(8,128)(2,1)S(1)}, bf16[256,512]{1,0:T(8,128)(2,1)}, u32[]{:S(2)}, u32[]{:S(2)}) collective-permute-start(bf16[256,512]{1,0:T(8,128)(2,1)S(1)} %collective-permute-done.5.refs_0_), channel_id=1, source_target_pairs={{4,20},{8,24},{24,8},{20,4},{5,21},{9,25},{25,9},{21,5},{6,22},{10... | collective-permute-start | bytes 786440 | tf_op jit(solution)/shard_map/ppermute | solution.py:258
  20.6 17.6 %collective-permute-start.13 = (bf16[256,512]{1,0:T(8,128)(2,1)}, bf16[256,512]{1,0:T(8,128)(2,1)}, u32[]{:S(2)}, u32[]{:S(2)}) collective-permute-start(bf16[256,512]{1,0:T(8,128)(2,1)} %collective-permute-done.4), channel_id=1, source_target_pairs={{20,8},{24,12},{8,20},{4,16},{21,9},{25,13},{9,21},{5,17},{22,10},... | collective-permute-start | bytes 786440 | tf_op jit(solution)/shard_map/ppermute | solution.py:211
  26.1 5.3 %collective-permute-start.6 = (bf16[256,512]{1,0:T(8,128)(2,1)}, bf16[256,512]{1,0:T(8,128)(2,1)S(1)}, u32[]{:S(2)}, u32[]{:S(2)}) collective-permute-start(bf16[256,512]{1,0:T(8,128)(2,1)} %collective-permute-done.3), channel_id=1, source_target_pairs={{0,1},{1,0},{2,3},{3,2},{4,5},{5,4},{6,7},{7,6},{8,9},{9,8},{10,11... | collective-permute-start | bytes 786440 | tf_op jit(solution)/shard_map/ppermute | solution.py:246
  26.1 12.7 %collective-permute-start.9 = (bf16[272,512]{1,0:T(8,128)(2,1)}, bf16[272,512]{1,0:T(8,128)(2,1)}, u32[]{:S(2)}, u32[]{:S(2)}) collective-permute-start(bf16[272,512]{1,0:T(8,128)(2,1)} %collective-permute-done.2), channel_id=1, source_target_pairs={{4,8},{8,12},{24,20},{20,16},{5,9},{9,13},{25,21},{21,17},{6,10},{... | collective-permute-start | bytes 835592 | tf_op jit(solution)/shard_map/ppermute | solution.py:263
  30.5 2.4 %collective-permute-start.8 = (bf16[272,512]{1,0:T(8,128)(2,1)}, bf16[272,512]{1,0:T(8,128)(2,1)S(1)}, u32[]{:S(2)}, u32[]{:S(2)}) collective-permute-start(bf16[272,512]{1,0:T(8,128)(2,1)} %collective-permute-done.2), channel_id=1, source_target_pairs={{0,1},{1,0},{2,3},{3,2},{4,5},{5,4},{6,7},{7,6},{8,9},{9,8},{10,11... | collective-permute-start | bytes 835592 | tf_op jit(solution)/shard_map/ppermute | solution.py:246
  30.8 9.0 %collective-permute-start.15 = (bf16[256,512]{1,0:T(8,128)(2,1)S(1)}, bf16[256,512]{1,0:T(8,128)(2,1)S(1)}, u32[]{:S(2)}, u32[]{:S(2)}) collective-permute-start(bf16[256,512]{1,0:T(8,128)(2,1)S(1)} %collective-permute-done.7.refs_2_), channel_id=1, source_target_pairs={{4,8},{8,12},{24,20},{20,16},{5,9},{9,13},{25,21},{21,17},{6,10},{... | collective-permute-start | bytes 786440 | tf_op jit(solution)/shard_map/ppermute | solution.py:287
  31.5 12.3 %collective-permute-start.11 = (bf16[256,512]{1,0:T(8,128)(2,1)}, bf16[256,512]{1,0:T(8,128)(2,1)}, u32[]{:S(2)}, u32[]{:S(2)}) collective-permute-start(bf16[256,512]{1,0:T(8,128)(2,1)} %collective-permute-done.10), channel_id=1, source_target_pairs={{20,8},{24,12},{8,20},{4,16},{21,9},{25,13},{9,21},{5,17},{22,10},... | collective-permute-start | bytes 786440 | tf_op jit(solution)/shard_map/ppermute | solution.py:211
  36.7 7.1 %collective-permute-start.12 = (f32[2,256]{1,0:T(2,128)S(1)}, f32[2,256]{1,0:T(2,128)S(1)}, u32[]{:S(2)}, u32[]{:S(2)}) collective-permute-start(f32[2,256]{1,0:T(2,128)S(1)} %get-tuple-element.30), channel_id=1, source_target_pairs={{4,0},{8,4},{12,8},{0,12},{24,28},{20,24},{16,20},{28,16},{5,1},{9... | collective-permute-start | bytes 6152 | tf_op jit(solution)/shard_map/ppermute | solution.py:295
  38.2 5.6 %collective-permute-start.14 = (bf16[256,512]{1,0:T(8,128)(2,1)}, bf16[256,512]{1,0:T(8,128)(2,1)S(1)}, u32[]{:S(2)}, u32[]{:S(2)}) collective-permute-start(bf16[256,512]{1,0:T(8,128)(2,1)} %collective-permute-done.13), channel_id=1, source_target_pairs={{0,1},{1,0},{2,3},{3,2},{4,5},{5,4},{6,7},{7,6},{8,9},{9,8},{10,11... | collective-permute-start | bytes 786440 | tf_op jit(solution)/shard_map/ppermute | solution.py:246
  39.6 4.2 %collective-permute-start.16 = (bf16[272,512]{1,0:T(8,128)(2,1)}, bf16[272,512]{1,0:T(8,128)(2,1)S(1)}, u32[]{:S(2)}, u32[]{:S(2)}) collective-permute-start(bf16[272,512]{1,0:T(8,128)(2,1)} %collective-permute-done.9), channel_id=1, source_target_pairs={{0,1},{1,0},{2,3},{3,2},{4,5},{5,4},{6,7},{7,6},{8,9},{9,8},{10,11... | collective-permute-start | bytes 835592 | tf_op jit(solution)/shard_map/ppermute | solution.py:246
  46.2 1.2 %collective-permute-start.17 = (f32[12,256]{1,0:T(8,128)S(1)}, f32[12,256]{1,0:T(8,128)S(1)}, u32[]{:S(2)}, u32[]{:S(2)}) collective-permute-start(f32[12,256]{1,0:T(8,128)S(1)} %pad_maximum_fusion.1), channel_id=1, source_target_pairs={{0,1},{1,0},{2,3},{3,2},{4,5},{5,4},{6,7},{7,6},{8,9},{9,8},{10,11... | collective-permute-start | bytes 36872 | tf_op jit(solution)/shard_map/ppermute | solution.py:314
  47.4 3.7 %collective-permute-start.18 = (f32[12,256]{1,0:T(8,128)S(1)}, f32[12,256]{1,0:T(8,128)S(1)}, u32[]{:S(2)}, u32[]{:S(2)}) collective-permute-start(f32[12,256]{1,0:T(8,128)S(1)} %fusion.7), channel_id=1, source_target_pairs={{0,2},{2,0},{1,3},{3,1},{4,6},{6,4},{5,7},{7,5},{8,10},{10,8},{9,1... | collective-permute-start | bytes 36872 | tf_op jit(solution)/shard_map/ppermute | solution.py:317
  51.2 6.5 %collective-permute-start.19 = (f32[2,4,256]{2,1,0:T(4,128)S(1)}, f32[2,4,256]{2,1,0:T(4,128)S(1)}, u32[]{:S(2)}, u32[]{:S(2)}) collective-permute-start(f32[2,4,256]{2,1,0:T(4,128)S(1)} %broadcast_select_fusion), channel_id=1, source_target_pairs={{8,0},{12,4},{0,8},{4,12},{20,28},{16,24},{28,20},{24,16},{9,1},{1... | collective-permute-start | bytes 24584 | tf_op jit(solution)/shard_map/ppermute | solution.py:322

commit v7 on v6

--- a/solution.py
+++ b/solution.py
@@ -34,9 +34,10 @@
         )
         for i, part in enumerate(parts)
     ]
-    part_copies.append(pltpu.make_async_copy(
+    note_copy = pltpu.make_async_copy(
         parts[-1].at[pl.ds(unit, note_rows)], raw_ref, part_copied.at[count]
-    ))
+    )
+    note_copy.start()
     for copy in part_copies:
         copy.start()
     valid, weights = [], []
@@ -63,8 +64,7 @@
 
     rows_ref[...] = jnp.zeros_like(rows_ref)
     total_ref[...] = jnp.zeros_like(total_ref)
-    for copy in part_copies:
-        copy.wait()
+    note_copy.wait()
     note_ref[...] = raw_ref[...].astype(jnp.float32)
     in_row = width // unit
     for segment in range(segments):
@@ -76,11 +76,13 @@
         wide_ref[0, segment] = jnp.transpose(jnp.broadcast_to(part_scale, (LANES, unit)))
         row_ids = lax.broadcasted_iota(jnp.int32, (unit, LANES), 0)
         wide_ref[1, segment] = (row_ids < valid[segment]).astype(jnp.float32)
-
-    def product(block, first, length):
+    for copy in part_copies:
+        copy.wait()
+
+    def product(block, first, length, used):
         return sum(
             lax.dot_general(
-                part_ref[half, first : first + length, :], held_ref[block, half], NT,
+                part_ref[half, first : first + length, :], held_ref[block, half, :used, :], NT,
                 preferred_element_type=jnp.float32,
             )
             for half in range(2)
@@ -89,7 +91,7 @@
     def tile(segment, block, gram):
         factor = weights[segment][block].astype(jnp.float32)
         row_ids = lax.broadcasted_iota(jnp.int32, (1, LANES), 1)
-        for start in range(0, rows, LANES):
+        for start in range(0, gram.shape[1], LANES):
             own_scale = scale_ref[block : block + 1, start : start + LANES] * LOG2E
             own_valid = jnp.where(row_ids + start < info_ref[blocks + block], factor, 0.0)
             summed = jnp.zeros((8, LANES), jnp.float32)
@@ -113,18 +115,20 @@
                 copy.wait()
             wanted = [weights[segment][block] != 0 for segment in range(segments)]
             every = functools.reduce(jnp.logical_and, wanted)
-
-            @pl.when(every)
-            def _():
-                gram = product(block, 0, segments * unit)
+            few = info_ref[blocks + block] <= rows // 2
+            for used, fits in ((rows // 2, few), (rows, jnp.logical_not(few))):
+
+                @pl.when(every & fits)
+                def _(used=used):
+                    gram = product(block, 0, segments * unit, used)
+                    for segment in range(segments):
+                        tile(segment, block, gram[segment * unit : (segment + 1) * unit])
+
                 for segment in range(segments):
-                    tile(segment, block, gram[segment * unit : (segment + 1) * unit])
-
-            for segment in range(segments):
-
-                @pl.when(wanted[segment] & jnp.logical_not(every))
-                def _(segment=segment):
-                    tile(segment, block, product(block, segment * unit, unit))
+
+                    @pl.when(wanted[segment] & jnp.logical_not(every) & fits)
+                    def _(segment=segment, used=used):
+                        tile(segment, block, product(block, segment * unit, unit, used))
 
     for segment in range(segments):
         columns_ref[segment : segment + 1, :] = jnp.sum(

time: 59.1 us -> 58.4 us (0.988)
  starting transfers between devices: 27.2 us -> 28.5 us
  Pallas kernels: 6.02 us -> 5.13 us
  waiting for transfers between devices: 18.6 us -> 18 us
    ppermute x1, starting transfers between devices: 1.47 us -> 2.56 us  [per_device(): lax.ppermute(columns, line, [(place(g, o + step), place(g, o)) for g in r...]
    pallas_call x2, Pallas kernels: 6.02 us -> 5.13 us  [tile_sums(): pl.pallas_call(tile_kernel, out_shape=(jax.ShapeDtypeStruct((blocks, rows...]
  transfers between devices with their start and end apart: 20 -> 20, of which waited for: 9 -> 9; matrix products, arithmetic and copies ran while one was open for 9% -> 9% of each run, Pallas kernels for 7% -> 6%
where the time goes in v7:
time: 58.4 us; the launch traced here: 58.1 us
  starting transfers between devices  28.5 us (49%)
  waiting for transfers between devices  18 us (31%)
  Pallas kernels  5.13 us (9%)
  local copies, waits for them, and re-layouts  4.94 us (8%)
  other arithmetic  1.32 us (2%)
    ppermute x6, starting transfers between devices, send(): return [lax.ppermute(array, line, to) for array in arrays]  11.9 us
    ppermute x6, waiting for transfers between devices, send(): return [lax.ppermute(array, line, to) for array in arrays]  7.41 us
    pallas_call x2, Pallas kernels, tile_sums(): pl.pallas_call(tile_kernel, out_shape=(jax.ShapeDtypeStruct((blocks, rows...  5.13 us
    ppermute x1, starting transfers between devices, per_device(): lax.ppermute(jnp.where(own_pair, outgoing, other), line, moves(rounds, ro...  5.1 us
    ppermute x1, waiting for transfers between devices, per_device(): lax.ppermute(columns, line, [(place(g, o + step), place(g, o)) for g in r...  3.43 us
    dynamic_slice x2, local copies, waits for them, and re-layouts, quarter(): return lax.dynamic_slice_in_dim(flat, pair * share + number * unit, unit, 0)  2.85 us
    ppermute x1, starting transfers between devices, per_device(): lax.ppermute(columns, line, [(place(g, o + step), place(g, o)) for g in r...  2.56 us
    ppermute x1, waiting for transfers between devices, per_device(): both = lax.ppermute(both, 'pairs', across)  2.25 us
  transfers between devices with their start and end apart: 20, of which 9 were waited for; matrix products, arithmetic and copies ran while one was open for 9% of the time, Pallas kernels for 6%

profile of v7, /device:TPU:0, one launch (start us, length us, event | category | flops | bytes accessed | tf_op | source)
XLA Modules:
  0.0 58.1 jit_solution(15073817354326185595)
XLA Ops:
  0.0 0.0 copy-start.4
  0.0 0.5 collective-permute-start
  0.6 1.0 %constant_dynamic-slice_fusion.4 = bf16[256,512]{1,0:T(8,128)(2,1)S(1)} fusion(bf16[2048,512]{1,0:T(8,128)(2,1)} %bitcast.21, s32[]{:T(128)S(6)} %select_n.84), kind=kLoop, calls=%fused_computation.20 | loop fusion | bytes 524292 | tf_op jit(solution)/shard_map/dynamic_slice | solution.py:209
  1.5 2.8 %collective-permute-start.3 = (bf16[256,512]{1,0:T(8,128)(2,1)S(1)}, bf16[256,512]{1,0:T(8,128)(2,1)}, u32[]{:S(2)}, u32[]{:S(2)}) collective-permute-start(bf16[256,512]{1,0:T(8,128)(2,1)S(1)} %constant_dynamic-slice_fusion.4), channel_id=1, source_target_pairs={{0,4},{4,8},{8,12},{12,0},{28,24},{24,20},{20,16},{16,28},{1,5},{5... | collective-permute-start | bytes 786440 | tf_op jit(solution)/shard_map/ppermute | solution.py:215
  4.3 1.9 %constant_dynamic-slice_fusion.1 = (bf16[256,512]{1,0:T(8,128)(2,1)}, bf16[256,512]{1,0:T(8,128)(2,1)S(1)}, bf16[256,512]{1,0:T(8,128)(2,1)S(1)}) fusion(bf16[2048,512]{1,0:T(8,128)(2,1)} %bitcast.22, s32[]{:T(128)S(6)} %select_n.90, s32[]{:T(128)S(6)} %select_n.89, s32[]{:T(128)S(6)} %select_n.85), kind=kLoop, calls=%fused_computation.17 | loop fusion | bytes 1572876 | tf_op jit(solution)/shard_map/dynamic_slice | solution.py:209
  6.2 1.6 %collective-permute-start.5 = (bf16[256,512]{1,0:T(8,128)(2,1)S(1)}, bf16[256,512]{1,0:T(8,128)(2,1)S(1)}, u32[]{:S(2)}, u32[]{:S(2)}) collective-permute-start(bf16[256,512]{1,0:T(8,128)(2,1)S(1)} %get-tuple-element.38), channel_id=1, source_target_pairs={{0,4},{4,8},{8,12},{12,0},{28,24},{24,20},{20,16},{16,28},{1,5},{5... | collective-permute-start | bytes 786440 | tf_op jit(solution)/shard_map/ppermute | solution.py:215
  7.8 0.0 copy-done.1
  7.8 0.0 copy-done.2
  7.8 0.0 collective-permute-done.peer_ref
  7.9 0.1 convert_reduce_fusion
  8.0 1.6 %collective-permute-start.1 = (f32[32]{0:T(128)S(1)}, f32[32]{0:T(128)S(1)}, u32[]{:S(2)}, u32[]{:S(2)}) collective-permute-start(f32[32]{0:T(128)S(1)} %convert_reduce_fusion), channel_id=1, source_target_pairs={{0,2},{2,0},{1,3},{3,1},{4,6},{6,4},{5,7},{7,5},{8,10},{10,8},{9,1... | collective-permute-start | bytes 392 | tf_op jit(solution)/shard_map/ppermute | solution.py:232
  9.5 2.0 %collective-permute-done.1 = f32[32]{0:T(128)S(1)} collective-permute-done((f32[32]{0:T(128)S(1)}, f32[32]{0:T(128)S(1)}, u32[]{:S(2)}, u32[]{:S(2)}) %collective-permute-start.1) | collective-permute-done | bytes 160 | tf_op jit(solution)/shard_map/ppermute | solution.py:232
  11.6 0.1 concatenate.15
  11.7 1.6 %collective-permute-start.2 = (bf16[272,512]{1,0:T(8,128)(2,1)S(1)}, bf16[272,512]{1,0:T(8,128)(2,1)}, u32[]{:S(2)}, u32[]{:S(2)}) collective-permute-start(bf16[272,512]{1,0:T(8,128)(2,1)S(1)} %pad_maximum_fusion), channel_id=1, source_target_pairs={{0,4},{4,8},{8,12},{12,0},{28,24},{24,20},{20,16},{16,28},{1,5},{5... | collective-permute-start | bytes 835592 | tf_op jit(solution)/shard_map/ppermute | solution.py:215
  13.4 0.2 collective-permute-done.3
  13.6 1.3 %collective-permute-start.4 = (bf16[256,512]{1,0:T(8,128)(2,1)}, bf16[256,512]{1,0:T(8,128)(2,1)}, u32[]{:S(2)}, u32[]{:S(2)}) collective-permute-start(bf16[256,512]{1,0:T(8,128)(2,1)} %collective-permute-done.3), channel_id=1, source_target_pairs={{4,20},{8,24},{24,8},{20,4},{5,21},{9,25},{25,9},{21,5},{6,22},{10... | collective-permute-start | bytes 786440 | tf_op jit(solution)/shard_map/ppermute | solution.py:261
  14.9 0.1 broadcast_and_fusion
  15.0 3.2 %collective-permute-start.7 = (bf16[256,512]{1,0:T(8,128)(2,1)}, bf16[256,512]{1,0:T(8,128)(2,1)S(1)}, u32[]{:S(2)}, u32[]{:S(2)}) collective-permute-start(bf16[256,512]{1,0:T(8,128)(2,1)} %get-tuple-element.26), channel_id=1, source_target_pairs={{0,4},{4,8},{8,12},{12,0},{28,24},{24,20},{20,16},{16,28},{1,5},{5... | collective-permute-start | bytes 786440 | tf_op jit(solution)/shard_map/ppermute | solution.py:215
  18.2 0.9 %collective-permute-done.5.refs_0_ = bf16[256,512]{1,0:T(8,128)(2,1)S(1)} collective-permute-done((bf16[256,512]{1,0:T(8,128)(2,1)S(1)}, bf16[256,512]{1,0:T(8,128)(2,1)S(1)}, u32[]{:S(2)}, u32[]{:S(2)}) %collective-permute-start.5) | collective-permute-done | bytes 262176 | tf_op jit(solution)/shard_map/ppermute | solution.py:215
  19.1 1.4 %collective-permute-start.10 = (bf16[256,512]{1,0:T(8,128)(2,1)S(1)}, bf16[256,512]{1,0:T(8,128)(2,1)}, u32[]{:S(2)}, u32[]{:S(2)}) collective-permute-start(bf16[256,512]{1,0:T(8,128)(2,1)S(1)} %collective-permute-done.5.refs_0_), channel_id=1, source_target_pairs={{4,20},{8,24},{24,8},{20,4},{5,21},{9,25},{25,9},{21,5},{6,22},{10... | collective-permute-start | bytes 786440 | tf_op jit(solution)/shard_map/ppermute | solution.py:262
  20.5 0.1 convert_element_type.39
  20.6 0.0 collective-permute-done.4
  20.6 1.4 %collective-permute-start.13 = (bf16[256,512]{1,0:T(8,128)(2,1)}, bf16[256,512]{1,0:T(8,128)(2,1)}, u32[]{:S(2)}, u32[]{:S(2)}) collective-permute-start(bf16[256,512]{1,0:T(8,128)(2,1)} %collective-permute-done.4), channel_id=1, source_target_pairs={{20,8},{24,12},{8,20},{4,16},{21,9},{25,13},{9,21},{5,17},{22,10},... | collective-permute-start | bytes 786440 | tf_op jit(solution)/shard_map/ppermute | solution.py:215
  21.9 3.3 %collective-permute-done.2 = bf16[272,512]{1,0:T(8,128)(2,1)} collective-permute-done((bf16[272,512]{1,0:T(8,128)(2,1)S(1)}, bf16[272,512]{1,0:T(8,128)(2,1)}, u32[]{:S(2)}, u32[]{:S(2)}) %collective-permute-start.2) | collective-permute-done | bytes 278560 | tf_op jit(solution)/shard_map/ppermute | solution.py:215
  25.2 0.7 %slice_bitcast_fusion.1 = bf16[2,4,8,128]{3,2,1,0:T(8,128)(2,1)S(1)} fusion(bf16[272,512]{1,0:T(8,128)(2,1)} %collective-permute-done.2), kind=kLoop, calls=%fused_computation.2 | loop fusion | bytes 32768
  26.0 0.1 dynamic-slice_convert_fusion.1
  26.0 0.1 concatenate.17.info_ref
  26.1 0.0 collective-permute-start.6
  26.1 1.4 %collective-permute-start.9 = (bf16[272,512]{1,0:T(8,128)(2,1)}, bf16[272,512]{1,0:T(8,128)(2,1)}, u32[]{:S(2)}, u32[]{:S(2)}) collective-permute-start(bf16[272,512]{1,0:T(8,128)(2,1)} %collective-permute-done.2), channel_id=1, source_target_pairs={{4,8},{8,12},{24,20},{20,16},{5,9},{9,13},{25,21},{21,17},{6,10},{... | collective-permute-start | bytes 835592 | tf_op jit(solution)/shard_map/ppermute | solution.py:267
  27.5 3.0 %collective-permute-done.7.refs_2_ = bf16[256,512]{1,0:T(8,128)(2,1)S(1)} collective-permute-done((bf16[256,512]{1,0:T(8,128)(2,1)}, bf16[256,512]{1,0:T(8,128)(2,1)S(1)}, u32[]{:S(2)}, u32[]{:S(2)}) %collective-permute-start.7) | collective-permute-done | bytes 262176 | tf_op jit(solution)/shard_map/ppermute | solution.py:215
  30.5 0.0 collective-permute-start.8
  30.5 0.1 pad_add_fusion.units_ref
  30.6 0.1 broadcast_in_dim.100
  30.7 0.1 broadcast_in_dim.105
  30.8 0.0 collective-permute-done.10
  30.8 0.7 %collective-permute-start.15 = (bf16[256,512]{1,0:T(8,128)(2,1)S(1)}, bf16[256,512]{1,0:T(8,128)(2,1)S(1)}, u32[]{:S(2)}, u32[]{:S(2)}) collective-permute-start(bf16[256,512]{1,0:T(8,128)(2,1)S(1)} %collective-permute-done.7.refs_2_), channel_id=1, source_target_pairs={{4,8},{8,12},{24,20},{20,16},{5,9},{9,13},{25,21},{21,17},{6,10},{... | collective-permute-start | bytes 786440 | tf_op jit(solution)/shard_map/ppermute | solution.py:291
  31.5 0.0 collective-permute-done.6.refs_1_
  31.5 1.4 %collective-permute-start.11 = (bf16[256,512]{1,0:T(8,128)(2,1)}, bf16[256,512]{1,0:T(8,128)(2,1)}, u32[]{:S(2)}, u32[]{:S(2)}) collective-permute-start(bf16[256,512]{1,0:T(8,128)(2,1)} %collective-permute-done.10), channel_id=1, source_target_pairs={{20,8},{24,12},{8,20},{4,16},{21,9},{25,13},{9,21},{5,17},{22,10},... | collective-permute-start | bytes 786440 | tf_op jit(solution)/shard_map/ppermute | solution.py:215
  32.9 0.0 collective-permute-done.8.refs_3_
  32.9 3.3 %shard_map.64 = (f32[8,256]{1,0:T(8,128)S(1)}, f32[2,256]{1,0:T(2,128)S(1)}) custom-call(s32[49]{0:T(128)S(1)} %concatenate.17.info_ref, s32[2]{0:T(128)S(1)} %pad_add_fusion.units_ref, bf16[8,256,512]{2,1,0:T(8,128)(2,1)S(1)} %copy-done, bf16[8,256,512]{2,1,0:T(8,128)(2,1)} %collective-permute-done.peer_ref, ...), custom_call_target="tpu_custom_call" | custom-call | tf_op jit(solution)/shard_map/pallas_call | solution.py:145
  36.1 2.6 %collective-permute-start.12 = (f32[2,256]{1,0:T(2,128)S(1)}, f32[2,256]{1,0:T(2,128)S(1)}, u32[]{:S(2)}, u32[]{:S(2)}) collective-permute-start(f32[2,256]{1,0:T(2,128)S(1)} %get-tuple-element.30), channel_id=1, source_target_pairs={{4,0},{8,4},{12,8},{0,12},{24,28},{20,24},{16,20},{28,16},{5,1},{9... | collective-permute-start | bytes 6152 | tf_op jit(solution)/shard_map/ppermute | solution.py:299
  38.7 0.0 collective-permute-done.13
  38.7 0.3 collective-permute-start.14
  39.0 0.0 collective-permute-done.9
  39.0 0.7 %slice_bitcast_fusion = bf16[2,4,8,128]{3,2,1,0:T(8,128)(2,1)S(1)} fusion(bf16[272,512]{1,0:T(8,128)(2,1)} %collective-permute-done.9), kind=kLoop, calls=%fused_computation.1 | loop fusion | bytes 32768
  39.7 0.3 collective-permute-start.16
  40.0 0.1 dynamic-slice_convert_fusion
  40.1 0.1 concatenate.18.info_ref
  40.2 0.0 collective-permute-done.15.refs_2_
  40.2 3.4 %collective-permute-done.12 = f32[2,256]{1,0:T(2,128)S(1)} collective-permute-done((f32[2,256]{1,0:T(2,128)S(1)}, f32[2,256]{1,0:T(2,128)S(1)}, u32[]{:S(2)}, u32[]{:S(2)}) %collective-permute-start.12) | collective-permute-done | bytes 2080 | tf_op jit(solution)/shard_map/ppermute | solution.py:299
  43.6 0.0 collective-permute-done.11.refs_0_
  43.6 0.0 collective-permute-done.14.refs_1_
  43.7 0.0 collective-permute-done.16.refs_3_
  43.7 1.9 %shard_map.65 = (f32[8,256]{1,0:T(8,128)S(1)}, f32[2,256]{1,0:T(2,128)S(1)}) custom-call(s32[49]{0:T(128)S(1)} %concatenate.18.info_ref, s32[2]{0:T(128)S(1)} %pad_add_fusion.units_ref, bf16[8,256,512]{2,1,0:T(8,128)(2,1)S(1)} %copy-done, bf16[8,256,512]{2,1,0:T(8,128)(2,1)} %collective-permute-done.peer_ref, ...), custom_call_target="tpu_custom_call" | custom-call | tf_op jit(solution)/shard_map/pallas_call | solution.py:145
  45.6 0.1 broadcast_select_fusion.1
  45.6 0.1 select_add_fusion
  45.7 0.0 collective-permute-start.17
  45.7 1.2 %collective-permute-done.17 = f32[12,256]{1,0:T(8,128)S(1)} collective-permute-done((f32[12,256]{1,0:T(8,128)S(1)}, f32[12,256]{1,0:T(8,128)S(1)}, u32[]{:S(2)}, u32[]{:S(2)}) %collective-permute-start.17) | collective-permute-done | bytes 12320 | tf_op jit(solution)/shard_map/ppermute | solution.py:318
  46.9 1.5 %collective-permute-start.18 = (f32[12,256]{1,0:T(8,128)S(1)}, f32[12,256]{1,0:T(8,128)S(1)}, u32[]{:S(2)}, u32[]{:S(2)}) collective-permute-start(f32[12,256]{1,0:T(8,128)S(1)} %fusion.7), channel_id=1, source_target_pairs={{0,2},{2,0},{1,3},{3,1},{4,6},{6,4},{5,7},{7,5},{8,10},{10,8},{9,1... | collective-permute-start | bytes 36872 | tf_op jit(solution)/shard_map/ppermute | solution.py:321
  48.4 2.2 %collective-permute-done.18 = f32[12,256]{1,0:T(8,128)S(1)} collective-permute-done((f32[12,256]{1,0:T(8,128)S(1)}, f32[12,256]{1,0:T(8,128)S(1)}, u32[]{:S(2)}, u32[]{:S(2)}) %collective-permute-start.18) | collective-permute-done | bytes 12320 | tf_op jit(solution)/shard_map/ppermute | solution.py:321
  50.6 0.1 broadcast_select_fusion
  50.7 5.1 %collective-permute-start.19 = (f32[2,4,256]{2,1,0:T(4,128)S(1)}, f32[2,4,256]{2,1,0:T(4,128)S(1)}, u32[]{:S(2)}, u32[]{:S(2)}) collective-permute-start(f32[2,4,256]{2,1,0:T(4,128)S(1)} %broadcast_select_fusion), channel_id=1, source_target_pairs={{8,0},{12,4},{0,8},{4,12},{20,28},{16,24},{28,20},{24,16},{9,1},{1... | collective-permute-start | bytes 24584 | tf_op jit(solution)/shard_map/ppermute | solution.py:326
  55.8 1.6 %collective-permute-done.19 = f32[2,4,256]{2,1,0:T(4,128)S(1)} collective-permute-done((f32[2,4,256]{2,1,0:T(4,128)S(1)}, f32[2,4,256]{2,1,0:T(4,128)S(1)}, u32[]{:S(2)}, u32[]{:S(2)}) %collective-permute-start.19) | collective-permute-done | bytes 8224 | tf_op jit(solution)/shard_map/ppermute | solution.py:326
  57.5 0.6 %fusion.1 = f32[8,256]{1,0:T(8,128)} fusion(f32[8,256]{1,0:T(8,128)S(1)} %reshape.110, f32[12,256]{1,0:T(8,128)S(1)} %collective-permute-done.18, f32[12,256]{1,0:T(8,128)S(1)} %fusion.7), kind=kLoop, calls=%fused_computation.6 | loop fusion | flops 4096 | bytes 32768 | tf_op jit(solution)/shard_map/log1p | solution.py:329
  (35 shorter events, 0.2 us)
Async XLA Ops:
  0.0 32.9 %copy-start = (bf16[8,256,512]{2,1,0:T(8,128)(2,1)S(1)}, bf16[8,256,512]{2,1,0:T(8,128)(2,1)}, u32[]{:S(2)}) copy-start(bf16[8,256,512]{2,1,0:T(8,128)(2,1)} %own_ref.3) | copy-start | bytes 6291460
  0.0 7.8 %copy-start.1 = (bf16[8,256]{1,0:T(8,128)(2,1)S(1)}, bf16[8,256]{1,0:T(8,128)(2,1)}, u32[]{:S(2)}) copy-start(bf16[8,256]{1,0:T(8,128)(2,1)} %param.7) | copy-start | bytes 12292
  0.0 7.8 %copy-start.2 = (s32[8]{0:T(128)S(1)}, s32[8]{0:T(128)}, u32[]{:S(2)}) copy-start(s32[8]{0:T(128)} %param.8) | copy-start | bytes 100
  0.0 7.8 %copy-start.3 = (s32[8]{0:T(128)S(1)}, s32[8]{0:T(128)}, u32[]{:S(2)}) copy-start(s32[8]{0:T(128)} %param.9) | copy-start | bytes 100
  0.0 7.8 %copy-start.5 = (s32[1,1,12,1]{2,3,1,0:T(1,128)S(1)}, s32[1,1,12,1]{2,3,1,0:T(1,128)}, u32[]{:S(2)}) copy-start(s32[1,1,12,1]{2,3,1,0:T(1,128)} %param.10) | copy-start | bytes 148
  0.0 7.8 %copy-start.4 = (s32[1,1,12]{2,1,0:T(1,128)S(1)}, s32[1,1,12]{2,1,0:T(1,128)}, u32[]{:S(2)}) copy-start(s32[1,1,12]{2,1,0:T(1,128)} %param.11) | copy-start | bytes 148
  0.0 7.8 %collective-permute-start = (bf16[8,256,512]{2,1,0:T(8,128)(2,1)}, bf16[8,256,512]{2,1,0:T(8,128)(2,1)}, u32[]{:S(2)}, u32[]{:S(2)}) collective-permute-start(bf16[8,256,512]{2,1,0:T(8,128)(2,1)} %own_ref.3), channel_id=1, source_target_pairs={{0,1},{1,0},{2,3},{3,2},{4,5},{5,4},{6,7},{7,6},{8,9},{9,8},{10,11... | collective-permute-start | bytes 6291464 | tf_op jit(solution)/shard_map/ppermute | solution.py:221
  1.5 12.1 %collective-permute-start.3 = (bf16[256,512]{1,0:T(8,128)(2,1)S(1)}, bf16[256,512]{1,0:T(8,128)(2,1)}, u32[]{:S(2)}, u32[]{:S(2)}) collective-permute-start(bf16[256,512]{1,0:T(8,128)(2,1)S(1)} %constant_dynamic-slice_fusion.4), channel_id=1, source_target_pairs={{0,4},{4,8},{8,12},{12,0},{28,24},{24,20},{20,16},{16,28},{1,5},{5... | collective-permute-start | bytes 786440 | tf_op jit(solution)/shard_map/ppermute | solution.py:215
  6.2 12.9 %collective-permute-start.5 = (bf16[256,512]{1,0:T(8,128)(2,1)S(1)}, bf16[256,512]{1,0:T(8,128)(2,1)S(1)}, u32[]{:S(2)}, u32[]{:S(2)}) collective-permute-start(bf16[256,512]{1,0:T(8,128)(2,1)S(1)} %get-tuple-element.38), channel_id=1, source_target_pairs={{0,4},{4,8},{8,12},{12,0},{28,24},{24,20},{20,16},{16,28},{1,5},{5... | collective-permute-start | bytes 786440 | tf_op jit(solution)/shard_map/ppermute | solution.py:215
  8.0 3.6 %collective-permute-start.1 = (f32[32]{0:T(128)S(1)}, f32[32]{0:T(128)S(1)}, u32[]{:S(2)}, u32[]{:S(2)}) collective-permute-start(f32[32]{0:T(128)S(1)} %convert_reduce_fusion), channel_id=1, source_target_pairs={{0,2},{2,0},{1,3},{3,1},{4,6},{6,4},{5,7},{7,5},{8,10},{10,8},{9,1... | collective-permute-start | bytes 392 | tf_op jit(solution)/shard_map/ppermute | solution.py:232
  11.7 13.5 %collective-permute-start.2 = (bf16[272,512]{1,0:T(8,128)(2,1)S(1)}, bf16[272,512]{1,0:T(8,128)(2,1)}, u32[]{:S(2)}, u32[]{:S(2)}) collective-permute-start(bf16[272,512]{1,0:T(8,128)(2,1)S(1)} %pad_maximum_fusion), channel_id=1, source_target_pairs={{0,4},{4,8},{8,12},{12,0},{28,24},{24,20},{20,16},{16,28},{1,5},{5... | collective-permute-start | bytes 835592 | tf_op jit(solution)/shard_map/ppermute | solution.py:215
  13.6 7.0 %collective-permute-start.4 = (bf16[256,512]{1,0:T(8,128)(2,1)}, bf16[256,512]{1,0:T(8,128)(2,1)}, u32[]{:S(2)}, u32[]{:S(2)}) collective-permute-start(bf16[256,512]{1,0:T(8,128)(2,1)} %collective-permute-done.3), channel_id=1, source_target_pairs={{4,20},{8,24},{24,8},{20,4},{5,21},{9,25},{25,9},{21,5},{6,22},{10... | collective-permute-start | bytes 786440 | tf_op jit(solution)/shard_map/ppermute | solution.py:261
  15.0 15.5 %collective-permute-start.7 = (bf16[256,512]{1,0:T(8,128)(2,1)}, bf16[256,512]{1,0:T(8,128)(2,1)S(1)}, u32[]{:S(2)}, u32[]{:S(2)}) collective-permute-start(bf16[256,512]{1,0:T(8,128)(2,1)} %get-tuple-element.26), channel_id=1, source_target_pairs={{0,4},{4,8},{8,12},{12,0},{28,24},{24,20},{20,16},{16,28},{1,5},{5... | collective-permute-start | bytes 786440 | tf_op jit(solution)/shard_map/ppermute | solution.py:215
  19.1 11.7 %collective-permute-start.10 = (bf16[256,512]{1,0:T(8,128)(2,1)S(1)}, bf16[256,512]{1,0:T(8,128)(2,1)}, u32[]{:S(2)}, u32[]{:S(2)}) collective-permute-start(bf16[256,512]{1,0:T(8,128)(2,1)S(1)} %collective-permute-done.5.refs_0_), channel_id=1, source_target_pairs={{4,20},{8,24},{24,8},{20,4},{5,21},{9,25},{25,9},{21,5},{6,22},{10... | collective-permute-start | bytes 786440 | tf_op jit(solution)/shard_map/ppermute | solution.py:262
  20.6 18.1 %collective-permute-start.13 = (bf16[256,512]{1,0:T(8,128)(2,1)}, bf16[256,512]{1,0:T(8,128)(2,1)}, u32[]{:S(2)}, u32[]{:S(2)}) collective-permute-start(bf16[256,512]{1,0:T(8,128)(2,1)} %collective-permute-done.4), channel_id=1, source_target_pairs={{20,8},{24,12},{8,20},{4,16},{21,9},{25,13},{9,21},{5,17},{22,10},... | collective-permute-start | bytes 786440 | tf_op jit(solution)/shard_map/ppermute | solution.py:215
  26.1 5.3 %collective-permute-start.6 = (bf16[256,512]{1,0:T(8,128)(2,1)}, bf16[256,512]{1,0:T(8,128)(2,1)S(1)}, u32[]{:S(2)}, u32[]{:S(2)}) collective-permute-start(bf16[256,512]{1,0:T(8,128)(2,1)} %collective-permute-done.3), channel_id=1, source_target_pairs={{0,1},{1,0},{2,3},{3,2},{4,5},{5,4},{6,7},{7,6},{8,9},{9,8},{10,11... | collective-permute-start | bytes 786440 | tf_op jit(solution)/shard_map/ppermute | solution.py:250
  26.1 12.9 %collective-permute-start.9 = (bf16[272,512]{1,0:T(8,128)(2,1)}, bf16[272,512]{1,0:T(8,128)(2,1)}, u32[]{:S(2)}, u32[]{:S(2)}) collective-permute-start(bf16[272,512]{1,0:T(8,128)(2,1)} %collective-permute-done.2), channel_id=1, source_target_pairs={{4,8},{8,12},{24,20},{20,16},{5,9},{9,13},{25,21},{21,17},{6,10},{... | collective-permute-start | bytes 835592 | tf_op jit(solution)/shard_map/ppermute | solution.py:267
  30.5 2.4 %collective-permute-start.8 = (bf16[272,512]{1,0:T(8,128)(2,1)}, bf16[272,512]{1,0:T(8,128)(2,1)S(1)}, u32[]{:S(2)}, u32[]{:S(2)}) collective-permute-start(bf16[272,512]{1,0:T(8,128)(2,1)} %collective-permute-done.2), channel_id=1, source_target_pairs={{0,1},{1,0},{2,3},{3,2},{4,5},{5,4},{6,7},{7,6},{8,9},{9,8},{10,11... | collective-permute-start | bytes 835592 | tf_op jit(solution)/shard_map/ppermute | solution.py:250
  30.8 9.4 %collective-permute-start.15 = (bf16[256,512]{1,0:T(8,128)(2,1)S(1)}, bf16[256,512]{1,0:T(8,128)(2,1)S(1)}, u32[]{:S(2)}, u32[]{:S(2)}) collective-permute-start(bf16[256,512]{1,0:T(8,128)(2,1)S(1)} %collective-permute-done.7.refs_2_), channel_id=1, source_target_pairs={{4,8},{8,12},{24,20},{20,16},{5,9},{9,13},{25,21},{21,17},{6,10},{... | collective-permute-start | bytes 786440 | tf_op jit(solution)/shard_map/ppermute | solution.py:291
  31.5 12.2 %collective-permute-start.11 = (bf16[256,512]{1,0:T(8,128)(2,1)}, bf16[256,512]{1,0:T(8,128)(2,1)}, u32[]{:S(2)}, u32[]{:S(2)}) collective-permute-start(bf16[256,512]{1,0:T(8,128)(2,1)} %collective-permute-done.10), channel_id=1, source_target_pairs={{20,8},{24,12},{8,20},{4,16},{21,9},{25,13},{9,21},{5,17},{22,10},... | collective-permute-start | bytes 786440 | tf_op jit(solution)/shard_map/ppermute | solution.py:215
  36.1 7.5 %collective-permute-start.12 = (f32[2,256]{1,0:T(2,128)S(1)}, f32[2,256]{1,0:T(2,128)S(1)}, u32[]{:S(2)}, u32[]{:S(2)}) collective-permute-start(f32[2,256]{1,0:T(2,128)S(1)} %get-tuple-element.30), channel_id=1, source_target_pairs={{4,0},{8,4},{12,8},{0,12},{24,28},{20,24},{16,20},{28,16},{5,1},{9... | collective-permute-start | bytes 6152 | tf_op jit(solution)/shard_map/ppermute | solution.py:299
  38.7 4.9 %collective-permute-start.14 = (bf16[256,512]{1,0:T(8,128)(2,1)}, bf16[256,512]{1,0:T(8,128)(2,1)S(1)}, u32[]{:S(2)}, u32[]{:S(2)}) collective-permute-start(bf16[256,512]{1,0:T(8,128)(2,1)} %collective-permute-done.13), channel_id=1, source_target_pairs={{0,1},{1,0},{2,3},{3,2},{4,5},{5,4},{6,7},{7,6},{8,9},{9,8},{10,11... | collective-permute-start | bytes 786440 | tf_op jit(solution)/shard_map/ppermute | solution.py:250
  39.7 3.9 %collective-permute-start.16 = (bf16[272,512]{1,0:T(8,128)(2,1)}, bf16[272,512]{1,0:T(8,128)(2,1)S(1)}, u32[]{:S(2)}, u32[]{:S(2)}) collective-permute-start(bf16[272,512]{1,0:T(8,128)(2,1)} %collective-permute-done.9), channel_id=1, source_target_pairs={{0,1},{1,0},{2,3},{3,2},{4,5},{5,4},{6,7},{7,6},{8,9},{9,8},{10,11... | collective-permute-start | bytes 835592 | tf_op jit(solution)/shard_map/ppermute | solution.py:250
  45.7 1.2 %collective-permute-start.17 = (f32[12,256]{1,0:T(8,128)S(1)}, f32[12,256]{1,0:T(8,128)S(1)}, u32[]{:S(2)}, u32[]{:S(2)}) collective-permute-start(f32[12,256]{1,0:T(8,128)S(1)} %pad_maximum_fusion.1), channel_id=1, source_target_pairs={{0,1},{1,0},{2,3},{3,2},{4,5},{5,4},{6,7},{7,6},{8,9},{9,8},{10,11... | collective-permute-start | bytes 36872 | tf_op jit(solution)/shard_map/ppermute | solution.py:318
  46.9 3.7 %collective-permute-start.18 = (f32[12,256]{1,0:T(8,128)S(1)}, f32[12,256]{1,0:T(8,128)S(1)}, u32[]{:S(2)}, u32[]{:S(2)}) collective-permute-start(f32[12,256]{1,0:T(8,128)S(1)} %fusion.7), channel_id=1, source_target_pairs={{0,2},{2,0},{1,3},{3,1},{4,6},{6,4},{5,7},{7,5},{8,10},{10,8},{9,1... | collective-permute-start | bytes 36872 | tf_op jit(solution)/shard_map/ppermute | solution.py:321
  50.7 6.7 %collective-permute-start.19 = (f32[2,4,256]{2,1,0:T(4,128)S(1)}, f32[2,4,256]{2,1,0:T(4,128)S(1)}, u32[]{:S(2)}, u32[]{:S(2)}) collective-permute-start(f32[2,4,256]{2,1,0:T(4,128)S(1)} %broadcast_select_fusion), channel_id=1, source_target_pairs={{8,0},{12,4},{0,8},{4,12},{20,28},{16,24},{28,20},{24,16},{9,1},{1... | collective-permute-start | bytes 24584 | tf_op jit(solution)/shard_map/ppermute | solution.py:326
